TPU v7x, 32 devices: a whole 2x2x4 slice. The times are simulated.
32 devices in a mesh: wide: 16 (over z, y, x), narrow: 2 (over core).
Axes of the slice: x: 2, y: 2, z: 4, core: 2. Of those that a mesh axis runs over, the one named last changes fastest.
Arguments:
- sublevel_symbol_entries: bfloat16 [1024, 4, 4096], P('wide', None, 'narrow'), may hold values from -160 to 160
- prior_symbol_memory: bfloat16 [1024, 4096], P('wide', 'narrow'), may hold values from -6 to 6
- entry_scaling_multiplier: float32 [4096], P('narrow'), may hold values from 0.25 to 1.75
- entry_scaling_offset: float32 [4096], P('narrow'), may hold values from -4 to 4
- learned_blending: float32 [6, 4096], P(None, 'narrow'), may hold values from 0 to 1
- blending_lowering_coefficients: bfloat16 [4096, 160], P('narrow'), may hold values from -0.09375 to 0.09375
- blending_raising_coefficients: bfloat16 [5, 32, 4096], P(None, None, 'narrow'), may hold values from -1 to 1
- fading_lowering_coefficients: bfloat16 [4096, 64], P('narrow'), may hold values from -0.09375 to 0.09375
- fading_raising_coefficients: bfloat16 [64, 4096], P(None, 'wide'), may hold values from -0.75 to 0.75
- learned_fading: float32 [4096], P('wide'), may hold values from -6 to 1
- immediate_item_premium: float32 [4096], P('wide'), may hold values from -3 to 3
- acceptor_projection: bfloat16 [4096, 4096], P('narrow', 'wide'), may hold values from -0.09375 to 0.09375
- lookup_projection: bfloat16 [4096, 4096], P('narrow', 'wide'), may hold values from -0.09375 to 0.09375
- payload_projection: bfloat16 [4096, 4096], P('narrow', 'wide'), may hold values from -0.09375 to 0.09375
- gating_projection: bfloat16 [4096, 4096], P('narrow', 'wide'), may hold values from -0.09375 to 0.09375
- emission_projection: bfloat16 [4096, 4096], P(None, 'wide'), may hold values from -0.09375 to 0.09375
- group_scaling_multiplier: float32 [4096], P('wide'), may hold values from 0.25 to 1.75
- group_scaling_offset: float32 [4096], P('wide'), may hold values from -4 to 4
- dialogue_group_memory: float32 [262144, 1024], P('wide', 'narrow'), may hold values from -6 to 6
Outputs:
- mixing_output: bfloat16 [1024, 4, 4096], P('narrow', None, 'wide')
- final_state: float32 [262144, 1024], P('wide', 'narrow')
All inputs are finite; a program needn't handle non-finite values.
Results may differ from a plain program's by a relative error of at most 0.034.
Values may be sent and summed in bfloat16 or wider, within the bound.
No kernel may reach another device: no remote copies, remote signals or barrier semaphores. Data moves between devices by JAX's collectives and lax.ppermute only.
A program may use at most 320 MiB of HBM per device.

v0:
```python
import jax
import jax.numpy as jnp
from jax import lax
from jax.sharding import PartitionSpec as P

CHANNEL_SPAN = 64
FEATURE_EXTENT = 4096


def per_device(
    sublevel_symbol_entries,
    prior_symbol_memory,
    entry_scaling_multiplier,
    entry_scaling_offset,
    learned_blending,
    blending_lowering_coefficients,
    blending_raising_coefficients,
    fading_lowering_coefficients,
    fading_raising_coefficients,
    learned_fading,
    immediate_item_premium,
    acceptor_projection,
    lookup_projection,
    payload_projection,
    gating_projection,
    emission_projection,
    group_scaling_multiplier,
    group_scaling_offset,
    dialogue_group_memory,
):
    rank = blending_raising_coefficients.shape[1]
    narrow_rows = dialogue_group_memory.shape[1]
    local_width = emission_projection.shape[1]
    group_partition = local_width // CHANNEL_SPAN
    weights = (acceptor_projection, lookup_projection, payload_projection, gating_projection)
    shift_gathered = lax.all_gather(prior_symbol_memory, "wide", axis=0, tiled=True)

    def channel_set_first(block):
        return block.reshape(narrow_rows, group_partition, CHANNEL_SPAN).transpose(1, 2, 0)

    present_symbol = dialogue_group_memory.reshape(
        group_partition, CHANNEL_SPAN, CHANNEL_SPAN, narrow_rows
    )
    previous_rows = prior_symbol_memory
    previous_all = shift_gathered
    results = []
    for index in range(sublevel_symbol_entries.shape[1]):
        floats = sublevel_symbol_entries[:, index : index + 1].astype(jnp.float32)
        totals, squares = lax.psum((jnp.sum(floats, -1), jnp.sum(floats * floats, -1)), "narrow")
        prepare_center = totals[..., None] / FEATURE_EXTENT
        spread = squares[..., None] / FEATURE_EXTENT - prepare_center * prepare_center
        normed = (
            (floats - prepare_center) * lax.rsqrt(spread + 1e-05) * entry_scaling_multiplier
            + entry_scaling_offset
        ).astype(jnp.bfloat16)
        previous = jnp.concatenate([previous_rows[:, None], normed[:, :-1]], 1)
        prepare_normalized_float = normed.astype(jnp.float32)
        prepare_shifted_input = previous.astype(jnp.float32) - prepare_normalized_float
        blended = (prepare_normalized_float + prepare_shifted_input * learned_blending[0]).astype(
            jnp.bfloat16
        )
        partial_mix = jnp.einsum(
            "smd,dr->smr",
            blended,
            blending_lowering_coefficients,
            preferred_element_type=jnp.float32,
        )
        hidden_activation = jnp.tanh(lax.psum(partial_mix, "narrow")).astype(jnp.bfloat16)
        decay_shift = jnp.einsum(
            "smr,rd->smd",
            hidden_activation[..., :rank],
            blending_raising_coefficients[0],
            preferred_element_type=jnp.float32,
        )
        decay_mix = (
            prepare_normalized_float + prepare_shifted_input * (learned_blending[1] + decay_shift)
        ).astype(jnp.bfloat16)
        partial_decay = jnp.einsum(
            "smd,dr->smr",
            decay_mix,
            fading_lowering_coefficients,
            preferred_element_type=jnp.float32,
        )
        decay_hidden = jnp.tanh(lax.psum(partial_decay, "narrow")).astype(jnp.bfloat16)
        small = jnp.concatenate([hidden_activation[..., rank:], decay_hidden], -1)
        prepare_normed_all = lax.all_gather(normed, "wide", axis=0, tiled=True)
        prepare_small_all = lax.all_gather(small, "wide", axis=0, tiled=True)
        normed, normed_all, small_all = (normed, prepare_normed_all, prepare_small_all)
        project_previous_all = previous_all[:, None]
        normalized_float = normed_all.astype(jnp.float32)
        shifted_input = project_previous_all.astype(jnp.float32) - normalized_float
        term_results = []
        for selector_index in range(4):
            low_rank_update = jnp.einsum(
                "smr,rd->smd",
                small_all[..., selector_index * rank : (selector_index + 1) * rank],
                blending_raising_coefficients[selector_index + 1],
                preferred_element_type=jnp.float32,
            )
            mixed_input = (
                normalized_float
                + shifted_input * (learned_blending[selector_index + 2] + low_rank_update)
            ).astype(jnp.bfloat16)
            term_results.append(
                jnp.einsum(
                    "smd,de->sme",
                    mixed_input,
                    weights[selector_index],
                    preferred_element_type=jnp.float32,
                )
            )
        project_transformed_outcome = lax.psum_scatter(
            jnp.concatenate(term_results, -1).astype(jnp.bfloat16),
            "narrow",
            scatter_dimension=0,
            tiled=True,
        ).astype(jnp.float32)
        rows_start = lax.axis_index("narrow") * narrow_rows
        decay_rows = lax.dynamic_slice_in_dim(
            small_all[..., 4 * rank :], rows_start, narrow_rows, 0
        )
        decay_log = learned_fading + jnp.einsum(
            "smr,rd->smd",
            decay_rows,
            fading_raising_coefficients,
            preferred_element_type=jnp.float32,
        )
        shrink_coefficient = jnp.exp(-jnp.exp(decay_log))
        recurrence_present_symbol = present_symbol
        each_group_reward = immediate_item_premium.reshape(group_partition, CHANNEL_SPAN)
        present_acceptor = channel_set_first(project_transformed_outcome[:, 0, :local_width])
        key_now = channel_set_first(
            project_transformed_outcome[:, 0, local_width : 2 * local_width]
        )
        value_now = channel_set_first(
            project_transformed_outcome[:, 0, 2 * local_width : 3 * local_width]
        )
        gate_now = project_transformed_outcome[:, 0, 3 * local_width :]
        forget_now = channel_set_first(shrink_coefficient[:, 0])
        dyadic_tensor = key_now[:, :, None, :] * value_now[:, None, :, :]
        memory_retrieval = jnp.sum(
            present_acceptor[:, :, None, :]
            * (recurrence_present_symbol + each_group_reward[:, :, None, None] * dyadic_tensor),
            1,
        )
        recurrence_present_symbol = (
            forget_now[:, :, None, :] * recurrence_present_symbol + dyadic_tensor
        )
        center = jnp.mean(memory_retrieval, 1, keepdims=True)
        offset = memory_retrieval - center
        scaled = offset * lax.rsqrt(jnp.mean(offset * offset, 1, keepdims=True) + 0.00064)
        squashed_vector = scaled.transpose(2, 0, 1).reshape(narrow_rows, local_width)
        pieces = [
            (
                (squashed_vector * group_scaling_multiplier + group_scaling_offset)
                * jax.nn.silu(gate_now)
            ).astype(jnp.bfloat16)
        ]
        present_symbol = recurrence_present_symbol
        gated = jnp.stack(pieces, 1)
        results.append(
            jnp.einsum(
                "smc,ce->sme",
                lax.all_gather(gated, "wide", axis=2, tiled=True),
                emission_projection,
                preferred_element_type=jnp.float32,
            ).astype(jnp.bfloat16)
        )
        previous_rows = normed[:, 0]
        previous_all = normed_all[:, 0]
    mixing_output = jnp.concatenate(results, 1)
    return (
        mixing_output,
        present_symbol.reshape(group_partition * CHANNEL_SPAN * CHANNEL_SPAN, narrow_rows),
    )


def solution(mesh):
    placed = (
        P("wide", None, "narrow"),
        P("wide", "narrow"),
        P("narrow"),
        P("narrow"),
        P(None, "narrow"),
        P("narrow", None),
        P(None, None, "narrow"),
        P("narrow", None),
        P(None, "wide"),
        P("wide"),
        P("wide"),
        P("narrow", "wide"),
        P("narrow", "wide"),
        P("narrow", "wide"),
        P("narrow", "wide"),
        P(None, "wide"),
        P("wide"),
        P("wide"),
        P("wide", "narrow"),
    )
    return jax.shard_map(
        per_device,
        mesh=mesh,
        in_specs=placed,
        out_specs=(P("narrow", None, "wide"), P("wide", "narrow")),
        check_vma=False,
    )
```

profile of v0, /device:TPU:0, one launch (start us, length us, event | category | flops | bytes accessed | tf_op | source)
XLA Modules:
  0.0 998.5 jit_solution(4118582770619577397)
XLA Ops:
  29.3 21.1 %all-reduce.8.cloned.1.call-done = (f32[64,1,160]{2,0,1:T(8,128)}, f32[64,1,160]{2,0,1:T(8,128)}, f32[64,1,160]{2,0,1:T(8,128)}, f32[64,1,160]{2,0,1:T(8,128)}) async-done(((f32[64,1,160]{2,0,1:T(8,128)}, f32[64,1,160]{2,0,1:T(8,128)}, f32[64,1,160]{2,0,1:T(8,128)}, f32[64,1,160]{2,0,1:T(8,128)}), (f32[64,1,160]{2,0,1:T(8,128)}, f32[64,1,160]{2,0,1:T(8,128)}, f32[64,1,160]{2,0,1:T(8,128)}, ...) | async-done | bytes 163856 | tf_op jit(solution)/shard_map/psum | solution.py:68
  66.8 15.1 %all-reduce.6.cloned.1.call-done = (f32[64,1,64]{2,0,1:T(8,128)}, f32[64,1,64]{2,0,1:T(8,128)}, f32[64,1,64]{2,0,1:T(8,128)}, f32[64,1,64]{2,0,1:T(8,128)}) async-done(((f32[64,1,64]{2,0,1:T(8,128)}, f32[64,1,64]{2,0,1:T(8,128)}, f32[64,1,64]{2,0,1:T(8,128)}, f32[64,1,64]{2,0,1:T(8,128)}), (f32[64,1,64]{2,0,1:T(8,128)}, f32[64,1,64]{2,0,1:T(8,128)}, f32[64,1,64]{2,0,1:T(8,128)}, ...) | async-done | bytes 65552 | tf_op jit(solution)/shard_map/psum | solution.py:84
  82.6 46.5 %all_gather.44 = bf16[1024,1,192]{2,0,1:T(8,128)(2,1)S(1)} all-gather(bf16[64,1,192]{2,0,1:T(8,128)(2,1)S(1)} %pad_maximum_fusion.6), channel_id=1, replica_groups=mesh['wide'=16,'narrow'=2] {'wide'}, dimensions={0}, use_global_device_ids=true | all-gather | bytes 417792 | tf_op jit(solution)/shard_map/all_gather | solution.py:87
  129.9 16.7 %all-gather.10.cloned.1.call-done = bf16[1024,1,2048]{2,0,1:T(8,128)(2,1)} async-done(((bf16[64,1,2048]{2,0,1:T(8,128)(2,1)}), bf16[1024,1,2048]{2,0,1:T(8,128)(2,1)}) %all-gather.10.cloned.1.call-update) | async-done | bytes 4194320 | tf_op jit(solution)/shard_map/all_gather | solution.py:86
  146.6 77.0 %all-gather.16.cloned.1.call-done = bf16[1024,1,2048]{2,0,1:T(8,128)(2,1)} async-done(((bf16[64,1,2048]{2,0,1:T(8,128)(2,1)}), bf16[1024,1,2048]{2,0,1:T(8,128)(2,1)}) %all-gather.16.cloned.1.call-update) | async-done | bytes 4194320 | tf_op jit(solution)/shard_map/all_gather | solution.py:86
  223.7 6.8 fusion.168
  230.5 7.9 fusion.165
  238.4 7.7 fusion.162
  246.1 8.1 fusion.159
  257.2 44.6 %all_gather.41 = bf16[1024,1,192]{2,0,1:T(8,128)(2,1)S(1)} all-gather(bf16[64,1,192]{2,0,1:T(8,128)(2,1)S(1)} %pad_maximum_fusion.5), channel_id=1, replica_groups=mesh['wide'=16,'narrow'=2] {'wide'}, dimensions={0}, use_global_device_ids=true | all-gather | bytes 417792 | tf_op jit(solution)/shard_map/all_gather | solution.py:87
  306.1 7.6 fusion.180
  313.7 7.9 fusion.177
  321.6 7.7 fusion.174
  329.3 7.9 fusion.171
  340.3 44.5 %all_gather.47 = bf16[1024,1,192]{2,0,1:T(8,128)(2,1)S(1)} all-gather(bf16[64,1,192]{2,0,1:T(8,128)(2,1)S(1)} %pad_maximum_fusion.7), channel_id=1, replica_groups=mesh['wide'=16,'narrow'=2] {'wide'}, dimensions={0}, use_global_device_ids=true | all-gather | bytes 417792 | tf_op jit(solution)/shard_map/all_gather | solution.py:87
  386.3 39.8 %all_gather.50 = bf16[1024,1,192]{2,0,1:T(8,128)(2,1)S(1)} all-gather(bf16[64,1,192]{2,0,1:T(8,128)(2,1)S(1)} %pad_maximum_fusion.8), channel_id=1, replica_groups=mesh['wide'=16,'narrow'=2] {'wide'}, dimensions={0}, use_global_device_ids=true | all-gather | bytes 417792 | tf_op jit(solution)/shard_map/all_gather | solution.py:87
  426.1 43.0 %all-gather.24.cloned.1.call-done = bf16[1024,1,2048]{2,0,1:T(8,128)(2,1)} async-done(((bf16[64,1,2048]{2,0,1:T(8,128)(2,1)}), bf16[1024,1,2048]{2,0,1:T(8,128)(2,1)}) %all-gather.24.cloned.1.call-update) | async-done | bytes 4194320 | tf_op jit(solution)/shard_map/all_gather | solution.py:86
  469.2 6.9 fusion.135
  476.1 7.7 fusion.138
  483.7 7.7 fusion.141
  491.4 8.1 fusion.144
  506.2 8.7 fusion.147
  514.9 7.8 fusion.150
  522.7 7.8 fusion.153
  530.5 7.9 fusion.156
  548.6 43.5 %broadcast_multiply_fusion.3 = (f32[4,64,64,512]{3,2,1,0:T(8,128)}, f32[4,64,64,512]{3,2,1,0:T(8,128)}, f32[4,64,64,512]{3,2,1,0:T(8,128)}) fusion(f32[4,64,512]{2,1,0:T(8,128)} %bitcast.836, f32[4,64,512]{2,1,0:T(8,128)} %bitcast.834, f32[4,64,512]{2,1,0:T(8,128)} %bitcast.832, f32[4,64,512]{2,1,0:T(8,128)} %bitcast.830, f32[16384,512]{1,0:T(8,128)} %param.37, ...), kind=kLoop, calls=%fused_computation.43 | loop fusion | flops 50331648 | bytes 137363456 | tf_op jit(solution)/shard_map/mul | solution.py:140
  594.4 70.6 %fusion.4 = (f32[4,64,512]{2,1,0:T(8,128)}, f32[4,64,512]{2,1,0:T(8,128)}, f32[4,512]{1,0:T(4,128)S(1)}, f32[4,512]{1,0:T(4,128)S(1)}, f32[4,512]{1,0:T(4,128)S(...) fusion(f32[4,64,64,512]{3,2,1,0:T(8,128)} %bitcast.822, ...), kind=kLoop, calls=%fused_computation.15 | loop fusion | flops 284680192 | bytes 177243136 | tf_op jit(solution)/shard_map/reduce_sum | solution.py:141
  681.4 64.7 %bitcast_add_fusion = f32[16384,512]{1,0:T(8,128)} fusion(f32[4,64,64,512]{3,2,1,0:T(8,128)} %get-tuple-element.48, f32[4,64,64,512]{3,2,1,0:T(8,128)} %get-tuple-element.47, f32[4,64,64,512]{3,2,1,0:T(8,128)} %get-tuple-element.46, f32[4,64,64,512]{3,2,1,0:T(8,128)} %get-tuple-element.44, f32[16384,512]{1,0:T(8,128)} %param.37, f32[4,64,512]{2,1,0:T(8,128)} %bitcast.838, ...), kind=kLoop, calls=%fused_computation | loop fusion | flops 67108864 | bytes 203423744 | tf_op jit(solution)/shard_map/add | solution.py:147
  746.1 7.0 all-gather.26.cloned.1.call-done
  756.6 73.9 %all-gather.22.cloned.1.call-done = bf16[512,1,4096]{0,2,1:T(8,128)(2,1)} async-done(((bf16[512,1,256]{0,2,1:T(8,128)(2,1)}), bf16[512,1,4096]{0,2,1:T(8,128)(2,1)}) %all-gather.22.cloned.1.call-update) | async-done | bytes 4194320 | tf_op jit(solution)/shard_map/all_gather | solution.py:164
  833.9 73.9 %all-gather.18.cloned.1.call-done = bf16[512,1,4096]{0,2,1:T(8,128)(2,1)} async-done(((bf16[512,1,256]{0,2,1:T(8,128)(2,1)}), bf16[512,1,4096]{0,2,1:T(8,128)(2,1)}) %all-gather.18.cloned.1.call-update) | async-done | bytes 4194320 | tf_op jit(solution)/shard_map/all_gather | solution.py:164
  911.3 73.9 %all-gather.14.cloned.1.call-done = bf16[512,1,4096]{0,2,1:T(8,128)(2,1)} async-done(((bf16[512,1,256]{0,2,1:T(8,128)(2,1)}), bf16[512,1,4096]{0,2,1:T(8,128)(2,1)}) %all-gather.14.cloned.1.call-update) | async-done | bytes 4194320 | tf_op jit(solution)/shard_map/all_gather | solution.py:164
  (166 shorter events, 101.9 us)
Async XLA Ops:
  8.0 745.1 %copy-start = (bf16[4096,256]{1,0:T(8,128)(2,1)S(1)}, bf16[4096,256]{1,0:T(8,128)(2,1)}, u32[]{:S(2)}) copy-start(bf16[4096,256]{1,0:T(8,128)(2,1)} %param.34) | copy-start | bytes 6291460
  8.0 13.2 %copy-start.1 = (bf16[2048,160]{0,1:T(8,128)(2,1)S(1)}, bf16[2048,160]{0,1:T(8,128)(2,1)}, u32[]{:S(2)}) copy-start(bf16[2048,160]{0,1:T(8,128)(2,1)} %param.24) | copy-start | bytes 1966084
  8.0 42.4 %all-reduce.8.cloned.1.call-start = ((), (), s32[]{:S(2)}) async-start(), calls=%async_computation.18 | async-start | bytes 524288 | tf_op jit(solution)/shard_map/psum | solution.py:68
  21.2 43.0 %copy-start.8 = (bf16[64,1,2048]{2,0,1:T(8,128)(2,1)}, bf16[64,1,2048]{2,0,1:T(8,128)(2,1)S(1)}, u32[]{:S(2)}) copy-start(bf16[64,1,2048]{2,0,1:T(8,128)(2,1)S(1)} %get-tuple-element.73) | copy-start | bytes 786436
  21.2 39.1 %copy-start.9 = (bf16[64,1,2048]{2,0,1:T(8,128)(2,1)S(1)}, bf16[64,1,2048]{2,0,1:T(8,128)(2,1)}, u32[]{:S(2)}) copy-start(bf16[64,1,2048]{2,0,1:T(8,128)(2,1)} %get-tuple-element.74) | copy-start | bytes 786436
  21.2 39.1 %copy-start.20 = (f32[1,2048]{1,0:T(1,128)S(1)}, f32[1,2048]{1,0:T(1,128)}, u32[]{:S(2)}) copy-start(f32[1,2048]{1,0:T(1,128)} %get-tuple-element.67) | copy-start | bytes 24580
  29.2 52.6 %all-reduce.6.cloned.1.call-start = ((), (), s32[]{:S(2)}) async-start(), calls=%async_computation.17 | async-start | bytes 262144 | tf_op jit(solution)/shard_map/psum | solution.py:84
  62.4 84.2 %all-gather.10.cloned.1.call-start = ((), (), s32[]{:S(2)}) async-start(), calls=%async_computation.4 | async-start | bytes 4456448 | tf_op jit(solution)/shard_map/all_gather | solution.py:86
  63.0 160.7 %all-gather.16.cloned.1.call-start = ((), (), s32[]{:S(2)}) async-start(), calls=%async_computation.8 | async-start | bytes 4456448 | tf_op jit(solution)/shard_map/all_gather | solution.py:86
  63.6 242.5 %all-gather.12.cloned.1.call-start = ((), (), s32[]{:S(2)}) async-start(), calls=%async_computation.5 | async-start | bytes 4456448 | tf_op jit(solution)/shard_map/all_gather | solution.py:36
  64.1 362.0 %all-gather.20.cloned.1.call-start = ((), (), s32[]{:S(2)}) async-start(), calls=%async_computation.11 | async-start | bytes 4456448 | tf_op jit(solution)/shard_map/all_gather | solution.py:86
  64.9 404.3 %all-gather.24.cloned.1.call-start = ((), (), s32[]{:S(2)}) async-start(), calls=%async_computation.14 | async-start | bytes 4456448 | tf_op jit(solution)/shard_map/all_gather | solution.py:86
  65.6 475.8 %reduce-scatter.7.cloned.1.call-start = ((), (), s32[]{:S(2)}) async-start(), calls=%async_computation.9 | async-start | bytes 3145728 | tf_op jit(solution)/shard_map/reduce_scatter | solution.py:112
  129.2 255.6 %copy-start.11 = (bf16[1024,1,192]{2,0,1:T(8,128)(2,1)}, bf16[1024,1,192]{2,0,1:T(8,128)(2,1)S(1)}, u32[]{:S(2)}) copy-start(bf16[1024,1,192]{2,0,1:T(8,128)(2,1)S(1)} %all_gather.44) | copy-start | bytes 1179652
  230.5 7.9 copy-start.18
  238.4 7.7 copy-start.19
  246.1 11.0 %copy-start.15 = (f32[64,1,64]{2,0,1:T(8,128)S(1)}, f32[64,1,64]{2,0,1:T(8,128)}, u32[]{:S(2)}) copy-start(f32[64,1,64]{2,0,1:T(8,128)} %get-tuple-element.31) | copy-start | bytes 49156
  257.1 286.8 %reduce-scatter.5.cloned.1.call-start = ((), (), s32[]{:S(2)}) async-start(), calls=%async_computation.6 | async-start | bytes 3145728 | tf_op jit(solution)/shard_map/reduce_scatter | solution.py:112
  337.2 49.1 %copy-start.14 = (f32[64,1,64]{2,0,1:T(8,128)S(1)}, f32[64,1,64]{2,0,1:T(8,128)}, u32[]{:S(2)}) copy-start(f32[64,1,64]{2,0,1:T(8,128)} %get-tuple-element.30) | copy-start | bytes 49156
  340.2 206.0 %reduce-scatter.11.cloned.1.call-start = ((), (), s32[]{:S(2)}) async-start(), calls=%async_computation.15 | async-start | bytes 3145728 | tf_op jit(solution)/shard_map/reduce_scatter | solution.py:112
  426.1 65.3 %copy-start.10 = (bf16[1024,1,192]{2,0,1:T(8,128)(2,1)}, bf16[1024,1,192]{2,0,1:T(8,128)(2,1)S(1)}, u32[]{:S(2)}) copy-start(bf16[1024,1,192]{2,0,1:T(8,128)(2,1)S(1)} %all_gather.50) | copy-start | bytes 1179652
  491.4 11.1 %slice-start.1 = ((bf16[1024,1,192]{2,0,1:T(8,128)(2,1)}), bf16[1024,1,64]{2,0,1:T(8,128)(2,1)S(1)}, s32[]{:S(2)}) async-start(bf16[1024,1,192]{2,0,1:T(8,128)(2,1)} %copy-done.11), calls=%async_computation.20 | async-start | bytes 524288 | tf_op jit(solution)/shard_map/slice | solution.py:120
  491.4 11.1 %copy-start.13 = (bf16[64,256]{1,0:T(8,128)(2,1)S(1)}, bf16[64,256]{1,0:T(8,128)(2,1)}, u32[]{:S(2)}) copy-start(bf16[64,256]{1,0:T(8,128)(2,1)} %param.27) | copy-start | bytes 98308
  491.4 11.1 %copy-start.16 = (f32[256]{0:T(256)S(1)}, f32[256]{0:T(256)}, u32[]{:S(2)}) copy-start(f32[256]{0:T(256)} %param.28) | copy-start | bytes 3076
  502.4 89.6 %reduce-scatter.9.cloned.1.call-start = ((), (), s32[]{:S(2)}) async-start(), calls=%async_computation.12 | async-start | bytes 3145728 | tf_op jit(solution)/shard_map/reduce_scatter | solution.py:112
  541.4 211.7 %all-gather.26.cloned.1.call-start = ((), (), s32[]{:S(2)}) async-start(), calls=%async_computation.16 | async-start | bytes 4456448 | tf_op jit(solution)/shard_map/all_gather | solution.py:164
  665.0 10.8 %copy-start.4 = (bf16[512,1,1024]{0,2,1:T(8,128)(2,1)S(1)}, bf16[512,1,1024]{0,2,1:T(8,128)(2,1)}, u32[]{:S(2)}) copy-start(bf16[512,1,1024]{0,2,1:T(8,128)(2,1)} %reduce-scatter.9.cloned.1.call-done) | copy-start | bytes 3145732
  665.0 11.1 %copy-start.2 = (bf16[512,1,1024]{0,2,1:T(8,128)(2,1)S(1)}, bf16[512,1,1024]{0,2,1:T(8,128)(2,1)}, u32[]{:S(2)}) copy-start(bf16[512,1,1024]{0,2,1:T(8,128)(2,1)} %reduce-scatter.7.cloned.1.call-done) | copy-start | bytes 3145732
  665.0 11.4 %copy-start.3 = (bf16[512,1,1024]{0,2,1:T(8,128)(2,1)S(1)}, bf16[512,1,1024]{0,2,1:T(8,128)(2,1)}, u32[]{:S(2)}) copy-start(bf16[512,1,1024]{0,2,1:T(8,128)(2,1)} %reduce-scatter.5.cloned.1.call-done) | copy-start | bytes 3145732
  678.4 152.0 %all-gather.22.cloned.1.call-start = ((), (), s32[]{:S(2)}) async-start(), calls=%async_computation.13 | async-start | bytes 4456448 | tf_op jit(solution)/shard_map/all_gather | solution.py:164
  679.0 228.8 %all-gather.18.cloned.1.call-start = ((), (), s32[]{:S(2)}) async-start(), calls=%async_computation.10 | async-start | bytes 4456448 | tf_op jit(solution)/shard_map/all_gather | solution.py:164
  679.6 305.6 %all-gather.14.cloned.1.call-start = ((), (), s32[]{:S(2)}) async-start(), calls=%async_computation.7 | async-start | bytes 4456448 | tf_op jit(solution)/shard_map/all_gather | solution.py:164
  (8 other events, 29.8 us)
Sparse Core Ops, SparseCore 0:
  29.3 20.9 all-reduce.7
  62.5 19.2 all-reduce.5
  257.2 8.0 reduce-scatter.6
  340.3 8.6 reduce-scatter.4
  502.6 8.1 reduce-scatter.10
  541.5 8.0 reduce-scatter.8
Sparse Core Ops, SparseCore 1:
  65.6 80.9 all-gather.9
  149.3 74.3 all-gather.15
  226.3 79.7 all-gather.11
  308.9 82.1 all-gather.19
  393.8 75.4 all-gather.23
  678.5 74.5 all-gather.25
  756.1 74.3 all-gather.21
  833.5 74.3 all-gather.17
  910.9 74.3 all-gather.13
where the time goes:
time: 1000 us; the launch traced here: 998 us
  waiting for transfers between devices  410 us (41%)
  other arithmetic  213 us (21%)
  blocking collectives  178 us (18%)
  matrix products  159 us (16%)
  local copies, waits for them, and re-layouts  20.5 us (2%)
  between operations  16.6 us (2%)
    all_gather x4, waiting for transfers between devices, per_device(): lax.all_gather(gated, 'wide', axis=2, tiled=True)  229 us
    all_gather x4, blocking collectives, per_device(): prepare_small_all = lax.all_gather(small, 'wide', axis=0, tiled=True)  175 us
    all_gather x4, waiting for transfers between devices, per_device(): prepare_normed_all = lax.all_gather(normed, 'wide', axis=0, tiled=True)  137 us
    dot_general x16, matrix products, per_device(): jnp.einsum('smd,de->sme', mixed_input, weights[selector_index], preferred...  124 us
    reduce_sum x1, other arithmetic, per_device(): jnp.sum(present_acceptor[:, :, None, :] * (recurrence_present_symbol + ea...  70.6 us
    add x1, other arithmetic, per_device(): forget_now[:, :, None, :] * recurrence_present_symbol + dyadic_tensor  64.7 us
    mul x1, other arithmetic, per_device(): dyadic_tensor = key_now[:, :, None, :] * value_now[:, None, :, :]  43.5 us
    psum x1, waiting for transfers between devices, per_device(): lax.psum(partial_mix, 'narrow')  21.1 us
  transfers between devices with their start and end apart: 15, of which 10 were waited for; matrix products, arithmetic and copies ran while one was open for 27% of the time, Pallas kernels for 0%

commit v1 on v0

--- a/solution.py
+++ b/solution.py
@@ -1,13 +1,16 @@
+import functools
 import jax
 import jax.numpy as jnp
 from jax import lax
+from jax.experimental import pallas as pl
+from jax.experimental.pallas import tpu as pltpu
 from jax.sharding import PartitionSpec as P
 
 CHANNEL_SPAN = 64
 FEATURE_EXTENT = 4096
 
 
-def per_device(
+def plain_device(
     sublevel_symbol_entries,
     prior_symbol_memory,
     entry_scaling_multiplier,
@@ -175,6 +178,385 @@
     )
 
 
+PLANES = 4
+F32 = jnp.float32
+BF16 = jnp.bfloat16
+
+
+def pairs(move):
+    moved = [(here, move(here)) for here in range(4 * PLANES)]
+    return [(here, there) for here, there in moved if there is not None]
+
+
+def x_mate(here):
+    return here ^ 1
+
+
+def y_mate(here):
+    return here ^ 2
+
+
+def z_mate(here):
+    return here ^ 4
+
+
+def z_middle(here):
+    return {1: here + 4, 2: here - 4}.get(here // 4)
+
+
+def z_outward(here):
+    return {1: here - 4, 2: here + 4}.get(here // 4)
+
+
+def z_shift(amount):
+    return lambda here: (here + 4 * amount) % (4 * PLANES)
+
+
+def send(block, move):
+    return lax.ppermute(block, "wide", pairs(move))
+
+
+def swap(block):
+    return lax.ppermute(block, "narrow", [(0, 1), (1, 0)])
+
+
+def project_kernel(now_ref, before_ref, small_ref, raise_ref, blend_ref, *refs):
+    weights, out_ref, total_ref = refs[:8], refs[8], refs[9]
+    step = pl.program_id(0)
+    rank = raise_ref.shape[1]
+    tile = 256
+    for start in range(0, now_ref.shape[0], tile):
+        rows = slice(start, start + tile)
+        now = now_ref[rows, :].astype(F32)
+        shift = before_ref[rows, :].astype(F32) - now
+        for kind in range(4):
+            low = jnp.dot(
+                small_ref[rows, kind * rank : (kind + 1) * rank],
+                raise_ref[kind],
+                preferred_element_type=F32,
+            )
+            mixed = (now + shift * (blend_ref[kind : kind + 1, :] + low)).astype(BF16)
+            for side in range(2):
+                term = jnp.dot(mixed, weights[2 * kind + side][...], preferred_element_type=F32)
+                slot = 2 * kind + side
+
+                @pl.when(step == 0)
+                def _():
+                    total_ref[slot, rows, :] = term
+
+                @pl.when(step > 0)
+                def _():
+                    total_ref[slot, rows, :] += term
+
+    @pl.when(step == pl.num_programs(0) - 1)
+    def _():
+        out_ref[...] = total_ref[...].astype(BF16)
+
+
+def project(now, before, small, raising, blending, weights):
+    rows, features = now.shape
+    columns = weights[0].shape[1]
+    depth = 512
+    return pl.pallas_call(
+        project_kernel,
+        grid=(features // depth,),
+        in_specs=[
+            pl.BlockSpec((rows, depth), lambda k: (0, k)),
+            pl.BlockSpec((rows, depth), lambda k: (0, k)),
+            pl.BlockSpec(small.shape, lambda k: (0, 0)),
+            pl.BlockSpec((4, raising.shape[1], depth), lambda k: (0, 0, k)),
+            pl.BlockSpec((4, depth), lambda k: (0, k)),
+        ]
+        + [pl.BlockSpec((depth, columns), lambda k: (k, 0))] * 8,
+        out_specs=pl.BlockSpec((8, rows, columns), lambda k: (0, 0, 0)),
+        out_shape=jax.ShapeDtypeStruct((8, rows, columns), BF16),
+        scratch_shapes=[pltpu.VMEM((8, rows, columns), F32)],
+        compiler_params=pltpu.CompilerParams(vmem_limit_bytes=48 * 2**20),
+        cost_estimate=pl.CostEstimate(
+            flops=2 * rows * features * columns * 8 + 8 * rows * features * 32,
+            bytes_accessed=16 * features * columns + 4 * rows * features + 16 * rows * columns,
+            transcendentals=0,
+        ),
+        name="project",
+    )(now, before, small, raising, blending, *weights)
+
+
+def recall_kernel(steps, *refs):
+    state_ref, line_refs, refs = refs[0], refs[1 : 2 + steps], refs[2 + steps :]
+    decay_ref, bonus_ref, gain_ref, offset_ref, out_ref, reach_ref, total_ref = refs
+    part = pl.program_id(1)
+    depth = state_ref.shape[1]
+    span = state_ref.shape[2]
+    width = state_ref.shape[3]
+    now_ref = line_refs[steps]
+
+    @pl.when(part == 0)
+    def _():
+        reach = now_ref[0]
+        for step in range(steps):
+            reach = reach * decay_ref[step]
+        reach_ref[...] = reach
+        total_ref[...] = jnp.zeros_like(total_ref)
+
+    for start in range(0, width, 128):
+        lanes = slice(start, start + 128)
+        total = total_ref[:, lanes]
+        reach = reach_ref[pl.ds(pl.multiple_of(part * depth, depth), depth), lanes]
+        for row in range(depth):
+            total = total + reach[row : row + 1, :] * state_ref[0, row, :, lanes]
+        total_ref[:, lanes] = total
+
+    @pl.when(part == pl.num_programs(1) - 1)
+    def _():
+        acceptor = now_ref[0]
+        readout = total_ref[...]
+        weight = jnp.sum(acceptor * bonus_ref[...] * now_ref[1], 0, keepdims=True)
+        readout = readout + weight * now_ref[2]
+        for step in reversed(range(steps)):
+            weight = jnp.sum(acceptor * line_refs[step][1], 0, keepdims=True)
+            readout = readout + weight * line_refs[step][2]
+            if step:
+                acceptor = acceptor * decay_ref[step]
+        center = jnp.sum(readout, 0, keepdims=True) * (1.0 / span)
+        offset = readout - center
+        spread = jnp.sum(offset * offset, 0, keepdims=True) * (1.0 / span)
+        scaled = offset * lax.rsqrt(spread + 0.00064)
+        gate = now_ref[3]
+        grouped = scaled * gain_ref[...] + offset_ref[...]
+        out_ref[...] = (grouped * (gate / (1.0 + jnp.exp(-gate)))).astype(BF16)
+
+
+def recall(state, lines, decay, bonus, gain, offset):
+    heads, span, _, width = state.shape
+    steps = len(lines) - 1
+    depth = 16
+    column = pl.BlockSpec((span, 1), lambda h, p: (h, 0))
+    return pl.pallas_call(
+        functools.partial(recall_kernel, steps),
+        grid=(heads, span // depth),
+        in_specs=[pl.BlockSpec((1, depth, span, width), lambda h, p: (h, p, 0, 0))]
+        + [pl.BlockSpec((4, span, width), lambda h, p: (0, h, 0))] * (steps + 1)
+        + [pl.BlockSpec((4, span, width), lambda h, p: (0, h, 0))]
+        + [column] * 3,
+        out_specs=pl.BlockSpec((span, width), lambda h, p: (h, 0)),
+        out_shape=jax.ShapeDtypeStruct((heads * span, width), BF16),
+        scratch_shapes=[pltpu.VMEM((span, width), F32), pltpu.VMEM((span, width), F32)],
+        compiler_params=pltpu.CompilerParams(vmem_limit_bytes=32 * 2**20),
+        cost_estimate=pl.CostEstimate(
+            flops=2 * heads * span * span * width,
+            bytes_accessed=4 * heads * span * span * width,
+            transcendentals=heads * span * width,
+        ),
+        name="recall",
+    )(state, *lines, decay, bonus, gain, offset)
+
+
+def renew_kernel(state_ref, *refs):
+    line_refs, decay_ref, out_ref, keep_ref, key_ref = refs[:-4], *refs[-4:]
+    steps = len(line_refs)
+    part = pl.program_id(1)
+    depth = state_ref.shape[1]
+    width = state_ref.shape[3]
+
+    @pl.when(part == 0)
+    def _():
+        keep = jnp.ones_like(keep_ref)
+        for step in reversed(range(steps)):
+            key_ref[step] = line_refs[step][1] * keep
+            keep = keep * decay_ref[step]
+        keep_ref[...] = keep
+
+    for start in range(0, width, 128):
+        lanes = slice(start, start + 128)
+        rows = pl.ds(pl.multiple_of(part * depth, depth), depth)
+        keep = keep_ref[rows, lanes]
+        keys = [key_ref[step, rows, lanes] for step in range(steps)]
+        values = [line_refs[step][2, :, lanes] for step in range(steps)]
+        for row in range(depth):
+            here = slice(row, row + 1)
+            total = keep[here] * state_ref[0, row, :, lanes]
+            for step in range(steps):
+                total = total + keys[step][here] * values[step]
+            out_ref[0, row, :, lanes] = total
+
+
+def renew(state, lines, decay):
+    heads, span, _, width = state.shape
+    depth = 16
+    steps = len(lines)
+    block = pl.BlockSpec((1, depth, span, width), lambda h, p: (h, p, 0, 0))
+    return pl.pallas_call(
+        renew_kernel,
+        grid=(heads, span // depth),
+        in_specs=[block] + [pl.BlockSpec((4, span, width), lambda h, p: (0, h, 0))] * (steps + 1),
+        out_specs=block,
+        out_shape=jax.ShapeDtypeStruct(state.shape, F32),
+        scratch_shapes=[pltpu.VMEM((span, width), F32), pltpu.VMEM((steps, span, width), F32)],
+        compiler_params=pltpu.CompilerParams(vmem_limit_bytes=32 * 2**20),
+        cost_estimate=pl.CostEstimate(
+            flops=9 * heads * span * span * width,
+            bytes_accessed=8 * heads * span * span * width,
+            transcendentals=0,
+        ),
+        name="renew",
+    )(state, *lines, decay)
+
+
+def boxed_device(
+    sublevel_symbol_entries,
+    prior_symbol_memory,
+    entry_scaling_multiplier,
+    entry_scaling_offset,
+    learned_blending,
+    blending_lowering_coefficients,
+    blending_raising_coefficients,
+    fading_lowering_coefficients,
+    fading_raising_coefficients,
+    learned_fading,
+    immediate_item_premium,
+    acceptor_projection,
+    lookup_projection,
+    payload_projection,
+    gating_projection,
+    emission_projection,
+    group_scaling_multiplier,
+    group_scaling_offset,
+    dialogue_group_memory,
+):
+    rank = blending_raising_coefficients.shape[1]
+    chats, moves, features = sublevel_symbol_entries.shape
+    narrow_rows = dialogue_group_memory.shape[1]
+    local_width = emission_projection.shape[1]
+    groups = local_width // CHANNEL_SPAN
+    wide, narrow = lax.axis_index("wide"), lax.axis_index("narrow")
+    z, y, x = wide // 4, (wide // 2) % 2, wide % 2
+    weights = (acceptor_projection, lookup_projection, payload_projection, gating_projection)
+
+    def in_order(bit, mine, theirs):
+        first = bit == 0
+        return [jnp.where(first, mine, theirs), jnp.where(first, theirs, mine)]
+
+    def gather(block):
+        near = jnp.stack(in_order(z % 2, block, send(block, z_mate)))
+        across = send(near, z_middle)
+        far = jnp.where((z == 1) | (z == 2), across, send(across, z_outward))
+        near = jnp.stack(in_order(y, near, send(near, y_mate)), 1)
+        far = jnp.stack(in_order(y, far, send(far, y_mate)), 1)
+        both = jnp.stack(in_order(z // 2, near, far))
+        return both.reshape((8 * block.shape[0],) + block.shape[1:])
+
+    all_weights = []
+    for weight in weights:
+        all_weights += [weight, send(weight, x_mate)]
+
+    prior_all = gather(prior_symbol_memory)
+    floats = sublevel_symbol_entries.astype(F32).transpose(1, 0, 2)
+    sums = jnp.stack([jnp.sum(floats, -1), jnp.sum(floats * floats, -1)])
+    sums = sums + swap(sums)
+    center = sums[0][..., None] / FEATURE_EXTENT
+    spread = sums[1][..., None] / FEATURE_EXTENT - center * center
+    normed = (
+        (floats - center) * lax.rsqrt(spread + 1e-05) * entry_scaling_multiplier
+        + entry_scaling_offset
+    ).astype(BF16)
+    normed_all = [gather(normed[step]) for step in range(moves)]
+
+    previous = jnp.concatenate([prior_symbol_memory[None], normed[:-1]], 0)
+    normed_float = normed.astype(F32)
+    shifted = previous.astype(F32) - normed_float
+    blended = (normed_float + shifted * learned_blending[0]).astype(BF16)
+    partial_mix = jnp.einsum(
+        "msd,dr->msr", blended, blending_lowering_coefficients, preferred_element_type=F32
+    )
+    hidden = jnp.tanh(partial_mix + swap(partial_mix)).astype(BF16)
+    decay_shift = jnp.einsum(
+        "msr,rd->msd",
+        hidden[..., :rank],
+        blending_raising_coefficients[0],
+        preferred_element_type=F32,
+    )
+    decay_mix = (normed_float + shifted * (learned_blending[1] + decay_shift)).astype(BF16)
+    partial_decay = jnp.einsum(
+        "msd,dr->msr", decay_mix, fading_lowering_coefficients, preferred_element_type=F32
+    )
+    decay_hidden = jnp.tanh(partial_decay + swap(partial_decay)).astype(BF16)
+    small = jnp.concatenate([hidden[..., rank:], decay_hidden], -1).transpose(1, 0, 2)
+    small_width = small.shape[-1]
+    small_all = gather(small.reshape(chats, moves * small_width))
+    small_all = small_all.reshape(-1, moves, small_width)
+
+    half = small_all.shape[0] // 2
+    decay_mine = lax.dynamic_slice_in_dim(small_all[..., 4 * rank :], narrow * half, half, 0)
+    decay_theirs = send(decay_mine, x_mate)
+
+    def weave(mine, theirs):
+        shape = mine.shape[:-2] + (-1, chats, mine.shape[-1])
+        both = jnp.stack(in_order(x, mine.reshape(shape), theirs.reshape(shape)), -3)
+        return both.reshape(mine.shape[:-2] + (narrow_rows, mine.shape[-1]))
+
+    decay_rows = weave(decay_mine.transpose(1, 0, 2), decay_theirs.transpose(1, 0, 2))
+    decay_log = learned_fading[:, None] + jnp.einsum(
+        "rd,msr->mds", fading_raising_coefficients, decay_rows, preferred_element_type=F32
+    )
+    decay = jnp.exp(-jnp.exp(decay_log))
+
+    plane = emission_projection.shape[0] // PLANES
+    piece = plane // 2
+    emission = []
+    for shift in range(PLANES):
+        start = ((z + PLANES - shift) % PLANES) * plane
+        if shift == 0:
+            emission.append(lax.dynamic_slice_in_dim(emission_projection, start, plane, 0))
+        else:
+            own = lax.dynamic_slice_in_dim(
+                emission_projection, start + narrow * piece, piece, 0
+            )
+            own = send(own, z_shift(-shift))
+            emission.append(jnp.concatenate(in_order(narrow, own, swap(own)), 0))
+    emission = jnp.concatenate(emission, 1)
+    emission = emission.reshape(2, 2, local_width, PLANES * local_width)
+    emission = jnp.stack(in_order(y, emission[0], emission[1]))
+    emission = jnp.stack(in_order(x, emission[:, 0], emission[:, 1]), 1)
+    emission = emission.reshape(plane, PLANES * local_width)
+
+    state = dialogue_group_memory.reshape(groups, CHANNEL_SPAN, CHANNEL_SPAN, narrow_rows)
+    bonus = immediate_item_premium[:, None]
+    gain = group_scaling_multiplier[:, None]
+    offset = group_scaling_offset[:, None]
+    lines, results = [], []
+    for step in range(moves):
+        before = normed_all[step - 1] if step else prior_all
+        partial = project(
+            normed_all[step],
+            before,
+            small_all[:, step, : 4 * rank],
+            blending_raising_coefficients[1:],
+            learned_blending[2:],
+            all_weights,
+        )
+        kept = lax.dynamic_slice_in_dim(partial, narrow * half, half, 1)
+        given = lax.dynamic_slice_in_dim(partial, (1 - narrow) * half, half, 1)
+        whole = kept.astype(F32) + swap(given).astype(F32)
+        whole = whole.reshape(4, 2, half, local_width)
+        theirs = send(whole[:, 1].astype(BF16), x_mate)
+        line = weave(whole[:, 0], theirs.astype(F32)).transpose(0, 2, 1)
+        lines.append(line)
+        gated = recall(state, lines, decay, bonus, gain, offset)
+        gated = jnp.concatenate([gated, send(gated, x_mate)], 0)
+        gated = jnp.concatenate([gated, send(gated, y_mate)], 0)
+        product = jnp.einsum("cs,ce->se", gated, emission, preferred_element_type=F32)
+        total = product[:, :local_width]
+        for shift in range(1, PLANES):
+            columns = product[:, shift * local_width : (shift + 1) * local_width]
+            total = total + send(columns.astype(BF16), z_shift(shift)).astype(F32)
+        results.append(total.astype(BF16))
+    final = renew(state, lines, decay)
+    return (
+        jnp.stack(results, 1),
+        final.reshape(groups * CHANNEL_SPAN * CHANNEL_SPAN, narrow_rows),
+    )
+
+
 def solution(mesh):
     placed = (
         P("wide", None, "narrow"),
@@ -197,8 +579,10 @@
         P("wide"),
         P("wide", "narrow"),
     )
+    boxed = mesh.shape["wide"] == PLANES * 4 and mesh.shape["narrow"] == 2
+    body = boxed_device if boxed else plain_device
     return jax.shard_map(
-        per_device,
+        body,
         mesh=mesh,
         in_specs=placed,
         out_specs=(P("narrow", None, "wide"), P("wide", "narrow")),

time: 1000 us -> 682 us (0.68)
  Pallas kernels: 0 us -> 212 us
  blocking collectives: 178 us -> 0 us
  other arithmetic: 213 us -> 44.4 us
  waiting for transfers between devices: 410 us -> 251 us
  matrix products: 159 us -> 10.1 us
  starting transfers between devices: 0.83 us -> 94.9 us
  local copies, waits for them, and re-layouts: 20.5 us -> 60.8 us
  between operations: 16.6 us -> 2.24 us
    all_gather x9 -> x0, waiting for transfers between devices: 370 us -> none  [the longest x4 229 us: per_device(): lax.all_gather(gated, 'wide', axis=2, tiled=True)]
    ppermute x0 -> x72, waiting for transfers between devices: none -> 251 us  [the longest x62 251 us: send(): return lax.ppermute(block, 'wide', pairs(move))]
    pallas_call x0 -> x9, Pallas kernels: none -> 212 us  [the longest x4 111 us: project(): pl.pallas_call(project_kernel, grid=(features // depth,), in_specs=[pl.Bl...]
    all_gather x4 -> x0, blocking collectives: 175 us -> none  [per_device(): prepare_small_all = lax.all_gather(small, 'wide', axis=0, tiled=True)]
    dot_general x32 -> x7, matrix products: 159 us -> 10.1 us  [the longest x4 5.09 us: boxed_device(): jnp.einsum('cs,ce->se', gated, emission, preferred_element_type=F32)]
    ppermute x0 -> x72, starting transfers between devices: none -> 94.9 us  [the longest x62 92.4 us: send(): return lax.ppermute(block, 'wide', pairs(move))]
    reduce_sum x7 -> x1, other arithmetic: 76 us -> 2.61 us  [boxed_device(): sums = jnp.stack([jnp.sum(floats, -1), jnp.sum(floats * floats, -1)])]
    add x1 -> x5, other arithmetic: 64.7 us -> 0.93 us  [the longest x4 0.92 us: boxed_device(): whole = kept.astype(F32) + swap(given).astype(F32)]
  transfers between devices with their start and end apart: 15 -> 72, of which waited for: 10 -> 30; matrix products, arithmetic and copies ran while one was open for 27% -> 13% of each run, Pallas kernels for 0% -> 21%
where the time goes in v1:
time: 682 us; the launch traced here: 675 us
  waiting for transfers between devices  251 us (37%)
  Pallas kernels  212 us (31%)
  starting transfers between devices  94.9 us (14%)
  local copies, waits for them, and re-layouts  60.8 us (9%)
  other arithmetic  44.4 us (7%)
  matrix products  10.1 us (1%)
    ppermute x62, waiting for transfers between devices, send(): return lax.ppermute(block, 'wide', pairs(move))  251 us
    pallas_call x4, Pallas kernels, project(): pl.pallas_call(project_kernel, grid=(features // depth,), in_specs=[pl.Bl...  111 us
    ppermute x62, starting transfers between devices, send(): return lax.ppermute(block, 'wide', pairs(move))  92.4 us
    pallas_call x4, Pallas kernels, recall(): pl.pallas_call(functools.partial(recall_kernel, steps), grid=(heads, span...  69.8 us
    pallas_call x1, Pallas kernels, renew(): pl.pallas_call(renew_kernel, grid=(heads, span // depth), in_specs=[block...  31.8 us
  transfers between devices with their start and end apart: 72, of which 30 were waited for; matrix products, arithmetic and copies ran while one was open for 13% of the time, Pallas kernels for 21%

profile of v1, /device:TPU:0, one launch (start us, length us, event | category | flops | bytes accessed | tf_op | source)
XLA Modules:
  0.0 675.2 jit_solution(5933415617937287388)
XLA Ops:
  38.5 16.5 %collective-permute-done.36 = bf16[64,2048]{1,0:T(8,128)(2,1)} collective-permute-done((bf16[64,2048]{1,0:T(8,128)(2,1)}, bf16[64,2048]{1,0:T(8,128)(2,1)}, u32[]{:S(2)}, u32[]{:S(2)}) %collective-permute-start.36) | collective-permute-done | bytes 262176 | tf_op jit(solution)/shard_map/ppermute | solution.py:216
  70.9 11.7 %maximum_maximum_fusion = bf16[1024,1024]{1,0:T(8,128)(2,1)} fusion(bf16[512,256]{1,0:T(8,128)(2,1)S(1)} %get-tuple-element.98, bf16[512,256]{1,0:T(8,128)(2,1)S(1)} %get-tuple-element.97, bf16[512,256]{1,0:T(8,128)(2,1)S(1)} %get-tuple-element.96, bf16[512,256]{1,0:T(8,128)(2,1)S(1)} %get-tuple-element.95, bf16[512,256]{1,0:T(8,128)(2,1)S(1)} %get-tuple-element.94, ...), kind=kLoop, calls=%fused_computation.10 | loop fusion | flops 14680064 | bytes 4194304 | tf_op jit(solution)/shard_map/concatenate | solution.py:516
  85.8 10.7 %collective-permute-done.16 = bf16[2,64,768]{2,1,0:T(8,128)(2,1)S(1)} collective-permute-done((bf16[2,64,768]{2,1,0:T(8,128)(2,1)S(1)}, bf16[2,64,768]{2,1,0:T(8,128)(2,1)S(1)}, u32[]{:S(2)}, u32[]{:S(2)}) %collective-permute-start.16) | collective-permute-done | bytes 196640 | tf_op jit(solution)/shard_map/ppermute | solution.py:216
  99.6 11.9 %collective-permute-done.2 = bf16[2,64,2048]{2,1,0:T(8,128)(2,1)S(1)} collective-permute-done((bf16[2,64,2048]{2,1,0:T(8,128)(2,1)}, bf16[2,64,2048]{2,1,0:T(8,128)(2,1)S(1)}, u32[]{:S(2)}, u32[]{:S(2)}) %collective-permute-start.2) | collective-permute-done | bytes 524320 | tf_op jit(solution)/shard_map/ppermute | solution.py:216
  113.5 9.2 %collective-permute-done.49 = bf16[2,64,2048]{2,1,0:T(8,128)(2,1)S(1)} collective-permute-done((bf16[2,64,2048]{2,1,0:T(8,128)(2,1)}, bf16[2,64,2048]{2,1,0:T(8,128)(2,1)S(1)}, u32[]{:S(2)}, u32[]{:S(2)}) %collective-permute-start.49) | collective-permute-done | bytes 524320 | tf_op jit(solution)/shard_map/ppermute | solution.py:216
  124.7 9.3 %collective-permute-done.37 = bf16[2,64,2048]{2,1,0:T(8,128)(2,1)S(1)} collective-permute-done((bf16[2,64,2048]{2,1,0:T(8,128)(2,1)}, bf16[2,64,2048]{2,1,0:T(8,128)(2,1)S(1)}, u32[]{:S(2)}, u32[]{:S(2)}) %collective-permute-start.37) | collective-permute-done | bytes 524320 | tf_op jit(solution)/shard_map/ppermute | solution.py:216
  136.6 6.9 %collective-permute-done.61 = bf16[2,64,2048]{2,1,0:T(8,128)(2,1)S(1)} collective-permute-done((bf16[2,64,2048]{2,1,0:T(8,128)(2,1)S(1)}, bf16[2,64,2048]{2,1,0:T(8,128)(2,1)S(1)}, u32[]{:S(2)}, u32[]{:S(2)}) %collective-permute-start.61) | collective-permute-done | bytes 524320 | tf_op jit(solution)/shard_map/ppermute | solution.py:216
  174.5 8.2 %collective-permute-done.4 = bf16[2,64,2048]{2,1,0:T(8,128)(2,1)} collective-permute-done((bf16[2,64,2048]{2,1,0:T(8,128)(2,1)}, bf16[2,64,2048]{2,1,0:T(8,128)(2,1)}, u32[]{:S(2)}, u32[]{:S(2)}) %collective-permute-start.4) | collective-permute-done | bytes 524320 | tf_op jit(solution)/shard_map/ppermute | solution.py:216
  185.8 8.1 %collective-permute-done.51 = bf16[2,64,2048]{2,1,0:T(8,128)(2,1)S(1)} collective-permute-done((bf16[2,64,2048]{2,1,0:T(8,128)(2,1)}, bf16[2,64,2048]{2,1,0:T(8,128)(2,1)S(1)}, u32[]{:S(2)}, u32[]{:S(2)}) %collective-permute-start.51) | collective-permute-done | bytes 524320 | tf_op jit(solution)/shard_map/ppermute | solution.py:216
  195.2 9.9 %collective-permute-done.39 = bf16[2,64,2048]{2,1,0:T(8,128)(2,1)S(1)} collective-permute-done((bf16[2,64,2048]{2,1,0:T(8,128)(2,1)}, bf16[2,64,2048]{2,1,0:T(8,128)(2,1)S(1)}, u32[]{:S(2)}, u32[]{:S(2)}) %collective-permute-start.39) | collective-permute-done | bytes 524320 | tf_op jit(solution)/shard_map/ppermute | solution.py:216
  220.2 10.3 %collective-permute-done.5 = bf16[2,64,2048]{2,1,0:T(8,128)(2,1)S(1)} collective-permute-done((bf16[2,64,2048]{2,1,0:T(8,128)(2,1)S(1)}, bf16[2,64,2048]{2,1,0:T(8,128)(2,1)S(1)}, u32[]{:S(2)}, u32[]{:S(2)}) %collective-permute-start.5) | collective-permute-done | bytes 524320 | tf_op jit(solution)/shard_map/ppermute | solution.py:216
  232.9 11.5 %collective-permute-done.52 = bf16[2,64,2048]{2,1,0:T(8,128)(2,1)S(1)} collective-permute-done((bf16[2,64,2048]{2,1,0:T(8,128)(2,1)S(1)}, bf16[2,64,2048]{2,1,0:T(8,128)(2,1)S(1)}, u32[]{:S(2)}, u32[]{:S(2)}) %collective-permute-start.52) | collective-permute-done | bytes 524320 | tf_op jit(solution)/shard_map/ppermute | solution.py:216
  246.5 12.4 %collective-permute-done.40 = bf16[2,64,2048]{2,1,0:T(8,128)(2,1)S(1)} collective-permute-done((bf16[2,64,2048]{2,1,0:T(8,128)(2,1)S(1)}, bf16[2,64,2048]{2,1,0:T(8,128)(2,1)S(1)}, u32[]{:S(2)}, u32[]{:S(2)}) %collective-permute-start.40) | collective-permute-done | bytes 524320 | tf_op jit(solution)/shard_map/ppermute | solution.py:216
  261.3 6.8 %collective-permute-done.64 = bf16[2,64,2048]{2,1,0:T(8,128)(2,1)S(1)} collective-permute-done((bf16[2,64,2048]{2,1,0:T(8,128)(2,1)S(1)}, bf16[2,64,2048]{2,1,0:T(8,128)(2,1)S(1)}, u32[]{:S(2)}, u32[]{:S(2)}) %collective-permute-start.64) | collective-permute-done | bytes 524320 | tf_op jit(solution)/shard_map/ppermute | solution.py:216
  271.5 27.9 %project.6 = bf16[8,512,256]{2,1,0:T(8,128)(2,1)} custom-call(bf16[512,2048]{1,0:T(8,128)(2,1)} %bitcast.274, bf16[512,2048]{1,0:T(8,128)(2,1)} %bitcast.276, bf16[512,128]{1,0:T(8,128)(2,1)S(1)} %get-tuple-element.116.small_ref, bf16[4,32,2048]{2,1,0:T(8,128)(2,1)S(1)} %slice.175.raise_ref, f32[4,2048]{1,0:T(4,128)S(1)} %copy-done.8, ...), custom_call_target="tpu_custom_call" | custom-call | flops 4563402752 | bytes 14680064 | tf_op jit(solution)/shard_map/project/pallas_call | solution.py:260
  300.7 27.5 %project.7 = bf16[8,512,256]{2,1,0:T(8,128)(2,1)} custom-call(bf16[512,2048]{1,0:T(8,128)(2,1)} %bitcast.278, bf16[512,2048]{1,0:T(8,128)(2,1)} %bitcast.275, bf16[512,128]{1,0:T(8,128)(2,1)S(1)} %get-tuple-element.115.small_ref, bf16[4,32,2048]{2,1,0:T(8,128)(2,1)S(1)} %slice.175.raise_ref, f32[4,2048]{1,0:T(4,128)S(1)} %copy-done.8, ...), custom_call_target="tpu_custom_call" | custom-call | flops 4563402752 | bytes 14680064 | tf_op jit(solution)/shard_map/project/pallas_call | solution.py:260
  331.0 27.5 %project.5 = bf16[8,512,256]{2,1,0:T(8,128)(2,1)} custom-call(bf16[512,2048]{1,0:T(8,128)(2,1)} %bitcast.277, bf16[512,2048]{1,0:T(8,128)(2,1)} %bitcast.272, bf16[512,128]{1,0:T(8,128)(2,1)S(1)} %get-tuple-element.117.small_ref, bf16[4,32,2048]{2,1,0:T(8,128)(2,1)S(1)} %slice.175.raise_ref, f32[4,2048]{1,0:T(4,128)S(1)} %copy-done.8, ...), custom_call_target="tpu_custom_call" | custom-call | flops 4563402752 | bytes 14680064 | tf_op jit(solution)/shard_map/project/pallas_call | solution.py:260
  359.8 27.7 %project.4 = bf16[8,512,256]{2,1,0:T(8,128)(2,1)} custom-call(bf16[512,2048]{1,0:T(8,128)(2,1)} %bitcast.273, bf16[512,2048]{1,0:T(8,128)(2,1)} %bitcast.271, bf16[512,128]{1,0:T(8,128)(2,1)S(1)} %get-tuple-element.118.small_ref, bf16[4,32,2048]{2,1,0:T(8,128)(2,1)S(1)} %slice.175.raise_ref, f32[4,2048]{1,0:T(4,128)S(1)} %copy-done.8, ...), custom_call_target="tpu_custom_call" | custom-call | flops 4563402752 | bytes 14680064 | tf_op jit(solution)/shard_map/project/pallas_call | solution.py:260
  398.2 6.4 collective-permute-done.66
  405.2 10.7 %collective-permute-done.54 = bf16[4,256,256]{2,1,0:T(8,128)(2,1)S(1)} collective-permute-done((bf16[4,256,256]{2,1,0:T(8,128)(2,1)S(1)}, bf16[4,256,256]{2,1,0:T(8,128)(2,1)S(1)}, u32[]{:S(2)}, u32[]{:S(2)}) %collective-permute-start.54) | collective-permute-done | bytes 524320 | tf_op jit(solution)/shard_map/ppermute | solution.py:216
  450.6 17.6 %recall.7 = bf16[256,512]{1,0:T(8,128)(2,1)S(1)} custom-call(f32[4,64,64,512]{3,2,1,0:T(8,128)} %bitcast.243, f32[4,256,512]{2,1,0:T(8,128)S(1)} %bitcast.229, f32[4,256,512]{2,1,0:T(8,128)S(1)} %bitcast.234, f32[4,256,512]{2,1,0:T(8,128)S(1)} %bitcast.238, f32[4,256,512]{2,1,0:T(8,128)S(1)} %bitcast.241, ...), custom_call_target="tpu_custom_call" | custom-call | flops 16777216 | bytes 33554432 | tf_op jit(solution)/shard_map/recall/pallas_call | solution.py:334
  468.9 17.4 %recall.4 = bf16[256,512]{1,0:T(8,128)(2,1)S(1)} custom-call(f32[4,64,64,512]{3,2,1,0:T(8,128)} %bitcast.244, f32[4,256,512]{2,1,0:T(8,128)S(1)} %bitcast.230, f32[4,256,512]{2,1,0:T(8,128)S(1)} %exponential_bitcast_fusion.refs_2_.refs_3_.refs_4_.refs_5_, f32[256,1]{1,0:T(8,128)S(1)} %copy.54.refs_3_.refs_4_.refs_5_.refs_6_, ...), custom_call_target="tpu_custom_call" | custom-call | flops 16777216 | bytes 33554432 | tf_op jit(solution)/shard_map/recall/pallas_call | solution.py:334
  488.1 17.4 %recall.5 = bf16[256,512]{1,0:T(8,128)(2,1)S(1)} custom-call(f32[4,64,64,512]{3,2,1,0:T(8,128)} %bitcast.245, f32[4,256,512]{2,1,0:T(8,128)S(1)} %bitcast.231, f32[4,256,512]{2,1,0:T(8,128)S(1)} %bitcast.235, f32[4,256,512]{2,1,0:T(8,128)S(1)} %exponential_bitcast_fusion.refs_2_.refs_3_.refs_4_.refs_5_, f32[256,1]{1,0:T(8,128)S(1)} %copy.54.refs_3_.refs_4_.refs_5_.refs_6_, ...), custom_call_target="tpu_custom_call" | custom-call | flops 16777216 | bytes 33554432 | tf_op jit(solution)/shard_map/recall/pallas_call | solution.py:334
  506.0 17.4 %recall.6 = bf16[256,512]{1,0:T(8,128)(2,1)S(1)} custom-call(f32[4,64,64,512]{3,2,1,0:T(8,128)} %bitcast.246, f32[4,256,512]{2,1,0:T(8,128)S(1)} %bitcast.232, f32[4,256,512]{2,1,0:T(8,128)S(1)} %bitcast.236, f32[4,256,512]{2,1,0:T(8,128)S(1)} %bitcast.239, f32[4,256,512]{2,1,0:T(8,128)S(1)} %exponential_bitcast_fusion.refs_2_.refs_3_.refs_4_.refs_5_, ...), custom_call_target="tpu_custom_call" | custom-call | flops 16777216 | bytes 33554432 | tf_op jit(solution)/shard_map/recall/pallas_call | solution.py:334
  527.0 31.8 %renew.1 = f32[4,64,64,512]{3,2,1,0:T(8,128)} custom-call(f32[4,64,64,512]{3,2,1,0:T(8,128)} %bitcast.247, f32[4,256,512]{2,1,0:T(8,128)S(1)} %bitcast.233, f32[4,256,512]{2,1,0:T(8,128)S(1)} %bitcast.237, f32[4,256,512]{2,1,0:T(8,128)S(1)} %bitcast.240, f32[4,256,512]{2,1,0:T(8,128)S(1)} %bitcast.242, ...), custom_call_target="tpu_custom_call" | custom-call | flops 75497472 | bytes 67108864 | tf_op jit(solution)/shard_map/renew/pallas_call | solution.py:388
  568.2 25.3 %collective-permute-done.56 = bf16[512,512]{1,0:T(8,128)(2,1)S(1)} collective-permute-done((bf16[512,512]{1,0:T(8,128)(2,1)S(1)}, bf16[512,512]{1,0:T(8,128)(2,1)S(1)}, u32[]{:S(2)}, u32[]{:S(2)}) %collective-permute-start.56) | collective-permute-done | bytes 524320 | tf_op jit(solution)/shard_map/ppermute | solution.py:216
  604.3 10.9 %collective-permute-done.70 = bf16[512,256]{1,0:T(8,128)(2,1)S(1)} collective-permute-done((bf16[512,256]{1,0:T(8,128)(2,1)S(1)}, bf16[512,256]{1,0:T(8,128)(2,1)S(1)}, u32[]{:S(2)}, u32[]{:S(2)}) %collective-permute-start.70) | collective-permute-done | bytes 262176 | tf_op jit(solution)/shard_map/ppermute | solution.py:216
  618.7 15.4 %collective-permute-start.34 = (bf16[512,256]{1,0:T(8,128)(2,1)S(1)}, bf16[512,256]{1,0:T(8,128)(2,1)S(1)}, u32[]{:S(2)}, u32[]{:S(2)}) collective-permute-start(bf16[512,256]{1,0:T(8,128)(2,1)S(1)} %get-tuple-element.43), channel_id=1, source_target_pairs={{0,16},{2,18},{4,20},{6,22},{8,24},{10,26},{12,28},{14,30},{16,0},... | collective-permute-start | bytes 786440 | tf_op jit(solution)/shard_map/ppermute | solution.py:216
  634.1 11.8 %collective-permute-done.58 = bf16[512,256]{1,0:T(8,128)(2,1)S(1)} collective-permute-done((bf16[512,256]{1,0:T(8,128)(2,1)S(1)}, bf16[512,256]{1,0:T(8,128)(2,1)S(1)}, u32[]{:S(2)}, u32[]{:S(2)}) %collective-permute-start.58) | collective-permute-done | bytes 262176 | tf_op jit(solution)/shard_map/ppermute | solution.py:216
  646.1 10.5 %collective-permute-start.46 = (bf16[512,256]{1,0:T(8,128)(2,1)S(1)}, bf16[512,256]{1,0:T(8,128)(2,1)S(1)}, u32[]{:S(2)}, u32[]{:S(2)}) collective-permute-start(bf16[512,256]{1,0:T(8,128)(2,1)S(1)} %get-tuple-element.46), channel_id=1, source_target_pairs={{0,16},{2,18},{4,20},{6,22},{8,24},{10,26},{12,28},{14,30},{16,0},... | collective-permute-start | bytes 786440 | tf_op jit(solution)/shard_map/ppermute | solution.py:216
  656.6 6.2 collective-permute-done.34
  663.0 9.9 %collective-permute-done.46 = bf16[512,256]{1,0:T(8,128)(2,1)S(1)} collective-permute-done((bf16[512,256]{1,0:T(8,128)(2,1)S(1)}, bf16[512,256]{1,0:T(8,128)(2,1)S(1)}, u32[]{:S(2)}, u32[]{:S(2)}) %collective-permute-start.46) | collective-permute-done | bytes 262176 | tf_op jit(solution)/shard_map/ppermute | solution.py:216
  (335 shorter events, 210.4 us)
Async XLA Ops:
  13.1 50.9 %collective-permute-start.27 = (bf16[512,256]{1,0:T(8,128)(2,1)}, bf16[512,256]{1,0:T(8,128)(2,1)}, u32[]{:S(2)}, u32[]{:S(2)}) collective-permute-start(bf16[512,256]{1,0:T(8,128)(2,1)} %get-tuple-element.22), channel_id=1, source_target_pairs={{0,24},{2,26},{4,28},{6,30},{8,0},{10,2},{12,4},{14,6},{16,8},{18,... | collective-permute-start | bytes 786440 | tf_op jit(solution)/shard_map/ppermute | solution.py:216
  25.2 29.8 %collective-permute-start.36 = (bf16[64,2048]{1,0:T(8,128)(2,1)}, bf16[64,2048]{1,0:T(8,128)(2,1)}, u32[]{:S(2)}, u32[]{:S(2)}) collective-permute-start(bf16[64,2048]{1,0:T(8,128)(2,1)} %get-tuple-element.69), channel_id=1, source_target_pairs={{0,8},{2,10},{4,12},{6,14},{8,0},{10,2},{12,4},{14,6},{16,24},{18,... | collective-permute-start | bytes 786440 | tf_op jit(solution)/shard_map/ppermute | solution.py:216
  25.6 34.4 %collective-permute-start.1 = (bf16[64,2048]{1,0:T(8,128)(2,1)}, bf16[64,2048]{1,0:T(8,128)(2,1)S(1)}, u32[]{:S(2)}, u32[]{:S(2)}) collective-permute-start(bf16[64,2048]{1,0:T(8,128)(2,1)} %get-tuple-element.70), channel_id=1, source_target_pairs={{0,8},{2,10},{4,12},{6,14},{8,0},{10,2},{12,4},{14,6},{16,24},{18,... | collective-permute-start | bytes 786440 | tf_op jit(solution)/shard_map/ppermute | solution.py:216
  32.4 33.0 %collective-permute-start.31 = (bf16[512,256]{1,0:T(8,128)(2,1)S(1)}, bf16[512,256]{1,0:T(8,128)(2,1)S(1)}, u32[]{:S(2)}, u32[]{:S(2)}) collective-permute-start(bf16[512,256]{1,0:T(8,128)(2,1)S(1)} %copy-done.28), channel_id=1, source_target_pairs={{0,8},{2,10},{4,12},{6,14},{8,16},{10,18},{12,20},{14,22},{16,24},... | collective-permute-start | bytes 786440 | tf_op jit(solution)/shard_map/ppermute | solution.py:216
  54.9 215.3 %collective-permute-start.18 = (bf16[2048,256]{1,0:T(8,128)(2,1)}, bf16[2048,256]{1,0:T(8,128)(2,1)}, u32[]{:S(2)}, u32[]{:S(2)}) collective-permute-start(bf16[2048,256]{1,0:T(8,128)(2,1)} %refs_0_.7), channel_id=1, source_target_pairs={{0,2},{2,0},{4,6},{6,4},{8,10},{10,8},{12,14},{14,12},{16,18},{18,... | collective-permute-start | bytes 3145736 | tf_op jit(solution)/shard_map/ppermute | solution.py:216
  64.0 89.0 %collective-permute-start.8 = (bf16[2,64,2048]{2,1,0:T(8,128)(2,1)}, bf16[2,64,2048]{2,1,0:T(8,128)(2,1)}, u32[]{:S(2)}, u32[]{:S(2)}) collective-permute-start(bf16[2,64,2048]{2,1,0:T(8,128)(2,1)} %pad_maximum_fusion.27), channel_id=1, source_target_pairs={{8,16},{10,18},{12,20},{14,22},{16,8},{18,10},{20,12},{22,14},{9,1... | collective-permute-start | bytes 1572872 | tf_op jit(solution)/shard_map/ppermute | solution.py:216
  66.0 31.4 %collective-permute-start.7 = (bf16[2,64,2048]{2,1,0:T(8,128)(2,1)}, bf16[2,64,2048]{2,1,0:T(8,128)(2,1)S(1)}, u32[]{:S(2)}, u32[]{:S(2)}) collective-permute-start(bf16[2,64,2048]{2,1,0:T(8,128)(2,1)} %pad_maximum_fusion.27), channel_id=1, source_target_pairs={{0,4},{2,6},{4,0},{6,2},{8,12},{10,14},{12,8},{14,10},{16,20},{18,... | collective-permute-start | bytes 1572872 | tf_op jit(solution)/shard_map/ppermute | solution.py:216
  82.6 71.9 %collective-permute-start.3 = (bf16[2,64,2048]{2,1,0:T(8,128)(2,1)}, bf16[2,64,2048]{2,1,0:T(8,128)(2,1)}, u32[]{:S(2)}, u32[]{:S(2)}) collective-permute-start(bf16[2,64,2048]{2,1,0:T(8,128)(2,1)} %pad_maximum_fusion.26), channel_id=1, source_target_pairs={{8,16},{10,18},{12,20},{14,22},{16,8},{18,10},{20,12},{22,14},{9,1... | collective-permute-start | bytes 1572872 | tf_op jit(solution)/shard_map/ppermute | solution.py:216
  134.0 30.9 %collective-permute-start.50 = (bf16[2,64,2048]{2,1,0:T(8,128)(2,1)}, bf16[2,64,2048]{2,1,0:T(8,128)(2,1)}, u32[]{:S(2)}, u32[]{:S(2)}) collective-permute-start(bf16[2,64,2048]{2,1,0:T(8,128)(2,1)} %pad_maximum_fusion.32), channel_id=1, source_target_pairs={{8,16},{10,18},{12,20},{14,22},{16,8},{18,10},{20,12},{22,14},{9,1... | collective-permute-start | bytes 1572872 | tf_op jit(solution)/shard_map/ppermute | solution.py:216
  173.9 96.2 %collective-permute-start.19 = (bf16[2048,256]{1,0:T(8,128)(2,1)S(1)}, bf16[2048,256]{1,0:T(8,128)(2,1)S(1)}, u32[]{:S(2)}, u32[]{:S(2)}) collective-permute-start(bf16[2048,256]{1,0:T(8,128)(2,1)S(1)} %copy-done.9), channel_id=1, source_target_pairs={{0,2},{2,0},{4,6},{6,4},{8,10},{10,8},{12,14},{14,12},{16,18},{18,... | collective-permute-start | bytes 3145736 | tf_op jit(solution)/shard_map/ppermute | solution.py:216
  185.2 85.0 %collective-permute-start.20 = (bf16[2048,256]{1,0:T(8,128)(2,1)S(1)}, bf16[2048,256]{1,0:T(8,128)(2,1)S(1)}, u32[]{:S(2)}, u32[]{:S(2)}) collective-permute-start(bf16[2048,256]{1,0:T(8,128)(2,1)S(1)} %copy-done.10), channel_id=1, source_target_pairs={{0,2},{2,0},{4,6},{6,4},{8,10},{10,8},{12,14},{14,12},{16,18},{18,... | collective-permute-start | bytes 3145736 | tf_op jit(solution)/shard_map/ppermute | solution.py:216
  212.2 58.0 %collective-permute-start.21 = (bf16[2048,256]{1,0:T(8,128)(2,1)S(1)}, bf16[2048,256]{1,0:T(8,128)(2,1)S(1)}, u32[]{:S(2)}, u32[]{:S(2)}) collective-permute-start(bf16[2048,256]{1,0:T(8,128)(2,1)S(1)} %copy-done.35), channel_id=1, source_target_pairs={{0,2},{2,0},{4,6},{6,4},{8,10},{10,8},{12,14},{14,12},{16,18},{18,... | collective-permute-start | bytes 3145736 | tf_op jit(solution)/shard_map/ppermute | solution.py:216
  330.4 59.1 %collective-permute-start.65 = (bf16[8,256,256]{2,1,0:T(8,128)(2,1)}, bf16[8,256,256]{2,1,0:T(8,128)(2,1)S(1)}, u32[]{:S(2)}, u32[]{:S(2)}) collective-permute-start(bf16[8,256,256]{2,1,0:T(8,128)(2,1)} %constant_dynamic-slice_fusion), channel_id=1, source_target_pairs={{0,1},{1,0},{2,3},{3,2},{4,5},{5,4},{6,7},{7,6},{8,9},{9,8},{10,11... | collective-permute-start | bytes 3145736 | tf_op jit(solution)/shard_map/ppermute | solution.py:220
  330.5 59.5 %collective-permute-start.53 = (bf16[8,256,256]{2,1,0:T(8,128)(2,1)S(1)}, bf16[8,256,256]{2,1,0:T(8,128)(2,1)S(1)}, u32[]{:S(2)}, u32[]{:S(2)}) collective-permute-start(bf16[8,256,256]{2,1,0:T(8,128)(2,1)S(1)} %constant_dynamic-slice_fusion.1), channel_id=1, source_target_pairs={{0,1},{1,0},{2,3},{3,2},{4,5},{5,4},{6,7},{7,6},{8,9},{9,8},{10,11... | collective-permute-start | bytes 3145736 | tf_op jit(solution)/shard_map/ppermute | solution.py:220
  359.7 32.6 %collective-permute-start.41 = (bf16[8,256,256]{2,1,0:T(8,128)(2,1)S(1)}, bf16[8,256,256]{2,1,0:T(8,128)(2,1)S(1)}, u32[]{:S(2)}, u32[]{:S(2)}) collective-permute-start(bf16[8,256,256]{2,1,0:T(8,128)(2,1)S(1)} %constant_dynamic-slice_fusion.2), channel_id=1, source_target_pairs={{0,1},{1,0},{2,3},{3,2},{4,5},{5,4},{6,7},{7,6},{8,9},{9,8},{10,11... | collective-permute-start | bytes 3145736 | tf_op jit(solution)/shard_map/ppermute | solution.py:220
  396.2 31.9 %collective-permute-start.42 = (bf16[4,256,256]{2,1,0:T(8,128)(2,1)}, bf16[4,256,256]{2,1,0:T(8,128)(2,1)}, u32[]{:S(2)}, u32[]{:S(2)}) collective-permute-start(bf16[4,256,256]{2,1,0:T(8,128)(2,1)} %fusion.40), channel_id=1, source_target_pairs={{0,2},{2,0},{4,6},{6,4},{8,10},{10,8},{12,14},{14,12},{16,18},{18,... | collective-permute-start | bytes 1572872 | tf_op jit(solution)/shard_map/ppermute | solution.py:216
  397.3 40.6 %collective-permute-start.23 = (bf16[4,256,256]{2,1,0:T(8,128)(2,1)S(1)}, bf16[4,256,256]{2,1,0:T(8,128)(2,1)}, u32[]{:S(2)}, u32[]{:S(2)}) collective-permute-start(bf16[4,256,256]{2,1,0:T(8,128)(2,1)S(1)} %fusion.39), channel_id=1, source_target_pairs={{0,2},{2,0},{4,6},{6,4},{8,10},{10,8},{12,14},{14,12},{16,18},{18,... | collective-permute-start | bytes 1572872 | tf_op jit(solution)/shard_map/ppermute | solution.py:216
  468.2 56.8 %collective-permute-start.67 = (bf16[256,512]{1,0:T(8,128)(2,1)S(1)}, bf16[256,512]{1,0:T(8,128)(2,1)S(1)}, u32[]{:S(2)}, u32[]{:S(2)}) collective-permute-start(bf16[256,512]{1,0:T(8,128)(2,1)S(1)} %recall.7), channel_id=1, source_target_pairs={{0,2},{2,0},{4,6},{6,4},{8,10},{10,8},{12,14},{14,12},{16,18},{18,... | collective-permute-start | bytes 786440 | tf_op jit(solution)/shard_map/ppermute | solution.py:216
  486.3 72.5 %collective-permute-start.25 = (bf16[256,512]{1,0:T(8,128)(2,1)S(1)}, bf16[256,512]{1,0:T(8,128)(2,1)S(1)}, u32[]{:S(2)}, u32[]{:S(2)}) collective-permute-start(bf16[256,512]{1,0:T(8,128)(2,1)S(1)} %recall.4), channel_id=1, source_target_pairs={{0,2},{2,0},{4,6},{6,4},{8,10},{10,8},{12,14},{14,12},{16,18},{18,... | collective-permute-start | bytes 786440 | tf_op jit(solution)/shard_map/ppermute | solution.py:216
  505.5 55.3 %collective-permute-start.43 = (bf16[256,512]{1,0:T(8,128)(2,1)S(1)}, bf16[256,512]{1,0:T(8,128)(2,1)S(1)}, u32[]{:S(2)}, u32[]{:S(2)}) collective-permute-start(bf16[256,512]{1,0:T(8,128)(2,1)S(1)} %recall.5), channel_id=1, source_target_pairs={{0,2},{2,0},{4,6},{6,4},{8,10},{10,8},{12,14},{14,12},{16,18},{18,... | collective-permute-start | bytes 786440 | tf_op jit(solution)/shard_map/ppermute | solution.py:216
  523.4 37.6 %collective-permute-start.55 = (bf16[256,512]{1,0:T(8,128)(2,1)S(1)}, bf16[256,512]{1,0:T(8,128)(2,1)S(1)}, u32[]{:S(2)}, u32[]{:S(2)}) collective-permute-start(bf16[256,512]{1,0:T(8,128)(2,1)S(1)} %recall.6), channel_id=1, source_target_pairs={{0,2},{2,0},{4,6},{6,4},{8,10},{10,8},{12,14},{14,12},{16,18},{18,... | collective-permute-start | bytes 786440 | tf_op jit(solution)/shard_map/ppermute | solution.py:216
  525.1 37.9 %collective-permute-start.68 = (bf16[512,512]{1,0:T(8,128)(2,1)S(1)}, bf16[512,512]{1,0:T(8,128)(2,1)S(1)}, u32[]{:S(2)}, u32[]{:S(2)}) collective-permute-start(bf16[512,512]{1,0:T(8,128)(2,1)S(1)} %pad_maximum_fusion.35), channel_id=1, source_target_pairs={{0,4},{2,6},{4,0},{6,2},{8,12},{10,14},{12,8},{14,10},{16,20},{18,... | collective-permute-start | bytes 1572872 | tf_op jit(solution)/shard_map/ppermute | solution.py:216
  558.9 41.5 %collective-permute-start.26 = (bf16[512,512]{1,0:T(8,128)(2,1)S(1)}, bf16[512,512]{1,0:T(8,128)(2,1)S(1)}, u32[]{:S(2)}, u32[]{:S(2)}) collective-permute-start(bf16[512,512]{1,0:T(8,128)(2,1)S(1)} %pad_maximum_fusion.29), channel_id=1, source_target_pairs={{0,4},{2,6},{4,0},{6,2},{8,12},{10,14},{12,8},{14,10},{16,20},{18,... | collective-permute-start | bytes 1572872 | tf_op jit(solution)/shard_map/ppermute | solution.py:216
  560.8 36.2 %collective-permute-start.44 = (bf16[512,512]{1,0:T(8,128)(2,1)S(1)}, bf16[512,512]{1,0:T(8,128)(2,1)S(1)}, u32[]{:S(2)}, u32[]{:S(2)}) collective-permute-start(bf16[512,512]{1,0:T(8,128)(2,1)S(1)} %pad_maximum_fusion.31), channel_id=1, source_target_pairs={{0,4},{2,6},{4,0},{6,2},{8,12},{10,14},{12,8},{14,10},{16,20},{18,... | collective-permute-start | bytes 1572872 | tf_op jit(solution)/shard_map/ppermute | solution.py:216
  561.1 32.3 %collective-permute-start.56 = (bf16[512,512]{1,0:T(8,128)(2,1)S(1)}, bf16[512,512]{1,0:T(8,128)(2,1)S(1)}, u32[]{:S(2)}, u32[]{:S(2)}) collective-permute-start(bf16[512,512]{1,0:T(8,128)(2,1)S(1)} %pad_maximum_fusion.33), channel_id=1, source_target_pairs={{0,4},{2,6},{4,0},{6,2},{8,12},{10,14},{12,8},{14,10},{16,20},{18,... | collective-permute-start | bytes 1572872 | tf_op jit(solution)/shard_map/ppermute | solution.py:216
  564.3 39.3 %collective-permute-start.69 = (bf16[512,256]{1,0:T(8,128)(2,1)S(1)}, bf16[512,256]{1,0:T(8,128)(2,1)S(1)}, u32[]{:S(2)}, u32[]{:S(2)}) collective-permute-start(bf16[512,256]{1,0:T(8,128)(2,1)S(1)} %get-tuple-element.50), channel_id=1, source_target_pairs={{0,8},{2,10},{4,12},{6,14},{8,16},{10,18},{12,20},{14,22},{16,24},... | collective-permute-start | bytes 786440 | tf_op jit(solution)/shard_map/ppermute | solution.py:216
  564.4 39.4 %collective-permute-start.71 = (bf16[512,256]{1,0:T(8,128)(2,1)S(1)}, bf16[512,256]{1,0:T(8,128)(2,1)S(1)}, u32[]{:S(2)}, u32[]{:S(2)}) collective-permute-start(bf16[512,256]{1,0:T(8,128)(2,1)S(1)} %get-tuple-element.51), channel_id=1, source_target_pairs={{0,24},{2,26},{4,28},{6,30},{8,0},{10,2},{12,4},{14,6},{16,8},{18,... | collective-permute-start | bytes 786440 | tf_op jit(solution)/shard_map/ppermute | solution.py:216
  600.4 33.8 %collective-permute-start.59 = (bf16[512,256]{1,0:T(8,128)(2,1)S(1)}, bf16[512,256]{1,0:T(8,128)(2,1)S(1)}, u32[]{:S(2)}, u32[]{:S(2)}) collective-permute-start(bf16[512,256]{1,0:T(8,128)(2,1)S(1)} %get-tuple-element.48), channel_id=1, source_target_pairs={{0,24},{2,26},{4,28},{6,30},{8,0},{10,2},{12,4},{14,6},{16,8},{18,... | collective-permute-start | bytes 786440 | tf_op jit(solution)/shard_map/ppermute | solution.py:216
  603.6 42.3 %collective-permute-start.58 = (bf16[512,256]{1,0:T(8,128)(2,1)S(1)}, bf16[512,256]{1,0:T(8,128)(2,1)S(1)}, u32[]{:S(2)}, u32[]{:S(2)}) collective-permute-start(bf16[512,256]{1,0:T(8,128)(2,1)S(1)} %get-tuple-element.49), channel_id=1, source_target_pairs={{0,16},{2,18},{4,20},{6,22},{8,24},{10,26},{12,28},{14,30},{16,0},... | collective-permute-start | bytes 786440 | tf_op jit(solution)/shard_map/ppermute | solution.py:216
  603.7 42.4 %collective-permute-start.33 = (bf16[512,256]{1,0:T(8,128)(2,1)S(1)}, bf16[512,256]{1,0:T(8,128)(2,1)S(1)}, u32[]{:S(2)}, u32[]{:S(2)}) collective-permute-start(bf16[512,256]{1,0:T(8,128)(2,1)S(1)} %get-tuple-element.41), channel_id=1, source_target_pairs={{0,8},{2,10},{4,12},{6,14},{8,16},{10,18},{12,20},{14,22},{16,24},... | collective-permute-start | bytes 786440 | tf_op jit(solution)/shard_map/ppermute | solution.py:216
  615.2 41.4 %collective-permute-start.35 = (bf16[512,256]{1,0:T(8,128)(2,1)S(1)}, bf16[512,256]{1,0:T(8,128)(2,1)S(1)}, u32[]{:S(2)}, u32[]{:S(2)}) collective-permute-start(bf16[512,256]{1,0:T(8,128)(2,1)S(1)} %get-tuple-element.42), channel_id=1, source_target_pairs={{0,24},{2,26},{4,28},{6,30},{8,0},{10,2},{12,4},{14,6},{16,8},{18,... | collective-permute-start | bytes 786440 | tf_op jit(solution)/shard_map/ppermute | solution.py:216
  618.7 44.1 %collective-permute-start.34 = (bf16[512,256]{1,0:T(8,128)(2,1)S(1)}, bf16[512,256]{1,0:T(8,128)(2,1)S(1)}, u32[]{:S(2)}, u32[]{:S(2)}) collective-permute-start(bf16[512,256]{1,0:T(8,128)(2,1)S(1)} %get-tuple-element.43), channel_id=1, source_target_pairs={{0,16},{2,18},{4,20},{6,22},{8,24},{10,26},{12,28},{14,30},{16,0},... | collective-permute-start | bytes 786440 | tf_op jit(solution)/shard_map/ppermute | solution.py:216
  (78 other events, 976.4 us)

commit v2 on v1

--- a/solution.py
+++ b/solution.py
@@ -196,18 +196,6 @@
     return here ^ 2
 
 
-def z_mate(here):
-    return here ^ 4
-
-
-def z_middle(here):
-    return {1: here + 4, 2: here - 4}.get(here // 4)
-
-
-def z_outward(here):
-    return {1: here - 4, 2: here + 4}.get(here // 4)
-
-
 def z_shift(amount):
     return lambda here: (here + 4 * amount) % (4 * PLANES)
 
@@ -220,128 +208,174 @@
     return lax.ppermute(block, "narrow", [(0, 1), (1, 0)])
 
 
-def project_kernel(now_ref, before_ref, small_ref, raise_ref, blend_ref, *refs):
-    weights, out_ref, total_ref = refs[:8], refs[8], refs[9]
-    step = pl.program_id(0)
-    rank = raise_ref.shape[1]
-    tile = 256
-    for start in range(0, now_ref.shape[0], tile):
-        rows = slice(start, start + tile)
-        now = now_ref[rows, :].astype(F32)
-        shift = before_ref[rows, :].astype(F32) - now
-        for kind in range(4):
-            low = jnp.dot(
-                small_ref[rows, kind * rank : (kind + 1) * rank],
-                raise_ref[kind],
-                preferred_element_type=F32,
-            )
-            mixed = (now + shift * (blend_ref[kind : kind + 1, :] + low)).astype(BF16)
-            for side in range(2):
-                term = jnp.dot(mixed, weights[2 * kind + side][...], preferred_element_type=F32)
-                slot = 2 * kind + side
-
-                @pl.when(step == 0)
-                def _():
-                    total_ref[slot, rows, :] = term
-
-                @pl.when(step > 0)
-                def _():
-                    total_ref[slot, rows, :] += term
-
-    @pl.when(step == pl.num_programs(0) - 1)
+def project_kernel(order_ref, *refs):
+    nows, befores, refs = refs[:8], refs[8:16], refs[16:]
+    small_ref, raise_ref, blend_ref, own_ref, mate_ref, *refs = refs
+    kept_refs, given_ref, now_ref, shift_ref, mix_ref = refs[:2], *refs[2:]
+    rows = nows[0].shape[0]
+    half, features = given_ref.shape[2], now_ref.shape[1]
+    first = order_ref[8] == 0
+
+    @pl.when(pl.program_id(0) == 0)
     def _():
-        out_ref[...] = total_ref[...].astype(BF16)
-
-
-def project(now, before, small, raising, blending, weights):
-    rows, features = now.shape
-    columns = weights[0].shape[1]
-    depth = 512
+        for block in range(8):
+            here = pl.ds(pl.multiple_of(order_ref[block] * rows, rows), rows)
+            now = nows[block][...]
+            now_ref[here, :] = now
+            shift_ref[here, :] = befores[block][...].astype(F32) - now.astype(F32)
+
+    for start in range(0, features, 512):
+        here = slice(start, start + 512)
+        low = jnp.dot(small_ref[...], raise_ref[0, :, here], preferred_element_type=F32)
+        mixed = now_ref[:, here].astype(F32) + shift_ref[:, here] * (blend_ref[0, :, here] + low)
+        mix_ref[:, here] = mixed.astype(BF16)
+    for side, weight_ref in enumerate((own_ref, mate_ref)):
+        total = jnp.dot(mix_ref[...], weight_ref[0], preferred_element_type=F32).astype(BF16)
+        kept_refs[side][0] = jnp.where(first, total[:half], total[half:])
+        given_ref[side, 0] = jnp.where(first, total[half:], total[:half])
+
+
+def project(order, nows, befores, small, raising, blending, own, mate):
+    columns, features = own.shape[2], own.shape[1]
+    rows = nows[0][0].shape[-2]
+    total = 8 * rows
+
+    def spec(source):
+        array, place, column = source
+        if place is None:
+            return pl.BlockSpec((rows, features), lambda c, order: (0, column))
+        return pl.BlockSpec((None, rows, features), lambda c, order: (place, 0, column))
+
+    kind = lambda shape: pl.BlockSpec((1,) + shape[1:], lambda c, order: (c, 0, 0))
+    sources = list(nows) + list(befores)
     return pl.pallas_call(
         project_kernel,
-        grid=(features // depth,),
-        in_specs=[
-            pl.BlockSpec((rows, depth), lambda k: (0, k)),
-            pl.BlockSpec((rows, depth), lambda k: (0, k)),
-            pl.BlockSpec(small.shape, lambda k: (0, 0)),
-            pl.BlockSpec((4, raising.shape[1], depth), lambda k: (0, 0, k)),
-            pl.BlockSpec((4, depth), lambda k: (0, k)),
-        ]
-        + [pl.BlockSpec((depth, columns), lambda k: (k, 0))] * 8,
-        out_specs=pl.BlockSpec((8, rows, columns), lambda k: (0, 0, 0)),
-        out_shape=jax.ShapeDtypeStruct((8, rows, columns), BF16),
-        scratch_shapes=[pltpu.VMEM((8, rows, columns), F32)],
+        grid_spec=pltpu.PrefetchScalarGridSpec(
+            num_scalar_prefetch=1,
+            grid=(4,),
+            in_specs=[spec(source) for source in sources]
+            + [pl.BlockSpec(small.shape, lambda c, order: (0, 0))]
+            + [kind(raising.shape), kind(blending.shape), kind(own.shape), kind(mate.shape)],
+            out_specs=[pl.BlockSpec((1, total // 2, columns), lambda c, order: (c, 0, 0))] * 2
+            + [pl.BlockSpec((2, 1, total // 2, columns), lambda c, order: (0, c, 0, 0))],
+            scratch_shapes=[
+                pltpu.VMEM((total, features), BF16),
+                pltpu.VMEM((total, features), F32),
+                pltpu.VMEM((total, features), BF16),
+            ],
+        ),
+        out_shape=[jax.ShapeDtypeStruct((4, total // 2, columns), BF16)] * 2
+        + [jax.ShapeDtypeStruct((2, 4, total // 2, columns), BF16)],
         compiler_params=pltpu.CompilerParams(vmem_limit_bytes=48 * 2**20),
         cost_estimate=pl.CostEstimate(
-            flops=2 * rows * features * columns * 8 + 8 * rows * features * 32,
-            bytes_accessed=16 * features * columns + 4 * rows * features + 16 * rows * columns,
+            flops=2 * total * features * columns * 12,
+            bytes_accessed=16 * features * columns + 4 * total * features,
             transcendentals=0,
         ),
         name="project",
-    )(now, before, small, raising, blending, *weights)
+    )(order, *[source[0] for source in sources], small, raising, blending, own, mate)
+
+
+def weave_kernel(x_ref, kept_ref, given_ref, mate_ref, out_ref):
+    chats = mate_ref.shape[1] // 4
+    own = kept_ref[0].astype(F32) + given_ref[0, 0].astype(F32)
+    mate = mate_ref[0].astype(F32)
+    first = x_ref[0] == 0
+    for block in range(4):
+        rows = slice(block * chats, (block + 1) * chats)
+        low = jnp.where(first, own[rows], mate[rows])
+        high = jnp.where(first, mate[rows], own[rows])
+        lanes = slice(2 * block * chats, 2 * (block + 1) * chats)
+        out_ref[0, :, lanes] = jnp.concatenate([low, high], 0).T
+
+
+def weave(x, kept, given, mate):
+    _, half, columns = kept.shape
+    side = pl.BlockSpec((1, half, columns), lambda c, x: (c, 0, 0))
+    return pl.pallas_call(
+        weave_kernel,
+        grid_spec=pltpu.PrefetchScalarGridSpec(
+            num_scalar_prefetch=1,
+            grid=(4,),
+            in_specs=[side, pl.BlockSpec((1, 1, half, columns), lambda c, x: (0, c, 0, 0)), side],
+            out_specs=pl.BlockSpec((1, columns, 2 * half), lambda c, x: (c, 0, 0)),
+        ),
+        out_shape=jax.ShapeDtypeStruct((4, columns, 2 * half), F32),
+        cost_estimate=pl.CostEstimate(
+            flops=8 * half * columns, bytes_accessed=64 * half * columns, transcendentals=0
+        ),
+        name="weave",
+    )(x, kept, given, mate)
 
 
 def recall_kernel(steps, *refs):
-    state_ref, line_refs, refs = refs[0], refs[1 : 2 + steps], refs[2 + steps :]
-    decay_ref, bonus_ref, gain_ref, offset_ref, out_ref, reach_ref, total_ref = refs
+    last = steps[-1]
+    state_ref, line_refs, refs = refs[0], refs[1 : 2 + last], refs[2 + last :]
+    decay_ref, bonus_ref, gain_ref, offset_ref = refs[:4]
+    out_refs, (reach_ref, total_ref) = refs[4:-2], refs[-2:]
     part = pl.program_id(1)
     depth = state_ref.shape[1]
     span = state_ref.shape[2]
     width = state_ref.shape[3]
-    now_ref = line_refs[steps]
 
     @pl.when(part == 0)
     def _():
-        reach = now_ref[0]
-        for step in range(steps):
-            reach = reach * decay_ref[step]
-        reach_ref[...] = reach
+        for slot, step in enumerate(steps):
+            reach = line_refs[step][0]
+            for earlier in range(step):
+                reach = reach * decay_ref[earlier]
+            reach_ref[slot] = reach
         total_ref[...] = jnp.zeros_like(total_ref)
 
     for start in range(0, width, 128):
         lanes = slice(start, start + 128)
-        total = total_ref[:, lanes]
-        reach = reach_ref[pl.ds(pl.multiple_of(part * depth, depth), depth), lanes]
+        here = pl.ds(pl.multiple_of(part * depth, depth), depth)
+        totals = [total_ref[slot, :, lanes] for slot in range(len(steps))]
+        reaches = [reach_ref[slot, here, lanes] for slot in range(len(steps))]
         for row in range(depth):
-            total = total + reach[row : row + 1, :] * state_ref[0, row, :, lanes]
-        total_ref[:, lanes] = total
+            memory = state_ref[0, row, :, lanes]
+            for slot in range(len(steps)):
+                totals[slot] = totals[slot] + reaches[slot][row : row + 1, :] * memory
+        for slot in range(len(steps)):
+            total_ref[slot, :, lanes] = totals[slot]
 
     @pl.when(part == pl.num_programs(1) - 1)
     def _():
-        acceptor = now_ref[0]
-        readout = total_ref[...]
-        weight = jnp.sum(acceptor * bonus_ref[...] * now_ref[1], 0, keepdims=True)
-        readout = readout + weight * now_ref[2]
-        for step in reversed(range(steps)):
-            weight = jnp.sum(acceptor * line_refs[step][1], 0, keepdims=True)
-            readout = readout + weight * line_refs[step][2]
-            if step:
-                acceptor = acceptor * decay_ref[step]
-        center = jnp.sum(readout, 0, keepdims=True) * (1.0 / span)
-        offset = readout - center
-        spread = jnp.sum(offset * offset, 0, keepdims=True) * (1.0 / span)
-        scaled = offset * lax.rsqrt(spread + 0.00064)
-        gate = now_ref[3]
-        grouped = scaled * gain_ref[...] + offset_ref[...]
-        out_ref[...] = (grouped * (gate / (1.0 + jnp.exp(-gate)))).astype(BF16)
-
-
-def recall(state, lines, decay, bonus, gain, offset):
+        for slot, step in enumerate(steps):
+            now_ref = line_refs[step]
+            acceptor = now_ref[0]
+            readout = total_ref[slot]
+            weight = jnp.sum(acceptor * bonus_ref[...] * now_ref[1], 0, keepdims=True)
+            readout = readout + weight * now_ref[2]
+            for earlier in reversed(range(step)):
+                weight = jnp.sum(acceptor * line_refs[earlier][1], 0, keepdims=True)
+                readout = readout + weight * line_refs[earlier][2]
+                if earlier:
+                    acceptor = acceptor * decay_ref[earlier]
+            center = jnp.sum(readout, 0, keepdims=True) * (1.0 / span)
+            offset = readout - center
+            spread = jnp.sum(offset * offset, 0, keepdims=True) * (1.0 / span)
+            scaled = offset * lax.rsqrt(spread + 0.00064)
+            gate = now_ref[3]
+            grouped = scaled * gain_ref[...] + offset_ref[...]
+            out_refs[slot][...] = (grouped * (gate / (1.0 + jnp.exp(-gate)))).astype(BF16)
+
+
+def recall(state, steps, lines, decay, bonus, gain, offset):
     heads, span, _, width = state.shape
-    steps = len(lines) - 1
-    depth = 16
+    depth = span // 2
     column = pl.BlockSpec((span, 1), lambda h, p: (h, 0))
     return pl.pallas_call(
         functools.partial(recall_kernel, steps),
         grid=(heads, span // depth),
         in_specs=[pl.BlockSpec((1, depth, span, width), lambda h, p: (h, p, 0, 0))]
-        + [pl.BlockSpec((4, span, width), lambda h, p: (0, h, 0))] * (steps + 1)
-        + [pl.BlockSpec((4, span, width), lambda h, p: (0, h, 0))]
+        + [pl.BlockSpec((4, span, width), lambda h, p: (0, h, 0))] * len(lines)
+        + [pl.BlockSpec((decay.shape[0], span, width), lambda h, p: (0, h, 0))]
         + [column] * 3,
-        out_specs=pl.BlockSpec((span, width), lambda h, p: (h, 0)),
-        out_shape=jax.ShapeDtypeStruct((heads * span, width), BF16),
-        scratch_shapes=[pltpu.VMEM((span, width), F32), pltpu.VMEM((span, width), F32)],
-        compiler_params=pltpu.CompilerParams(vmem_limit_bytes=32 * 2**20),
+        out_specs=[pl.BlockSpec((span, width), lambda h, p: (h, 0))] * len(steps),
+        out_shape=[jax.ShapeDtypeStruct((heads * span, width), BF16)] * len(steps),
+        scratch_shapes=[pltpu.VMEM((len(steps), span, width), F32)] * 2,
+        compiler_params=pltpu.CompilerParams(vmem_limit_bytes=60 * 2**20),
         cost_estimate=pl.CostEstimate(
             flops=2 * heads * span * span * width,
             bytes_accessed=4 * heads * span * span * width,
@@ -382,7 +416,7 @@
 
 def renew(state, lines, decay):
     heads, span, _, width = state.shape
-    depth = 16
+    depth = span // 2
     steps = len(lines)
     block = pl.BlockSpec((1, depth, span, width), lambda h, p: (h, p, 0, 0))
     return pl.pallas_call(
@@ -392,7 +426,7 @@
         out_specs=block,
         out_shape=jax.ShapeDtypeStruct(state.shape, F32),
         scratch_shapes=[pltpu.VMEM((span, width), F32), pltpu.VMEM((steps, span, width), F32)],
-        compiler_params=pltpu.CompilerParams(vmem_limit_bytes=32 * 2**20),
+        compiler_params=pltpu.CompilerParams(vmem_limit_bytes=40 * 2**20),
         cost_estimate=pl.CostEstimate(
             flops=9 * heads * span * span * width,
             bytes_accessed=8 * heads * span * span * width,
@@ -436,20 +470,29 @@
         first = bit == 0
         return [jnp.where(first, mine, theirs), jnp.where(first, theirs, mine)]
 
-    def gather(block):
-        near = jnp.stack(in_order(z % 2, block, send(block, z_mate)))
-        across = send(near, z_middle)
-        far = jnp.where((z == 1) | (z == 2), across, send(across, z_outward))
-        near = jnp.stack(in_order(y, near, send(near, y_mate)), 1)
-        far = jnp.stack(in_order(y, far, send(far, y_mate)), 1)
-        both = jnp.stack(in_order(z // 2, near, far))
-        return both.reshape((8 * block.shape[0],) + block.shape[1:])
-
-    all_weights = []
-    for weight in weights:
-        all_weights += [weight, send(weight, x_mate)]
-
-    prior_all = gather(prior_symbol_memory)
+    def after(value, *earlier):
+        return lax.optimization_barrier((value, *earlier))[0]
+
+    order = jnp.stack(
+        [
+            2 * ((z + PLANES - shift) % PLANES) + row
+            for row in (y, 1 - y)
+            for shift in range(PLANES)
+        ]
+        + [narrow]
+    ).astype(jnp.int32)
+
+    own_weights = jnp.stack(weights)
+    mate_weights = send(own_weights, x_mate)
+
+    def send_z(block, *earlier):
+        return [
+            send(after(block, *[one[shift - 1] for one in earlier]), z_shift(shift))
+            for shift in range(1, PLANES)
+        ]
+
+    prior_z = send_z(prior_symbol_memory)
+
     floats = sublevel_symbol_entries.astype(F32).transpose(1, 0, 2)
     sums = jnp.stack([jnp.sum(floats, -1), jnp.sum(floats * floats, -1)])
     sums = sums + swap(sums)
@@ -459,8 +502,6 @@
         (floats - center) * lax.rsqrt(spread + 1e-05) * entry_scaling_multiplier
         + entry_scaling_offset
     ).astype(BF16)
-    normed_all = [gather(normed[step]) for step in range(moves)]
-
     previous = jnp.concatenate([prior_symbol_memory[None], normed[:-1]], 0)
     normed_float = normed.astype(F32)
     shifted = previous.astype(F32) - normed_float
@@ -480,77 +521,167 @@
         "msd,dr->msr", decay_mix, fading_lowering_coefficients, preferred_element_type=F32
     )
     decay_hidden = jnp.tanh(partial_decay + swap(partial_decay)).astype(BF16)
-    small = jnp.concatenate([hidden[..., rank:], decay_hidden], -1).transpose(1, 0, 2)
-    small_width = small.shape[-1]
-    small_all = gather(small.reshape(chats, moves * small_width))
-    small_all = small_all.reshape(-1, moves, small_width)
+
+    small = jnp.concatenate(
+        [hidden[step, :, rank:] for step in range(moves)]
+        + [decay_hidden[step] for step in range(moves)],
+        1,
+    )
+    def in_plane(passed):
+        passed = jnp.stack((passed[:1] + passed[:0:-1]) * 2)
+        return lax.dynamic_slice_in_dim(passed, (PLANES - z) % PLANES, PLANES, 0)
+
+    first = jnp.concatenate([normed[0], normed[1]], 1)
+    second = jnp.concatenate([normed[2], normed[3]], 1)
+    normed_y = send(jnp.stack([first, second]), y_mate)
+    small_z = send_z(small, prior_z)
+    prior_y = send(jnp.stack([prior_symbol_memory] + prior_z), y_mate)
+    first_z = send_z(first, small_z)
+    small_plane = in_plane([small] + small_z)
+    small_y = send(small_plane, y_mate)
+    first_near_y = send(after(first_z[0], normed_y), y_mate)
+    second_z = send_z(second, first_z, (prior_y, small_y, first_near_y))
+    first_far_y = send(jnp.stack(first_z[1:]), y_mate)
+    second_near_y = send(after(second_z[0], first_near_y), y_mate)
+    small_all = jnp.stack(in_order(y, small_plane, small_y), 1).reshape(-1, small.shape[1])
+
+    prior_sources = [(prior_symbol_memory, None, 0)] + [(one, None, 0) for one in prior_z]
+    prior_sources += [(prior_y, place, 0) for place in range(PLANES)]
+
+    def first_sources(step):
+        found = [(first, None, step)] + [(one, None, step) for one in first_z]
+        found += [(normed_y, 0, step), (first_near_y, None, step)]
+        return found + [(first_far_y, place, step) for place in range(2)]
 
     half = small_all.shape[0] // 2
-    decay_mine = lax.dynamic_slice_in_dim(small_all[..., 4 * rank :], narrow * half, half, 0)
-    decay_theirs = send(decay_mine, x_mate)
-
-    def weave(mine, theirs):
-        shape = mine.shape[:-2] + (-1, chats, mine.shape[-1])
-        both = jnp.stack(in_order(x, mine.reshape(shape), theirs.reshape(shape)), -3)
-        return both.reshape(mine.shape[:-2] + (narrow_rows, mine.shape[-1]))
-
-    decay_rows = weave(decay_mine.transpose(1, 0, 2), decay_theirs.transpose(1, 0, 2))
+    decay_width = decay_hidden.shape[-1]
+    decay_own = lax.dynamic_slice_in_dim(small_all[:, moves * 4 * rank :], narrow * half, half, 0)
+    decay_rows = jnp.stack(
+        in_order(x, decay_own.reshape(-1, chats, moves * decay_width),
+                 send(decay_own, x_mate).reshape(-1, chats, moves * decay_width)),
+        1,
+    ).reshape(narrow_rows, moves, decay_width)
     decay_log = learned_fading[:, None] + jnp.einsum(
-        "rd,msr->mds", fading_raising_coefficients, decay_rows, preferred_element_type=F32
+        "rd,smr->mds", fading_raising_coefficients, decay_rows, preferred_element_type=F32
     )
     decay = jnp.exp(-jnp.exp(decay_log))
 
-    plane = emission_projection.shape[0] // PLANES
-    piece = plane // 2
-    emission = []
-    for shift in range(PLANES):
-        start = ((z + PLANES - shift) % PLANES) * plane
-        if shift == 0:
-            emission.append(lax.dynamic_slice_in_dim(emission_projection, start, plane, 0))
-        else:
-            own = lax.dynamic_slice_in_dim(
-                emission_projection, start + narrow * piece, piece, 0
-            )
-            own = send(own, z_shift(-shift))
-            emission.append(jnp.concatenate(in_order(narrow, own, swap(own)), 0))
-    emission = jnp.concatenate(emission, 1)
-    emission = emission.reshape(2, 2, local_width, PLANES * local_width)
-    emission = jnp.stack(in_order(y, emission[0], emission[1]))
-    emission = jnp.stack(in_order(x, emission[:, 0], emission[:, 1]), 1)
-    emission = emission.reshape(plane, PLANES * local_width)
-
+    blocks = emission_projection.reshape(4 * PLANES, local_width, local_width)
+
+    def plane_rows(shift, mates):
+        start = ((z + PLANES - shift) % PLANES) * 4
+        rows = [
+            lax.dynamic_index_in_dim(blocks, start + (wide % 4 ^ mate), 0, False)
+            for mate in mates
+        ]
+        return jnp.concatenate(rows, 0)
+
+    emission_own = plane_rows(0, range(4))
     state = dialogue_group_memory.reshape(groups, CHANNEL_SPAN, CHANNEL_SPAN, narrow_rows)
     bonus = immediate_item_premium[:, None]
     gain = group_scaling_multiplier[:, None]
     offset = group_scaling_offset[:, None]
-    lines, results = [], []
-    for step in range(moves):
-        before = normed_all[step - 1] if step else prior_all
-        partial = project(
-            normed_all[step],
-            before,
-            small_all[:, step, : 4 * rank],
-            blending_raising_coefficients[1:],
-            learned_blending[2:],
-            all_weights,
-        )
-        kept = lax.dynamic_slice_in_dim(partial, narrow * half, half, 1)
-        given = lax.dynamic_slice_in_dim(partial, (1 - narrow) * half, half, 1)
-        whole = kept.astype(F32) + swap(given).astype(F32)
-        whole = whole.reshape(4, 2, half, local_width)
-        theirs = send(whole[:, 1].astype(BF16), x_mate)
-        line = weave(whole[:, 0], theirs.astype(F32)).transpose(0, 2, 1)
-        lines.append(line)
-        gated = recall(state, lines, decay, bonus, gain, offset)
+    raising = jnp.stack(
+        [
+            jnp.pad(blending_raising_coefficients[kind + 1], ((kind * rank, (3 - kind) * rank), (0, 0)))
+            for kind in range(4)
+        ]
+    )
+    blending = learned_blending[2:, None]
+    x_here = x.astype(jnp.int32)[None]
+    lines = []
+
+    def make(step, nows, befores, *earlier):
+        return project(
+            after(order, *earlier),
+            nows,
+            befores,
+            small_all[:, step * 4 * rank : (step + 1) * 4 * rank],
+            raising,
+            blending,
+            own_weights,
+            mate_weights,
+        )
+
+    def pass_on(made, *earlier):
+        _, mate_kept, given = made
+        theirs = after(mate_kept, *earlier).astype(F32) + given[1].astype(F32)
+        theirs = theirs.astype(BF16)
+        return theirs, send(theirs, x_mate)
+
+    def line_up(made, arrived, *earlier):
+        lines.append(weave(after(x_here, *earlier), made[0], made[2], arrived))
+        return lines[-1]
+
+    def read(step, *earlier):
+        line = lines[: step + 1]
+        gated = recall(state, (step,), line, decay, after(bonus, *earlier), gain, offset)[0]
         gated = jnp.concatenate([gated, send(gated, x_mate)], 0)
-        gated = jnp.concatenate([gated, send(gated, y_mate)], 0)
-        product = jnp.einsum("cs,ce->se", gated, emission, preferred_element_type=F32)
-        total = product[:, :local_width]
-        for shift in range(1, PLANES):
-            columns = product[:, shift * local_width : (shift + 1) * local_width]
-            total = total + send(columns.astype(BF16), z_shift(shift)).astype(F32)
-        results.append(total.astype(BF16))
-    final = renew(state, lines, decay)
+        return gated, jnp.concatenate([gated, send(gated, y_mate)], 0)
+
+    def emit(gated, *earlier):
+        gated = after(gated, *earlier)
+        own = jnp.einsum("cs,ce->se", gated, emission_own, preferred_element_type=F32)
+        far = jnp.einsum("cs,ce->se", gated, emission_far, preferred_element_type=F32)
+        return own, far.astype(BF16)
+
+    def gather_up(product, *earlier):
+        total, far = product
+        arrived = [
+            send(far[:, shift * local_width : (shift + 1) * local_width], z_shift(shift + 1))
+            for shift in range(PLANES - 1)
+        ]
+        if earlier:
+            arrived = after(tuple(arrived), *earlier)
+        for one in arrived:
+            total = total + one.astype(F32)
+        return total.astype(BF16)
+
+    def halves(made):
+        return made[0], made[1], swap(made[2])
+
+    made = [halves(make(0, first_sources(0), prior_sources))]
+    second_far_y = send(after(jnp.stack(second_z[1:]), made[0][0]), y_mate)
+
+    def second_sources(step):
+        found = [(second, None, step)] + [(one, None, step) for one in second_z]
+        found += [(normed_y, 1, step), (second_near_y, None, step)]
+        return found + [(second_far_y, place, step) for place in range(2)]
+
+    made.append(halves(make(1, first_sources(1), first_sources(0), second_near_y, made[0][0])))
+    passed = [pass_on(made[0], made[1][0])]
+    emission_z = [
+        send(
+            after(plane_rows(shift, (2 * narrow, 2 * narrow + 1)), second_z[shift - 1], passed[0][0]),
+            z_shift(-shift),
+        )
+        for shift in range(1, PLANES)
+    ]
+    passed.append(pass_on(made[1]))
+    line_up(made[0], passed[0][1])
+    gated = [read(0)]
+    made.append(halves(make(2, second_sources(0), first_sources(1), gated[0][0])))
+    line_up(made[1], passed[1][1], made[2][0])
+    passed.append(pass_on(made[2], lines[1]))
+    made.append(
+        halves(make(3, second_sources(1), second_sources(0), lines[1], *emission_z))
+    )
+    emission_near = jnp.concatenate(emission_z, 1)
+    emission_far = jnp.concatenate(in_order(narrow, emission_near, swap(emission_near)), 0)
+    products = [emit(gated[0][1], made[3][0])]
+    results = [gather_up(products[0])]
+    passed.append(pass_on(made[3], products[0][1]))
+    gated.append(read(1, products[0][1], passed[2][0], passed[3][0]))
+    line_up(made[2], passed[2][1], gated[1][0])
+    gated.append(read(2))
+    line_up(made[3], passed[3][1], gated[2][0])
+    products.append(emit(gated[1][1], lines[3]))
+    gated.append(read(3, products[1][1], results[0]))
+    products.append(emit(gated[2][1], gated[3][0]))
+    products.append(emit(gated[3][1], products[2][1]))
+    final = renew(after(state, products[3][1]), lines, decay)
+    results += [gather_up(products[1]), gather_up(products[2])]
+    results.append(gather_up(products[3], final))
     return (
         jnp.stack(results, 1),
         final.reshape(groups * CHANNEL_SPAN * CHANNEL_SPAN, narrow_rows),

time: 682 us -> 405 us (0.59)
  waiting for transfers between devices: 251 us -> 97.4 us
  Pallas kernels: 212 us -> 154 us
  local copies, waits for them, and re-layouts: 60.8 us -> 26.9 us
  starting transfers between devices: 94.9 us -> 78 us
  other arithmetic: 44.4 us -> 32.1 us
    ppermute x62 -> x48, waiting for transfers between devices: 251 us -> 96.4 us  [send(): return lax.ppermute(block, 'wide', pairs(move))]
    pallas_call x4 -> x8, Pallas kernels: 111 us -> 63 us  [the longest x4 46.5 us: project(): pl.pallas_call(project_kernel, grid_spec=pltpu.PrefetchScalarGridSpec(num...]
    another operation x11 -> x5, local copies, waits for them, and re-layouts: 16.6 us -> 0.32 us  [the longest x2 0.17 us: boxed_device(): jnp.stack([jnp.pad(blending_raising_coefficients[kind + 1], ((kind * rank...]
    ppermute x62 -> x48, starting transfers between devices: 92.4 us -> 76.5 us  [send(): return lax.ppermute(block, 'wide', pairs(move))]
    reshape x6 -> x1, local copies, waits for them, and re-layouts: 12.8 us -> 1.1 us  [boxed_device(): decay_rows = jnp.stack(in_order(x, decay_own.reshape(-1, chats, moves * d...]
    dynamic_slice x7 -> x2, local copies, waits for them, and re-layouts: 9.51 us -> 0.05 us  [the longest x1 0.04 us: in_plane(): return lax.dynamic_slice_in_dim(passed, (PLANES - z) % PLANES, PLANES, 0)]
    another operation x33 -> x10, other arithmetic: 16.4 us -> 9.4 us  [the longest x1 3.82 us: boxed_device(): own_weights = jnp.stack(weights)]
  transfers between devices with their start and end apart: 72 -> 56, of which waited for: 30 -> 17; matrix products, arithmetic and copies ran while one was open for 13% -> 15% of each run, Pallas kernels for 21% -> 33%
where the time goes in v2:
time: 405 us; the launch traced here: 404 us
  Pallas kernels  154 us (38%)
  waiting for transfers between devices  97.4 us (24%)
  starting transfers between devices  78 us (19%)
  other arithmetic  32.1 us (8%)
  local copies, waits for them, and re-layouts  26.9 us (7%)
  matrix products  13.9 us (3%)
    ppermute x48, waiting for transfers between devices, send(): return lax.ppermute(block, 'wide', pairs(move))  96.4 us
    ppermute x48, starting transfers between devices, send(): return lax.ppermute(block, 'wide', pairs(move))  76.5 us
    pallas_call x4, Pallas kernels, recall(): pl.pallas_call(functools.partial(recall_kernel, steps), grid=(heads, span...  63.5 us
    pallas_call x4, Pallas kernels, project(): pl.pallas_call(project_kernel, grid_spec=pltpu.PrefetchScalarGridSpec(num...  46.5 us
    pallas_call x1, Pallas kernels, renew(): pl.pallas_call(renew_kernel, grid=(heads, span // depth), in_specs=[block...  27.1 us
    pallas_call x4, Pallas kernels, weave(): pl.pallas_call(weave_kernel, grid_spec=pltpu.PrefetchScalarGridSpec(num_s...  16.5 us
    unnamed x136, local copies, waits for them, and re-layouts  13.5 us
  transfers between devices with their start and end apart: 56, of which 17 were waited for; matrix products, arithmetic and copies ran while one was open for 15% of the time, Pallas kernels for 33%

profile of v2, /device:TPU:0, one launch (start us, length us, event | category | flops | bytes accessed | tf_op | source)
XLA Modules:
  0.0 403.6 jit_solution(1317892669495651045)
XLA Ops:
  0.6 5.1 %collective-permute-start.9 = (bf16[64,2048]{1,0:T(8,128)(2,1)}, bf16[64,2048]{1,0:T(8,128)(2,1)S(1)}, u32[]{:S(2)}, u32[]{:S(2)}) collective-permute-start(bf16[64,2048]{1,0:T(8,128)(2,1)} %refs_8_.1), channel_id=1, source_target_pairs={{0,24},{2,26},{4,28},{6,30},{8,0},{10,2},{12,4},{14,6},{16,8},{18,... | collective-permute-start | bytes 786440 | tf_op jit(solution)/shard_map/ppermute | solution.py:204
  9.9 3.8 pad_maximum_fusion.refs_19_
  41.5 4.6 %collective-permute-done.10 = bf16[64,768]{1,0:T(8,128)(2,1)S(1)} collective-permute-done((bf16[64,768]{1,0:T(8,128)(2,1)S(1)}, bf16[64,768]{1,0:T(8,128)(2,1)S(1)}, u32[]{:S(2)}, u32[]{:S(2)}) %collective-permute-start.10) | collective-permute-done | bytes 98336 | tf_op jit(solution)/shard_map/ppermute | solution.py:204
  49.4 3.4 collective-permute-start.11
  53.0 21.3 %collective-permute-done.8.refs_2_.refs_10_ = bf16[64,4096]{1,0:T(8,128)(2,1)S(1)} collective-permute-done((bf16[64,4096]{1,0:T(8,128)(2,1)S(1)}, bf16[64,4096]{1,0:T(8,128)(2,1)S(1)}, u32[]{:S(2)}, u32[]{:S(2)}) %collective-permute-start.8) | collective-permute-done | bytes 524320 | tf_op jit(solution)/shard_map/ppermute | solution.py:204
  75.2 10.7 %collective-permute-start.5 = (bf16[64,4096]{1,0:T(8,128)(2,1)S(1)}, bf16[64,4096]{1,0:T(8,128)(2,1)S(1)}, u32[]{:S(2)}, u32[]{:S(2)}) collective-permute-start(bf16[64,4096]{1,0:T(8,128)(2,1)S(1)} %get-tuple-element.53.refs_0_.refs_8_), channel_id=1, source_target_pairs={{0,8},{2,10},{4,12},{6,14},{8,16},{10,18},{12,20},{14,22},{16,24},... | collective-permute-start | bytes 1572872 | tf_op jit(solution)/shard_map/ppermute | solution.py:204
  86.0 5.1 %collective-permute-done.16 = bf16[4,64,768]{2,1,0:T(8,128)(2,1)S(1)} collective-permute-done((bf16[4,64,768]{2,1,0:T(8,128)(2,1)S(1)}, bf16[4,64,768]{2,1,0:T(8,128)(2,1)S(1)}, u32[]{:S(2)}, u32[]{:S(2)}) %collective-permute-start.16) | collective-permute-done | bytes 393248 | tf_op jit(solution)/shard_map/ppermute | solution.py:204
  93.6 6.8 %collective-permute-done.5.refs_1_.refs_9_ = bf16[64,4096]{1,0:T(8,128)(2,1)S(1)} collective-permute-done((bf16[64,4096]{1,0:T(8,128)(2,1)S(1)}, bf16[64,4096]{1,0:T(8,128)(2,1)S(1)}, u32[]{:S(2)}, u32[]{:S(2)}) %collective-permute-start.5) | collective-permute-done | bytes 524320 | tf_op jit(solution)/shard_map/ppermute | solution.py:204
  102.5 7.3 %collective-permute-done.22 = bf16[256,256]{1,0:T(8,128)(2,1)S(1)} collective-permute-done((bf16[256,256]{1,0:T(8,128)(2,1)S(1)}, bf16[256,256]{1,0:T(8,128)(2,1)S(1)}, u32[]{:S(2)}, u32[]{:S(2)}) %collective-permute-start.22) | collective-permute-done | bytes 131104 | tf_op jit(solution)/shard_map/ppermute | solution.py:204
  111.7 15.3 %collective-permute-done.13.refs_5_.refs_13_ = bf16[64,4096]{1,0:T(8,128)(2,1)S(1)} collective-permute-done((bf16[64,4096]{1,0:T(8,128)(2,1)S(1)}, bf16[64,4096]{1,0:T(8,128)(2,1)S(1)}, u32[]{:S(2)}, u32[]{:S(2)}) %collective-permute-start.13) | collective-permute-done | bytes 524320 | tf_op jit(solution)/shard_map/ppermute | solution.py:204
  127.0 6.8 %collective-permute-start.26 = (bf16[64,4096]{1,0:T(8,128)(2,1)S(1)}, bf16[64,4096]{1,0:T(8,128)(2,1)}, u32[]{:S(2)}, u32[]{:S(2)}) collective-permute-start(bf16[64,4096]{1,0:T(8,128)(2,1)S(1)} %get-tuple-element.65.refs_0_.refs_8_), channel_id=1, source_target_pairs={{0,24},{2,26},{4,28},{6,30},{8,0},{10,2},{12,4},{14,6},{16,8},{18,... | collective-permute-start | bytes 1572872 | tf_op jit(solution)/shard_map/ppermute | solution.py:204
  136.2 11.7 %project.4 = (bf16[4,256,256]{2,1,0:T(8,128)(2,1)S(1)}, bf16[4,256,256]{2,1,0:T(8,128)(2,1)S(1)}, bf16[2,4,256,256]{3,2,1,0:T(8,128)(2,1)}) custom-call(s32[9]{0:T(128)S(1)} %stack.166.order_ref, bf16[64,4096]{1,0:T(8,128)(2,1)S(1)} %get-tuple-element.53.refs_0_.refs_8_, bf16[64,4096]{1,0:T(8,128)(2,1)S(1)} %collective-permute-done.5.refs_1_.refs_9_, ...), custom_call_target="tpu_custom_call" | custom-call | flops 6442450944 | bytes 12582912 | tf_op jit(solution)/shard_map/project/pallas_call | solution.py:251
  149.6 11.7 %project.5 = (bf16[4,256,256]{2,1,0:T(8,128)(2,1)S(1)}, bf16[4,256,256]{2,1,0:T(8,128)(2,1)S(1)}, bf16[2,4,256,256]{3,2,1,0:T(8,128)(2,1)}) custom-call(s32[9]{0:T(128)S(1)} %stack.166.order_ref, bf16[64,4096]{1,0:T(8,128)(2,1)S(1)} %get-tuple-element.53.refs_0_.refs_8_, bf16[64,4096]{1,0:T(8,128)(2,1)S(1)} %collective-permute-done.5.refs_1_.refs_9_, ...), custom_call_target="tpu_custom_call" | custom-call | flops 6442450944 | bytes 12582912 | tf_op jit(solution)/shard_map/project/pallas_call | solution.py:251
  174.6 6.8 %collective-permute-done.21.mate_ref = bf16[4,256,256]{2,1,0:T(8,128)(2,1)S(1)} collective-permute-done((bf16[4,256,256]{2,1,0:T(8,128)(2,1)S(1)}, bf16[4,256,256]{2,1,0:T(8,128)(2,1)S(1)}, u32[]{:S(2)}, u32[]{:S(2)}) %collective-permute-start.21) | collective-permute-done | bytes 524320 | tf_op jit(solution)/shard_map/ppermute | solution.py:204
  182.3 4.1 %weave.4.refs_1_.refs_0_ = f32[4,256,512]{2,1,0:T(8,128)} custom-call(s32[1]{0:T(128)} %bitcast.1.x_ref, bf16[4,256,256]{2,1,0:T(8,128)(2,1)} %copy-done.10, bf16[2,4,256,256]{3,2,1,0:T(8,128)(2,1)} %collective-permute-done.18.given_ref, bf16[4,256,256]{2,1,0:T(8,128)(2,1)} %copy-done.41), custom_call_target="tpu_custom_call" | custom-call | flops 524288 | bytes 4194304 | tf_op jit(solution)/shard_map/weave/pallas_call | solution.py:295
  186.4 15.0 %recall.4 = bf16[256,512]{1,0:T(8,128)(2,1)} custom-call(f32[4,64,64,512]{3,2,1,0:T(8,128)} %bitcast.206, f32[4,256,512]{2,1,0:T(8,128)} %weave.4.refs_1_.refs_0_, f32[4,256,512]{2,1,0:T(8,128)} %exponential_bitcast_fusion.refs_2_.refs_3_.refs_4_.refs_5_, f32[256,1]{1,0:T(8,128)} %copy.32.refs_3_.refs_5_, f32[256,1]{1,0:T(8,128)} %copy.33.refs_4_.refs_5_.refs_6_.refs_7_, ...), custom_call_target="tpu_custom_call" | custom-call | flops 16777216 | bytes 33554432 | tf_op jit(solution)/shard_map/recall/pallas_call | solution.py:368
  212.2 11.8 %project.6 = (bf16[4,256,256]{2,1,0:T(8,128)(2,1)S(1)}, bf16[4,256,256]{2,1,0:T(8,128)(2,1)S(1)}, bf16[2,4,256,256]{3,2,1,0:T(8,128)(2,1)}) custom-call(s32[9]{0:T(128)S(1)} %stack.166.order_ref, bf16[64,4096]{1,0:T(8,128)(2,1)S(1)} %get-tuple-element.65.refs_0_.refs_8_, bf16[64,4096]{1,0:T(8,128)(2,1)S(1)} %copy-done.20, ...), custom_call_target="tpu_custom_call" | custom-call | flops 6442450944 | bytes 12582912 | tf_op jit(solution)/shard_map/project/pallas_call | solution.py:251
  224.8 4.2 %weave.5.refs_2_.refs_1_ = f32[4,256,512]{2,1,0:T(8,128)} custom-call(s32[1]{0:T(128)} %bitcast.1.x_ref, bf16[4,256,256]{2,1,0:T(8,128)(2,1)} %copy-done.8, bf16[2,4,256,256]{3,2,1,0:T(8,128)(2,1)} %collective-permute-done.28.given_ref, bf16[4,256,256]{2,1,0:T(8,128)(2,1)} %collective-permute-done.29.mate_ref), custom_call_target="tpu_custom_call" | custom-call | flops 524288 | bytes 4194304 | tf_op jit(solution)/shard_map/weave/pallas_call | solution.py:295
  230.0 11.2 %project.7 = (bf16[4,256,256]{2,1,0:T(8,128)(2,1)S(1)}, bf16[4,256,256]{2,1,0:T(8,128)(2,1)S(1)}, bf16[2,4,256,256]{3,2,1,0:T(8,128)(2,1)S(1)}) custom-call(s32[9]{0:T(128)S(1)} %stack.166.order_ref, bf16[64,4096]{1,0:T(8,128)(2,1)S(1)} %get-tuple-element.65.refs_0_.refs_8_, bf16[64,4096]{1,0:T(8,128)(2,1)S(1)} %copy-done.21, ...), custom_call_target="tpu_custom_call" | custom-call | flops 6442450944 | bytes 12582912 | tf_op jit(solution)/shard_map/project/pallas_call | solution.py:251
  251.5 15.5 %recall.5 = bf16[256,512]{1,0:T(8,128)(2,1)} custom-call(f32[4,64,64,512]{3,2,1,0:T(8,128)} %bitcast.207, f32[4,256,512]{2,1,0:T(8,128)} %weave.4.refs_1_.refs_0_, f32[4,256,512]{2,1,0:T(8,128)} %weave.5.refs_2_.refs_1_, f32[4,256,512]{2,1,0:T(8,128)} %exponential_bitcast_fusion.refs_2_.refs_3_.refs_4_.refs_5_, f32[256,1]{1,0:T(8,128)} %copy.35.refs_4_, ...), custom_call_target="tpu_custom_call" | custom-call | flops 16777216 | bytes 33554432 | tf_op jit(solution)/shard_map/recall/pallas_call | solution.py:368
  268.9 3.8 collective-permute-start.36
  278.0 4.1 %weave.6.refs_3_.refs_2_ = f32[4,256,512]{2,1,0:T(8,128)} custom-call(s32[1]{0:T(128)} %bitcast.1.x_ref, bf16[4,256,256]{2,1,0:T(8,128)(2,1)} %copy-done.9, bf16[2,4,256,256]{3,2,1,0:T(8,128)(2,1)} %collective-permute-done.37.given_ref, bf16[4,256,256]{2,1,0:T(8,128)(2,1)} %copy-done.40), custom_call_target="tpu_custom_call" | custom-call | flops 524288 | bytes 4194304 | tf_op jit(solution)/shard_map/weave/pallas_call | solution.py:295
  282.1 16.3 %recall.6 = bf16[256,512]{1,0:T(8,128)(2,1)} custom-call(f32[4,64,64,512]{3,2,1,0:T(8,128)} %bitcast.208, f32[4,256,512]{2,1,0:T(8,128)} %weave.4.refs_1_.refs_0_, f32[4,256,512]{2,1,0:T(8,128)} %weave.5.refs_2_.refs_1_, f32[4,256,512]{2,1,0:T(8,128)} %weave.6.refs_3_.refs_2_, f32[4,256,512]{2,1,0:T(8,128)} %exponential_bitcast_fusion.refs_2_.refs_3_.refs_4_.refs_5_, ...), custom_call_target="tpu_custom_call" | custom-call | flops 16777216 | bytes 33554432 | tf_op jit(solution)/shard_map/recall/pallas_call | solution.py:368
  301.8 3.6 collective-permute-done.42
  306.3 4.2 %weave.7.refs_4_.refs_3_ = f32[4,256,512]{2,1,0:T(8,128)} custom-call(s32[1]{0:T(128)} %bitcast.1.x_ref, bf16[4,256,256]{2,1,0:T(8,128)(2,1)} %copy-done.7, bf16[2,4,256,256]{3,2,1,0:T(8,128)(2,1)} %collective-permute-done.38.given_ref, bf16[4,256,256]{2,1,0:T(8,128)(2,1)} %collective-permute-done.43.mate_ref), custom_call_target="tpu_custom_call" | custom-call | flops 524288 | bytes 4194304 | tf_op jit(solution)/shard_map/weave/pallas_call | solution.py:295
  313.4 16.8 %recall.7 = bf16[256,512]{1,0:T(8,128)(2,1)} custom-call(f32[4,64,64,512]{3,2,1,0:T(8,128)} %bitcast.209, f32[4,256,512]{2,1,0:T(8,128)} %weave.4.refs_1_.refs_0_, f32[4,256,512]{2,1,0:T(8,128)} %weave.5.refs_2_.refs_1_, f32[4,256,512]{2,1,0:T(8,128)} %weave.6.refs_3_.refs_2_, f32[4,256,512]{2,1,0:T(8,128)} %weave.7.refs_4_.refs_3_, ...), custom_call_target="tpu_custom_call" | custom-call | flops 16777216 | bytes 33554432 | tf_op jit(solution)/shard_map/recall/pallas_call | solution.py:368
  331.5 3.8 collective-permute-start.46
  339.4 3.3 collective-permute-done.44
  344.8 8.3 %collective-permute-done.45 = bf16[512,256]{1,0:T(8,128)(2,1)S(1)} collective-permute-done((bf16[512,256]{1,0:T(8,128)(2,1)S(1)}, bf16[512,256]{1,0:T(8,128)(2,1)S(1)}, u32[]{:S(2)}, u32[]{:S(2)}) %collective-permute-start.45) | collective-permute-done | bytes 262176 | tf_op jit(solution)/shard_map/ppermute | solution.py:204
  355.9 3.8 collective-permute-start.51
  364.0 27.1 %renew.1 = f32[4,64,64,512]{3,2,1,0:T(8,128)} custom-call(f32[4,64,64,512]{3,2,1,0:T(8,128)} %bitcast.210, f32[4,256,512]{2,1,0:T(8,128)S(1)} %copy-done.3, f32[4,256,512]{2,1,0:T(8,128)S(1)} %copy-done.4, f32[4,256,512]{2,1,0:T(8,128)S(1)} %copy-done.5, f32[4,256,512]{2,1,0:T(8,128)S(1)} %copy-done.6, f32[4,256,512]{2,1,0:T(8,128)S(1)} %copy-done.2), custom_call_target="tpu_custom_call" | custom-call | flops 75497472 | bytes 67108864 | tf_op jit(solution)/shard_map/renew/pallas_call | solution.py:422
  394.0 7.5 %collective-permute-done.54 = bf16[512,256]{1,0:T(8,128)(2,1)S(1)} collective-permute-done((bf16[512,256]{1,0:T(8,128)(2,1)S(1)}, bf16[512,256]{1,0:T(8,128)(2,1)S(1)}, u32[]{:S(2)}, u32[]{:S(2)}) %collective-permute-start.54) | collective-permute-done | bytes 262176 | tf_op jit(solution)/shard_map/ppermute | solution.py:204
  (308 shorter events, 117.3 us)
Async XLA Ops:
  0.6 35.8 %collective-permute-start.9 = (bf16[64,2048]{1,0:T(8,128)(2,1)}, bf16[64,2048]{1,0:T(8,128)(2,1)S(1)}, u32[]{:S(2)}, u32[]{:S(2)}) collective-permute-start(bf16[64,2048]{1,0:T(8,128)(2,1)} %refs_8_.1), channel_id=1, source_target_pairs={{0,24},{2,26},{4,28},{6,30},{8,0},{10,2},{12,4},{14,6},{16,8},{18,... | collective-permute-start | bytes 786440 | tf_op jit(solution)/shard_map/ppermute | solution.py:204
  5.7 30.7 %collective-permute-start.6 = (bf16[64,2048]{1,0:T(8,128)(2,1)}, bf16[64,2048]{1,0:T(8,128)(2,1)S(1)}, u32[]{:S(2)}, u32[]{:S(2)}) collective-permute-start(bf16[64,2048]{1,0:T(8,128)(2,1)} %refs_8_.1), channel_id=1, source_target_pairs={{0,16},{2,18},{4,20},{6,22},{8,24},{10,26},{12,28},{14,30},{16,0},... | collective-permute-start | bytes 786440 | tf_op jit(solution)/shard_map/ppermute | solution.py:204
  5.8 30.7 %collective-permute-start.3 = (bf16[64,2048]{1,0:T(8,128)(2,1)}, bf16[64,2048]{1,0:T(8,128)(2,1)S(1)}, u32[]{:S(2)}, u32[]{:S(2)}) collective-permute-start(bf16[64,2048]{1,0:T(8,128)(2,1)} %refs_8_.1), channel_id=1, source_target_pairs={{0,8},{2,10},{4,12},{6,14},{8,16},{10,18},{12,20},{14,22},{16,24},... | collective-permute-start | bytes 786440 | tf_op jit(solution)/shard_map/ppermute | solution.py:204
  13.7 121.5 %collective-permute-start.17 = (bf16[4,2048,256]{2,1,0:T(8,128)(2,1)}, bf16[4,2048,256]{2,1,0:T(8,128)(2,1)}, u32[]{:S(2)}, u32[]{:S(2)}) collective-permute-start(bf16[4,2048,256]{2,1,0:T(8,128)(2,1)} %pad_maximum_fusion.refs_19_), channel_id=1, source_target_pairs={{0,2},{2,0},{4,6},{6,4},{8,10},{10,8},{12,14},{14,12},{16,18},{18,... | collective-permute-start | bytes 12582920 | tf_op jit(solution)/shard_map/ppermute | solution.py:204
  34.7 65.8 %collective-permute-start.12 = (bf16[2,64,4096]{2,1,0:T(8,128)(2,1)}, bf16[2,64,4096]{2,1,0:T(8,128)(2,1)}, u32[]{:S(2)}, u32[]{:S(2)}) collective-permute-start(bf16[2,64,4096]{2,1,0:T(8,128)(2,1)} %pad_maximum_fusion.5), channel_id=1, source_target_pairs={{0,4},{2,6},{4,0},{6,2},{8,12},{10,14},{12,8},{14,10},{16,20},{18,... | collective-permute-start | bytes 3145736 | tf_op jit(solution)/shard_map/ppermute | solution.py:204
  46.1 55.0 %collective-permute-start.15 = (bf16[4,64,2048]{2,1,0:T(8,128)(2,1)S(1)}, bf16[4,64,2048]{2,1,0:T(8,128)(2,1)S(1)}, u32[]{:S(2)}, u32[]{:S(2)}) collective-permute-start(bf16[4,64,2048]{2,1,0:T(8,128)(2,1)S(1)} %fusion.14), channel_id=1, source_target_pairs={{0,4},{2,6},{4,0},{6,2},{8,12},{10,14},{12,8},{14,10},{16,20},{18,... | collective-permute-start | bytes 3145736 | tf_op jit(solution)/shard_map/ppermute | solution.py:204
  47.3 27.0 %collective-permute-start.8 = (bf16[64,4096]{1,0:T(8,128)(2,1)S(1)}, bf16[64,4096]{1,0:T(8,128)(2,1)S(1)}, u32[]{:S(2)}, u32[]{:S(2)}) collective-permute-start(bf16[64,4096]{1,0:T(8,128)(2,1)S(1)} %get-tuple-element.53.refs_0_.refs_8_), channel_id=1, source_target_pairs={{0,16},{2,18},{4,20},{6,22},{8,24},{10,26},{12,28},{14,30},{16,0},... | collective-permute-start | bytes 1572872 | tf_op jit(solution)/shard_map/ppermute | solution.py:204
  49.4 25.8 %collective-permute-start.11 = (bf16[64,4096]{1,0:T(8,128)(2,1)S(1)}, bf16[64,4096]{1,0:T(8,128)(2,1)S(1)}, u32[]{:S(2)}, u32[]{:S(2)}) collective-permute-start(bf16[64,4096]{1,0:T(8,128)(2,1)S(1)} %get-tuple-element.53.refs_0_.refs_8_), channel_id=1, source_target_pairs={{0,24},{2,26},{4,28},{6,30},{8,0},{10,2},{12,4},{14,6},{16,8},{18,... | collective-permute-start | bytes 1572872 | tf_op jit(solution)/shard_map/ppermute | solution.py:204
  75.2 25.3 %collective-permute-start.5 = (bf16[64,4096]{1,0:T(8,128)(2,1)S(1)}, bf16[64,4096]{1,0:T(8,128)(2,1)S(1)}, u32[]{:S(2)}, u32[]{:S(2)}) collective-permute-start(bf16[64,4096]{1,0:T(8,128)(2,1)S(1)} %get-tuple-element.53.refs_0_.refs_8_), channel_id=1, source_target_pairs={{0,8},{2,10},{4,12},{6,14},{8,16},{10,18},{12,20},{14,22},{16,24},... | collective-permute-start | bytes 1572872 | tf_op jit(solution)/shard_map/ppermute | solution.py:204
  91.1 44.1 %collective-permute-start.14 = (bf16[2,64,4096]{2,1,0:T(8,128)(2,1)S(1)}, bf16[2,64,4096]{2,1,0:T(8,128)(2,1)S(1)}, u32[]{:S(2)}, u32[]{:S(2)}) collective-permute-start(bf16[2,64,4096]{2,1,0:T(8,128)(2,1)S(1)} %pad_maximum_fusion.6), channel_id=1, source_target_pairs={{0,4},{2,6},{4,0},{6,2},{8,12},{10,14},{12,8},{14,10},{16,20},{18,... | collective-permute-start | bytes 3145736 | tf_op jit(solution)/shard_map/ppermute | solution.py:204
  100.5 26.5 %collective-permute-start.13 = (bf16[64,4096]{1,0:T(8,128)(2,1)S(1)}, bf16[64,4096]{1,0:T(8,128)(2,1)S(1)}, u32[]{:S(2)}, u32[]{:S(2)}) collective-permute-start(bf16[64,4096]{1,0:T(8,128)(2,1)S(1)} %collective-permute-done.5.refs_1_.refs_9_), channel_id=1, source_target_pairs={{0,4},{2,6},{4,0},{6,2},{8,12},{10,14},{12,8},{14,10},{16,20},{18,... | collective-permute-start | bytes 1572872 | tf_op jit(solution)/shard_map/ppermute | solution.py:204
  101.1 32.7 %collective-permute-start.19 = (bf16[64,4096]{1,0:T(8,128)(2,1)S(1)}, bf16[64,4096]{1,0:T(8,128)(2,1)S(1)}, u32[]{:S(2)}, u32[]{:S(2)}) collective-permute-start(bf16[64,4096]{1,0:T(8,128)(2,1)S(1)} %get-tuple-element.65.refs_0_.refs_8_), channel_id=1, source_target_pairs={{0,8},{2,10},{4,12},{6,14},{8,16},{10,18},{12,20},{14,22},{16,24},... | collective-permute-start | bytes 1572872 | tf_op jit(solution)/shard_map/ppermute | solution.py:204
  109.7 54.0 %collective-permute-start.25 = (bf16[64,4096]{1,0:T(8,128)(2,1)S(1)}, bf16[64,4096]{1,0:T(8,128)(2,1)}, u32[]{:S(2)}, u32[]{:S(2)}) collective-permute-start(bf16[64,4096]{1,0:T(8,128)(2,1)S(1)} %get-tuple-element.65.refs_0_.refs_8_), channel_id=1, source_target_pairs={{0,16},{2,18},{4,20},{6,22},{8,24},{10,26},{12,28},{14,30},{16,0},... | collective-permute-start | bytes 1572872 | tf_op jit(solution)/shard_map/ppermute | solution.py:204
  127.0 36.7 %collective-permute-start.26 = (bf16[64,4096]{1,0:T(8,128)(2,1)S(1)}, bf16[64,4096]{1,0:T(8,128)(2,1)}, u32[]{:S(2)}, u32[]{:S(2)}) collective-permute-start(bf16[64,4096]{1,0:T(8,128)(2,1)S(1)} %get-tuple-element.65.refs_0_.refs_8_), channel_id=1, source_target_pairs={{0,24},{2,26},{4,28},{6,30},{8,0},{10,2},{12,4},{14,6},{16,8},{18,... | collective-permute-start | bytes 1572872 | tf_op jit(solution)/shard_map/ppermute | solution.py:204
  166.0 46.1 %collective-permute-start.27 = (bf16[2,64,4096]{2,1,0:T(8,128)(2,1)}, bf16[2,64,4096]{2,1,0:T(8,128)(2,1)}, u32[]{:S(2)}, u32[]{:S(2)}) collective-permute-start(bf16[2,64,4096]{2,1,0:T(8,128)(2,1)} %pad_maximum_fusion.8), channel_id=1, source_target_pairs={{0,4},{2,6},{4,0},{6,2},{8,12},{10,14},{12,8},{14,10},{16,20},{18,... | collective-permute-start | bytes 3145736 | tf_op jit(solution)/shard_map/ppermute | solution.py:204
  170.6 30.8 %collective-permute-start.30 = (bf16[512,256]{1,0:T(8,128)(2,1)}, bf16[512,256]{1,0:T(8,128)(2,1)}, u32[]{:S(2)}, u32[]{:S(2)}) collective-permute-start(bf16[512,256]{1,0:T(8,128)(2,1)} %pad_maximum_fusion.24), channel_id=1, source_target_pairs={{0,24},{2,26},{4,28},{6,30},{8,0},{10,2},{12,4},{14,6},{16,8},{18,... | collective-permute-start | bytes 786440 | tf_op jit(solution)/shard_map/ppermute | solution.py:204
  170.7 33.6 %collective-permute-start.31 = (bf16[512,256]{1,0:T(8,128)(2,1)}, bf16[512,256]{1,0:T(8,128)(2,1)}, u32[]{:S(2)}, u32[]{:S(2)}) collective-permute-start(bf16[512,256]{1,0:T(8,128)(2,1)} %pad_maximum_fusion.25), channel_id=1, source_target_pairs={{0,16},{2,18},{4,20},{6,22},{8,24},{10,26},{12,28},{14,30},{16,0},... | collective-permute-start | bytes 786440 | tf_op jit(solution)/shard_map/ppermute | solution.py:204
  170.7 35.3 %collective-permute-start.32 = (bf16[512,256]{1,0:T(8,128)(2,1)}, bf16[512,256]{1,0:T(8,128)(2,1)}, u32[]{:S(2)}, u32[]{:S(2)}) collective-permute-start(bf16[512,256]{1,0:T(8,128)(2,1)} %pad_maximum_fusion.26), channel_id=1, source_target_pairs={{0,8},{2,10},{4,12},{6,14},{8,16},{10,18},{12,20},{14,22},{16,24},... | collective-permute-start | bytes 786440 | tf_op jit(solution)/shard_map/ppermute | solution.py:204
  181.5 43.3 %collective-permute-start.29 = (bf16[4,256,256]{2,1,0:T(8,128)(2,1)}, bf16[4,256,256]{2,1,0:T(8,128)(2,1)}, u32[]{:S(2)}, u32[]{:S(2)}) collective-permute-start(bf16[4,256,256]{2,1,0:T(8,128)(2,1)} %fusion.19), channel_id=1, source_target_pairs={{0,2},{2,0},{4,6},{6,4},{8,10},{10,8},{12,14},{14,12},{16,18},{18,... | collective-permute-start | bytes 1572872 | tf_op jit(solution)/shard_map/ppermute | solution.py:204
  207.8 34.8 %collective-permute-start.33 = (bf16[512,768]{1,0:T(8,128)(2,1)}, bf16[512,768]{1,0:T(8,128)(2,1)}, u32[]{:S(2)}, u32[]{:S(2)}) collective-permute-start(bf16[512,768]{1,0:T(8,128)(2,1)} %constant_dynamic-update-slice_fusion), channel_id=1, source_target_pairs={{0,1},{1,0},{2,3},{3,2},{4,5},{5,4},{6,7},{7,6},{8,9},{9,8},{10,11... | collective-permute-start | bytes 2359304 | tf_op jit(solution)/shard_map/ppermute | solution.py:208
  210.7 33.3 %collective-permute-start.24 = (bf16[512,512]{1,0:T(8,128)(2,1)}, bf16[512,512]{1,0:T(8,128)(2,1)}, u32[]{:S(2)}, u32[]{:S(2)}) collective-permute-start(bf16[512,512]{1,0:T(8,128)(2,1)} %pad_maximum_fusion.18), channel_id=1, source_target_pairs={{0,4},{2,6},{4,0},{6,2},{8,12},{10,14},{12,8},{14,10},{16,20},{18,... | collective-permute-start | bytes 1572872 | tf_op jit(solution)/shard_map/ppermute | solution.py:204
  248.6 28.3 %collective-permute-start.41 = (bf16[4,256,256]{2,1,0:T(8,128)(2,1)}, bf16[4,256,256]{2,1,0:T(8,128)(2,1)S(1)}, u32[]{:S(2)}, u32[]{:S(2)}) collective-permute-start(bf16[4,256,256]{2,1,0:T(8,128)(2,1)} %fusion.18), channel_id=1, source_target_pairs={{0,2},{2,0},{4,6},{6,4},{8,10},{10,8},{12,14},{14,12},{16,18},{18,... | collective-permute-start | bytes 1572872 | tf_op jit(solution)/shard_map/ppermute | solution.py:204
  268.9 29.5 %collective-permute-start.34 = (bf16[512,256]{1,0:T(8,128)(2,1)S(1)}, bf16[512,256]{1,0:T(8,128)(2,1)}, u32[]{:S(2)}, u32[]{:S(2)}) collective-permute-start(bf16[512,256]{1,0:T(8,128)(2,1)S(1)} %get-tuple-element.125), channel_id=1, source_target_pairs={{0,8},{2,10},{4,12},{6,14},{8,16},{10,18},{12,20},{14,22},{16,24},... | collective-permute-start | bytes 786440 | tf_op jit(solution)/shard_map/ppermute | solution.py:204
  268.9 30.5 %collective-permute-start.36 = (bf16[512,256]{1,0:T(8,128)(2,1)}, bf16[512,256]{1,0:T(8,128)(2,1)}, u32[]{:S(2)}, u32[]{:S(2)}) collective-permute-start(bf16[512,256]{1,0:T(8,128)(2,1)} %get-tuple-element.126), channel_id=1, source_target_pairs={{0,24},{2,26},{4,28},{6,30},{8,0},{10,2},{12,4},{14,6},{16,8},{18,... | collective-permute-start | bytes 786440 | tf_op jit(solution)/shard_map/ppermute | solution.py:204
  272.7 26.7 %collective-permute-start.35 = (bf16[512,256]{1,0:T(8,128)(2,1)}, bf16[512,256]{1,0:T(8,128)(2,1)}, u32[]{:S(2)}, u32[]{:S(2)}) collective-permute-start(bf16[512,256]{1,0:T(8,128)(2,1)} %get-tuple-element.127), channel_id=1, source_target_pairs={{0,16},{2,18},{4,20},{6,22},{8,24},{10,26},{12,28},{14,30},{16,0},... | collective-permute-start | bytes 786440 | tf_op jit(solution)/shard_map/ppermute | solution.py:204
  276.2 30.0 %collective-permute-start.40 = (bf16[512,512]{1,0:T(8,128)(2,1)S(1)}, bf16[512,512]{1,0:T(8,128)(2,1)S(1)}, u32[]{:S(2)}, u32[]{:S(2)}) collective-permute-start(bf16[512,512]{1,0:T(8,128)(2,1)S(1)} %pad_maximum_fusion.20), channel_id=1, source_target_pairs={{0,4},{2,6},{4,0},{6,2},{8,12},{10,14},{12,8},{14,10},{16,20},{18,... | collective-permute-start | bytes 1572872 | tf_op jit(solution)/shard_map/ppermute | solution.py:204
  276.9 29.4 %collective-permute-start.43 = (bf16[4,256,256]{2,1,0:T(8,128)(2,1)S(1)}, bf16[4,256,256]{2,1,0:T(8,128)(2,1)}, u32[]{:S(2)}, u32[]{:S(2)}) collective-permute-start(bf16[4,256,256]{2,1,0:T(8,128)(2,1)S(1)} %fusion.17), channel_id=1, source_target_pairs={{0,2},{2,0},{4,6},{6,4},{8,10},{10,8},{12,14},{14,12},{16,18},{18,... | collective-permute-start | bytes 1572872 | tf_op jit(solution)/shard_map/ppermute | solution.py:204
  355.8 35.3 %collective-permute-start.49 = (bf16[512,256]{1,0:T(8,128)(2,1)S(1)}, bf16[512,256]{1,0:T(8,128)(2,1)S(1)}, u32[]{:S(2)}, u32[]{:S(2)}) collective-permute-start(bf16[512,256]{1,0:T(8,128)(2,1)S(1)} %get-tuple-element.119), channel_id=1, source_target_pairs={{0,8},{2,10},{4,12},{6,14},{8,16},{10,18},{12,20},{14,22},{16,24},... | collective-permute-start | bytes 786440 | tf_op jit(solution)/shard_map/ppermute | solution.py:204
  355.9 37.2 %collective-permute-start.51 = (bf16[512,256]{1,0:T(8,128)(2,1)S(1)}, bf16[512,256]{1,0:T(8,128)(2,1)S(1)}, u32[]{:S(2)}, u32[]{:S(2)}) collective-permute-start(bf16[512,256]{1,0:T(8,128)(2,1)S(1)} %get-tuple-element.120), channel_id=1, source_target_pairs={{0,24},{2,26},{4,28},{6,30},{8,0},{10,2},{12,4},{14,6},{16,8},{18,... | collective-permute-start | bytes 786440 | tf_op jit(solution)/shard_map/ppermute | solution.py:204
  359.7 33.4 %collective-permute-start.50 = (bf16[512,256]{1,0:T(8,128)(2,1)S(1)}, bf16[512,256]{1,0:T(8,128)(2,1)S(1)}, u32[]{:S(2)}, u32[]{:S(2)}) collective-permute-start(bf16[512,256]{1,0:T(8,128)(2,1)S(1)} %get-tuple-element.121), channel_id=1, source_target_pairs={{0,16},{2,18},{4,20},{6,22},{8,24},{10,26},{12,28},{14,30},{16,0},... | collective-permute-start | bytes 786440 | tf_op jit(solution)/shard_map/ppermute | solution.py:204
  360.9 33.1 %collective-permute-start.55 = (bf16[512,256]{1,0:T(8,128)(2,1)S(1)}, bf16[512,256]{1,0:T(8,128)(2,1)S(1)}, u32[]{:S(2)}, u32[]{:S(2)}) collective-permute-start(bf16[512,256]{1,0:T(8,128)(2,1)S(1)} %get-tuple-element.122), channel_id=1, source_target_pairs={{0,24},{2,26},{4,28},{6,30},{8,0},{10,2},{12,4},{14,6},{16,8},{18,... | collective-permute-start | bytes 786440 | tf_op jit(solution)/shard_map/ppermute | solution.py:204
  361.7 39.9 %collective-permute-start.54 = (bf16[512,256]{1,0:T(8,128)(2,1)S(1)}, bf16[512,256]{1,0:T(8,128)(2,1)S(1)}, u32[]{:S(2)}, u32[]{:S(2)}) collective-permute-start(bf16[512,256]{1,0:T(8,128)(2,1)S(1)} %get-tuple-element.123), channel_id=1, source_target_pairs={{0,16},{2,18},{4,20},{6,22},{8,24},{10,26},{12,28},{14,30},{16,0},... | collective-permute-start | bytes 786440 | tf_op jit(solution)/shard_map/ppermute | solution.py:204
  (87 other events, 980.4 us)

commit v3 on v2

--- a/solution.py
+++ b/solution.py
@@ -278,8 +278,8 @@
 
 def weave_kernel(x_ref, kept_ref, given_ref, mate_ref, out_ref):
     chats = mate_ref.shape[1] // 4
-    own = kept_ref[0].astype(F32) + given_ref[0, 0].astype(F32)
-    mate = mate_ref[0].astype(F32)
+    own = (kept_ref[0].astype(F32) + given_ref[0, 0].astype(F32)).astype(BF16)
+    mate = mate_ref[0]
     first = x_ref[0] == 0
     for block in range(4):
         rows = slice(block * chats, (block + 1) * chats)
@@ -300,7 +300,7 @@
             in_specs=[side, pl.BlockSpec((1, 1, half, columns), lambda c, x: (0, c, 0, 0)), side],
             out_specs=pl.BlockSpec((1, columns, 2 * half), lambda c, x: (c, 0, 0)),
         ),
-        out_shape=jax.ShapeDtypeStruct((4, columns, 2 * half), F32),
+        out_shape=jax.ShapeDtypeStruct((4, columns, 2 * half), BF16),
         cost_estimate=pl.CostEstimate(
             flops=8 * half * columns, bytes_accessed=64 * half * columns, transcendentals=0
         ),
@@ -321,7 +321,7 @@
     @pl.when(part == 0)
     def _():
         for slot, step in enumerate(steps):
-            reach = line_refs[step][0]
+            reach = line_refs[step][0].astype(F32)
             for earlier in range(step):
                 reach = reach * decay_ref[earlier]
             reach_ref[slot] = reach
@@ -343,20 +343,20 @@
     def _():
         for slot, step in enumerate(steps):
             now_ref = line_refs[step]
-            acceptor = now_ref[0]
+            acceptor = now_ref[0].astype(F32)
             readout = total_ref[slot]
-            weight = jnp.sum(acceptor * bonus_ref[...] * now_ref[1], 0, keepdims=True)
-            readout = readout + weight * now_ref[2]
+            weight = jnp.sum(acceptor * bonus_ref[...] * now_ref[1].astype(F32), 0, keepdims=True)
+            readout = readout + weight * now_ref[2].astype(F32)
             for earlier in reversed(range(step)):
-                weight = jnp.sum(acceptor * line_refs[earlier][1], 0, keepdims=True)
-                readout = readout + weight * line_refs[earlier][2]
+                weight = jnp.sum(acceptor * line_refs[earlier][1].astype(F32), 0, keepdims=True)
+                readout = readout + weight * line_refs[earlier][2].astype(F32)
                 if earlier:
                     acceptor = acceptor * decay_ref[earlier]
             center = jnp.sum(readout, 0, keepdims=True) * (1.0 / span)
             offset = readout - center
             spread = jnp.sum(offset * offset, 0, keepdims=True) * (1.0 / span)
             scaled = offset * lax.rsqrt(spread + 0.00064)
-            gate = now_ref[3]
+            gate = now_ref[3].astype(F32)
             grouped = scaled * gain_ref[...] + offset_ref[...]
             out_refs[slot][...] = (grouped * (gate / (1.0 + jnp.exp(-gate)))).astype(BF16)
 
@@ -396,7 +396,7 @@
     def _():
         keep = jnp.ones_like(keep_ref)
         for step in reversed(range(steps)):
-            key_ref[step] = line_refs[step][1] * keep
+            key_ref[step] = line_refs[step][1].astype(F32) * keep
             keep = keep * decay_ref[step]
         keep_ref[...] = keep
 
@@ -405,7 +405,7 @@
         rows = pl.ds(pl.multiple_of(part * depth, depth), depth)
         keep = keep_ref[rows, lanes]
         keys = [key_ref[step, rows, lanes] for step in range(steps)]
-        values = [line_refs[step][2, :, lanes] for step in range(steps)]
+        values = [line_refs[step][2, :, lanes].astype(F32) for step in range(steps)]
         for row in range(depth):
             here = slice(row, row + 1)
             total = keep[here] * state_ref[0, row, :, lanes]
@@ -566,7 +566,7 @@
     )
     decay = jnp.exp(-jnp.exp(decay_log))
 
-    blocks = emission_projection.reshape(4 * PLANES, local_width, local_width)
+    blocks = after(emission_projection, normed).reshape(4 * PLANES, local_width, local_width)
 
     def plane_rows(shift, mates):
         start = ((z + PLANES - shift) % PLANES) * 4
@@ -581,9 +581,10 @@
     bonus = immediate_item_premium[:, None]
     gain = group_scaling_multiplier[:, None]
     offset = group_scaling_offset[:, None]
+    mixing_raising = after(blending_raising_coefficients, normed)
     raising = jnp.stack(
         [
-            jnp.pad(blending_raising_coefficients[kind + 1], ((kind * rank, (3 - kind) * rank), (0, 0)))
+            jnp.pad(mixing_raising[kind + 1], ((kind * rank, (3 - kind) * rank), (0, 0)))
             for kind in range(4)
         ]
     )

time: 405 us -> 398 us (0.983)
  Pallas kernels: 154 us -> 148 us
    unnamed x136 -> x142, local copies, waits for them, and re-layouts: 13.5 us -> 14.7 us
  transfers between devices with their start and end apart: 56 -> 56, of which waited for: 17 -> 17; matrix products, arithmetic and copies ran while one was open for 15% -> 14% of each run, Pallas kernels for 33% -> 33%
where the time goes in v3:
time: 398 us; the launch traced here: 396 us
  Pallas kernels  148 us (37%)
  waiting for transfers between devices  98.2 us (25%)
  starting transfers between devices  78.1 us (20%)
  other arithmetic  29.9 us (8%)
  local copies, waits for them, and re-layouts  26.3 us (7%)
  matrix products  13.9 us (3%)
    ppermute x48, waiting for transfers between devices, send(): return lax.ppermute(block, 'wide', pairs(move))  97.2 us
    ppermute x48, starting transfers between devices, send(): return lax.ppermute(block, 'wide', pairs(move))  76.5 us
    pallas_call x4, Pallas kernels, recall(): pl.pallas_call(functools.partial(recall_kernel, steps), grid=(heads, span...  60.8 us
    pallas_call x4, Pallas kernels, project(): pl.pallas_call(project_kernel, grid_spec=pltpu.PrefetchScalarGridSpec(num...  46.4 us
    pallas_call x1, Pallas kernels, renew(): pl.pallas_call(renew_kernel, grid=(heads, span // depth), in_specs=[block...  26.1 us
    pallas_call x4, Pallas kernels, weave(): pl.pallas_call(weave_kernel, grid_spec=pltpu.PrefetchScalarGridSpec(num_s...  15.1 us
    unnamed x142, local copies, waits for them, and re-layouts  14.7 us
  transfers between devices with their start and end apart: 56, of which 17 were waited for; matrix products, arithmetic and copies ran while one was open for 14% of the time, Pallas kernels for 33%

profile of v3, /device:TPU:0, one launch (start us, length us, event | category | flops | bytes accessed | tf_op | source)
XLA Modules:
  0.0 396.5 jit_solution(16935166061889283880)
XLA Ops:
  0.6 5.1 %collective-permute-start.9 = (bf16[64,2048]{1,0:T(8,128)(2,1)}, bf16[64,2048]{1,0:T(8,128)(2,1)S(1)}, u32[]{:S(2)}, u32[]{:S(2)}) collective-permute-start(bf16[64,2048]{1,0:T(8,128)(2,1)} %refs_8_.1), channel_id=1, source_target_pairs={{0,24},{2,26},{4,28},{6,30},{8,0},{10,2},{12,4},{14,6},{16,8},{18,... | collective-permute-start | bytes 786440 | tf_op jit(solution)/shard_map/ppermute | solution.py:204
  9.5 3.8 pad_maximum_fusion.refs_19_
  39.5 4.6 %collective-permute-done.10 = bf16[64,768]{1,0:T(8,128)(2,1)S(1)} collective-permute-done((bf16[64,768]{1,0:T(8,128)(2,1)S(1)}, bf16[64,768]{1,0:T(8,128)(2,1)S(1)}, u32[]{:S(2)}, u32[]{:S(2)}) %collective-permute-start.10) | collective-permute-done | bytes 98336 | tf_op jit(solution)/shard_map/ppermute | solution.py:204
  47.5 3.4 collective-permute-start.11
  51.0 21.3 %collective-permute-done.8.refs_2_.refs_10_ = bf16[64,4096]{1,0:T(8,128)(2,1)S(1)} collective-permute-done((bf16[64,4096]{1,0:T(8,128)(2,1)S(1)}, bf16[64,4096]{1,0:T(8,128)(2,1)S(1)}, u32[]{:S(2)}, u32[]{:S(2)}) %collective-permute-start.8) | collective-permute-done | bytes 524320 | tf_op jit(solution)/shard_map/ppermute | solution.py:204
  73.2 10.8 %collective-permute-start.5 = (bf16[64,4096]{1,0:T(8,128)(2,1)S(1)}, bf16[64,4096]{1,0:T(8,128)(2,1)S(1)}, u32[]{:S(2)}, u32[]{:S(2)}) collective-permute-start(bf16[64,4096]{1,0:T(8,128)(2,1)S(1)} %get-tuple-element.55.refs_0_.refs_8_), channel_id=1, source_target_pairs={{0,8},{2,10},{4,12},{6,14},{8,16},{10,18},{12,20},{14,22},{16,24},... | collective-permute-start | bytes 1572872 | tf_op jit(solution)/shard_map/ppermute | solution.py:204
  84.1 5.1 %collective-permute-done.16 = bf16[4,64,768]{2,1,0:T(8,128)(2,1)S(1)} collective-permute-done((bf16[4,64,768]{2,1,0:T(8,128)(2,1)S(1)}, bf16[4,64,768]{2,1,0:T(8,128)(2,1)S(1)}, u32[]{:S(2)}, u32[]{:S(2)}) %collective-permute-start.16) | collective-permute-done | bytes 393248 | tf_op jit(solution)/shard_map/ppermute | solution.py:204
  91.7 6.8 %collective-permute-done.5.refs_1_.refs_9_ = bf16[64,4096]{1,0:T(8,128)(2,1)S(1)} collective-permute-done((bf16[64,4096]{1,0:T(8,128)(2,1)S(1)}, bf16[64,4096]{1,0:T(8,128)(2,1)S(1)}, u32[]{:S(2)}, u32[]{:S(2)}) %collective-permute-start.5) | collective-permute-done | bytes 524320 | tf_op jit(solution)/shard_map/ppermute | solution.py:204
  100.5 8.7 %collective-permute-done.22 = bf16[256,256]{1,0:T(8,128)(2,1)S(1)} collective-permute-done((bf16[256,256]{1,0:T(8,128)(2,1)S(1)}, bf16[256,256]{1,0:T(8,128)(2,1)S(1)}, u32[]{:S(2)}, u32[]{:S(2)}) %collective-permute-start.22) | collective-permute-done | bytes 131104 | tf_op jit(solution)/shard_map/ppermute | solution.py:204
  111.3 13.8 %collective-permute-done.13.refs_5_.refs_13_ = bf16[64,4096]{1,0:T(8,128)(2,1)S(1)} collective-permute-done((bf16[64,4096]{1,0:T(8,128)(2,1)S(1)}, bf16[64,4096]{1,0:T(8,128)(2,1)S(1)}, u32[]{:S(2)}, u32[]{:S(2)}) %collective-permute-start.13) | collective-permute-done | bytes 524320 | tf_op jit(solution)/shard_map/ppermute | solution.py:204
  125.1 6.8 %collective-permute-start.26 = (bf16[64,4096]{1,0:T(8,128)(2,1)S(1)}, bf16[64,4096]{1,0:T(8,128)(2,1)}, u32[]{:S(2)}, u32[]{:S(2)}) collective-permute-start(bf16[64,4096]{1,0:T(8,128)(2,1)S(1)} %get-tuple-element.68.refs_0_.refs_8_), channel_id=1, source_target_pairs={{0,24},{2,26},{4,28},{6,30},{8,0},{10,2},{12,4},{14,6},{16,8},{18,... | collective-permute-start | bytes 1572872 | tf_op jit(solution)/shard_map/ppermute | solution.py:204
  134.2 11.7 %project.4 = (bf16[4,256,256]{2,1,0:T(8,128)(2,1)S(1)}, bf16[4,256,256]{2,1,0:T(8,128)(2,1)S(1)}, bf16[2,4,256,256]{3,2,1,0:T(8,128)(2,1)}) custom-call(s32[9]{0:T(128)S(1)} %stack.166.order_ref, bf16[64,4096]{1,0:T(8,128)(2,1)S(1)} %get-tuple-element.55.refs_0_.refs_8_, bf16[64,4096]{1,0:T(8,128)(2,1)S(1)} %collective-permute-done.5.refs_1_.refs_9_, ...), custom_call_target="tpu_custom_call" | custom-call | flops 6442450944 | bytes 12582912 | tf_op jit(solution)/shard_map/project/pallas_call | solution.py:251
  147.6 11.7 %project.5 = (bf16[4,256,256]{2,1,0:T(8,128)(2,1)S(1)}, bf16[4,256,256]{2,1,0:T(8,128)(2,1)S(1)}, bf16[2,4,256,256]{3,2,1,0:T(8,128)(2,1)}) custom-call(s32[9]{0:T(128)S(1)} %stack.166.order_ref, bf16[64,4096]{1,0:T(8,128)(2,1)S(1)} %get-tuple-element.55.refs_0_.refs_8_, bf16[64,4096]{1,0:T(8,128)(2,1)S(1)} %collective-permute-done.5.refs_1_.refs_9_, ...), custom_call_target="tpu_custom_call" | custom-call | flops 6442450944 | bytes 12582912 | tf_op jit(solution)/shard_map/project/pallas_call | solution.py:251
  172.6 6.9 %collective-permute-done.21.mate_ref = bf16[4,256,256]{2,1,0:T(8,128)(2,1)S(1)} collective-permute-done((bf16[4,256,256]{2,1,0:T(8,128)(2,1)S(1)}, bf16[4,256,256]{2,1,0:T(8,128)(2,1)S(1)}, u32[]{:S(2)}, u32[]{:S(2)}) %collective-permute-start.21) | collective-permute-done | bytes 524320 | tf_op jit(solution)/shard_map/ppermute | solution.py:204
  180.4 3.7 weave.4.refs_1_.refs_0_
  184.1 14.8 %recall.4 = bf16[256,512]{1,0:T(8,128)(2,1)} custom-call(f32[4,64,64,512]{3,2,1,0:T(8,128)} %bitcast.206, bf16[4,256,512]{2,1,0:T(8,128)(2,1)} %weave.4.refs_1_.refs_0_, f32[4,256,512]{2,1,0:T(8,128)} %exponential_bitcast_fusion.refs_2_.refs_3_.refs_4_.refs_5_, f32[256,1]{1,0:T(8,128)} %copy.32.refs_3_.refs_5_, ...), custom_call_target="tpu_custom_call" | custom-call | flops 16777216 | bytes 33554432 | tf_op jit(solution)/shard_map/recall/pallas_call | solution.py:368
  209.7 11.8 %project.6 = (bf16[4,256,256]{2,1,0:T(8,128)(2,1)S(1)}, bf16[4,256,256]{2,1,0:T(8,128)(2,1)S(1)}, bf16[2,4,256,256]{3,2,1,0:T(8,128)(2,1)}) custom-call(s32[9]{0:T(128)S(1)} %stack.166.order_ref, bf16[64,4096]{1,0:T(8,128)(2,1)S(1)} %get-tuple-element.68.refs_0_.refs_8_, bf16[64,4096]{1,0:T(8,128)(2,1)S(1)} %copy-done.20, ...), custom_call_target="tpu_custom_call" | custom-call | flops 6442450944 | bytes 12582912 | tf_op jit(solution)/shard_map/project/pallas_call | solution.py:251
  222.3 3.8 weave.5.refs_2_.refs_1_
  227.2 11.2 %project.7 = (bf16[4,256,256]{2,1,0:T(8,128)(2,1)S(1)}, bf16[4,256,256]{2,1,0:T(8,128)(2,1)S(1)}, bf16[2,4,256,256]{3,2,1,0:T(8,128)(2,1)S(1)}) custom-call(s32[9]{0:T(128)S(1)} %stack.166.order_ref, bf16[64,4096]{1,0:T(8,128)(2,1)S(1)} %get-tuple-element.68.refs_0_.refs_8_, bf16[64,4096]{1,0:T(8,128)(2,1)S(1)} %copy-done.21, ...), custom_call_target="tpu_custom_call" | custom-call | flops 6442450944 | bytes 12582912 | tf_op jit(solution)/shard_map/project/pallas_call | solution.py:251
  248.0 15.0 %recall.5 = bf16[256,512]{1,0:T(8,128)(2,1)} custom-call(f32[4,64,64,512]{3,2,1,0:T(8,128)} %bitcast.207, bf16[4,256,512]{2,1,0:T(8,128)(2,1)} %weave.4.refs_1_.refs_0_, bf16[4,256,512]{2,1,0:T(8,128)(2,1)} %weave.5.refs_2_.refs_1_, f32[4,256,512]{2,1,0:T(8,128)} %exponential_bitcast_fusion.refs_2_.refs_3_.refs_4_.refs_5_, f32[256,1]{1,0:T(8,128)} %copy.35.refs_4_, ...), custom_call_target="tpu_custom_call" | custom-call | flops 16777216 | bytes 33554432 | tf_op jit(solution)/shard_map/recall/pallas_call | solution.py:368
  264.9 3.8 collective-permute-start.36
  274.0 3.7 weave.6.refs_3_.refs_2_
  277.8 15.3 %recall.6 = bf16[256,512]{1,0:T(8,128)(2,1)} custom-call(f32[4,64,64,512]{3,2,1,0:T(8,128)} %bitcast.208, bf16[4,256,512]{2,1,0:T(8,128)(2,1)} %weave.4.refs_1_.refs_0_, bf16[4,256,512]{2,1,0:T(8,128)(2,1)} %weave.5.refs_2_.refs_1_, bf16[4,256,512]{2,1,0:T(8,128)(2,1)} %weave.6.refs_3_.refs_2_, ...), custom_call_target="tpu_custom_call" | custom-call | flops 16777216 | bytes 33554432 | tf_op jit(solution)/shard_map/recall/pallas_call | solution.py:368
  296.6 3.5 collective-permute-done.42
  301.1 3.8 weave.7.refs_4_.refs_3_
  307.9 15.6 %recall.7 = bf16[256,512]{1,0:T(8,128)(2,1)} custom-call(f32[4,64,64,512]{3,2,1,0:T(8,128)} %bitcast.209, bf16[4,256,512]{2,1,0:T(8,128)(2,1)} %weave.4.refs_1_.refs_0_, bf16[4,256,512]{2,1,0:T(8,128)(2,1)} %weave.5.refs_2_.refs_1_, bf16[4,256,512]{2,1,0:T(8,128)(2,1)} %weave.6.refs_3_.refs_2_, bf16[4,256,512]{2,1,0:T(8,128)(2,1)} %weave.7.refs_4_.refs_3_, ...), custom_call_target="tpu_custom_call" | custom-call | flops 16777216 | bytes 33554432 | tf_op jit(solution)/shard_map/recall/pallas_call | solution.py:368
  324.7 3.8 collective-permute-start.46
  332.5 3.3 collective-permute-done.44
  337.9 8.3 %collective-permute-done.45 = bf16[512,256]{1,0:T(8,128)(2,1)S(1)} collective-permute-done((bf16[512,256]{1,0:T(8,128)(2,1)S(1)}, bf16[512,256]{1,0:T(8,128)(2,1)S(1)}, u32[]{:S(2)}, u32[]{:S(2)}) %collective-permute-start.45) | collective-permute-done | bytes 262176 | tf_op jit(solution)/shard_map/ppermute | solution.py:204
  349.0 3.8 collective-permute-start.51
  357.1 26.1 %renew.1 = f32[4,64,64,512]{3,2,1,0:T(8,128)} custom-call(f32[4,64,64,512]{3,2,1,0:T(8,128)} %bitcast.210, bf16[4,256,512]{2,1,0:T(8,128)(2,1)S(1)} %copy-done.3, bf16[4,256,512]{2,1,0:T(8,128)(2,1)S(1)} %copy-done.4, bf16[4,256,512]{2,1,0:T(8,128)(2,1)S(1)} %copy-done.5, bf16[4,256,512]{2,1,0:T(8,128)(2,1)S(1)} %copy-done.6, f32[4,256,512]{2,1,0:T(8,128)S(1)} %copy-done.2), custom_call_target="tpu_custom_call" | custom-call | flops 75497472 | bytes 67108864 | tf_op jit(solution)/shard_map/renew/pallas_call | solution.py:422
  386.2 8.2 %collective-permute-done.54 = bf16[512,256]{1,0:T(8,128)(2,1)S(1)} collective-permute-done((bf16[512,256]{1,0:T(8,128)(2,1)S(1)}, bf16[512,256]{1,0:T(8,128)(2,1)S(1)}, u32[]{:S(2)}, u32[]{:S(2)}) %collective-permute-start.54) | collective-permute-done | bytes 262176 | tf_op jit(solution)/shard_map/ppermute | solution.py:204
  (314 shorter events, 114.3 us)
Async XLA Ops:
  0.6 33.8 %collective-permute-start.9 = (bf16[64,2048]{1,0:T(8,128)(2,1)}, bf16[64,2048]{1,0:T(8,128)(2,1)S(1)}, u32[]{:S(2)}, u32[]{:S(2)}) collective-permute-start(bf16[64,2048]{1,0:T(8,128)(2,1)} %refs_8_.1), channel_id=1, source_target_pairs={{0,24},{2,26},{4,28},{6,30},{8,0},{10,2},{12,4},{14,6},{16,8},{18,... | collective-permute-start | bytes 786440 | tf_op jit(solution)/shard_map/ppermute | solution.py:204
  5.7 28.7 %collective-permute-start.6 = (bf16[64,2048]{1,0:T(8,128)(2,1)}, bf16[64,2048]{1,0:T(8,128)(2,1)S(1)}, u32[]{:S(2)}, u32[]{:S(2)}) collective-permute-start(bf16[64,2048]{1,0:T(8,128)(2,1)} %refs_8_.1), channel_id=1, source_target_pairs={{0,16},{2,18},{4,20},{6,22},{8,24},{10,26},{12,28},{14,30},{16,0},... | collective-permute-start | bytes 786440 | tf_op jit(solution)/shard_map/ppermute | solution.py:204
  5.8 28.7 %collective-permute-start.3 = (bf16[64,2048]{1,0:T(8,128)(2,1)}, bf16[64,2048]{1,0:T(8,128)(2,1)S(1)}, u32[]{:S(2)}, u32[]{:S(2)}) collective-permute-start(bf16[64,2048]{1,0:T(8,128)(2,1)} %refs_8_.1), channel_id=1, source_target_pairs={{0,8},{2,10},{4,12},{6,14},{8,16},{10,18},{12,20},{14,22},{16,24},... | collective-permute-start | bytes 786440 | tf_op jit(solution)/shard_map/ppermute | solution.py:204
  13.3 120.0 %collective-permute-start.17 = (bf16[4,2048,256]{2,1,0:T(8,128)(2,1)}, bf16[4,2048,256]{2,1,0:T(8,128)(2,1)}, u32[]{:S(2)}, u32[]{:S(2)}) collective-permute-start(bf16[4,2048,256]{2,1,0:T(8,128)(2,1)} %pad_maximum_fusion.refs_19_), channel_id=1, source_target_pairs={{0,2},{2,0},{4,6},{6,4},{8,10},{10,8},{12,14},{14,12},{16,18},{18,... | collective-permute-start | bytes 12582920 | tf_op jit(solution)/shard_map/ppermute | solution.py:204
  32.7 65.8 %collective-permute-start.12 = (bf16[2,64,4096]{2,1,0:T(8,128)(2,1)}, bf16[2,64,4096]{2,1,0:T(8,128)(2,1)}, u32[]{:S(2)}, u32[]{:S(2)}) collective-permute-start(bf16[2,64,4096]{2,1,0:T(8,128)(2,1)} %pad_maximum_fusion.5), channel_id=1, source_target_pairs={{0,4},{2,6},{4,0},{6,2},{8,12},{10,14},{12,8},{14,10},{16,20},{18,... | collective-permute-start | bytes 3145736 | tf_op jit(solution)/shard_map/ppermute | solution.py:204
  44.1 55.1 %collective-permute-start.15 = (bf16[4,64,2048]{2,1,0:T(8,128)(2,1)S(1)}, bf16[4,64,2048]{2,1,0:T(8,128)(2,1)S(1)}, u32[]{:S(2)}, u32[]{:S(2)}) collective-permute-start(bf16[4,64,2048]{2,1,0:T(8,128)(2,1)S(1)} %fusion.14), channel_id=1, source_target_pairs={{0,4},{2,6},{4,0},{6,2},{8,12},{10,14},{12,8},{14,10},{16,20},{18,... | collective-permute-start | bytes 3145736 | tf_op jit(solution)/shard_map/ppermute | solution.py:204
  45.3 27.0 %collective-permute-start.8 = (bf16[64,4096]{1,0:T(8,128)(2,1)S(1)}, bf16[64,4096]{1,0:T(8,128)(2,1)S(1)}, u32[]{:S(2)}, u32[]{:S(2)}) collective-permute-start(bf16[64,4096]{1,0:T(8,128)(2,1)S(1)} %get-tuple-element.55.refs_0_.refs_8_), channel_id=1, source_target_pairs={{0,16},{2,18},{4,20},{6,22},{8,24},{10,26},{12,28},{14,30},{16,0},... | collective-permute-start | bytes 1572872 | tf_op jit(solution)/shard_map/ppermute | solution.py:204
  47.5 25.7 %collective-permute-start.11 = (bf16[64,4096]{1,0:T(8,128)(2,1)S(1)}, bf16[64,4096]{1,0:T(8,128)(2,1)S(1)}, u32[]{:S(2)}, u32[]{:S(2)}) collective-permute-start(bf16[64,4096]{1,0:T(8,128)(2,1)S(1)} %get-tuple-element.55.refs_0_.refs_8_), channel_id=1, source_target_pairs={{0,24},{2,26},{4,28},{6,30},{8,0},{10,2},{12,4},{14,6},{16,8},{18,... | collective-permute-start | bytes 1572872 | tf_op jit(solution)/shard_map/ppermute | solution.py:204
  73.2 25.4 %collective-permute-start.5 = (bf16[64,4096]{1,0:T(8,128)(2,1)S(1)}, bf16[64,4096]{1,0:T(8,128)(2,1)S(1)}, u32[]{:S(2)}, u32[]{:S(2)}) collective-permute-start(bf16[64,4096]{1,0:T(8,128)(2,1)S(1)} %get-tuple-element.55.refs_0_.refs_8_), channel_id=1, source_target_pairs={{0,8},{2,10},{4,12},{6,14},{8,16},{10,18},{12,20},{14,22},{16,24},... | collective-permute-start | bytes 1572872 | tf_op jit(solution)/shard_map/ppermute | solution.py:204
  89.2 44.1 %collective-permute-start.14 = (bf16[2,64,4096]{2,1,0:T(8,128)(2,1)S(1)}, bf16[2,64,4096]{2,1,0:T(8,128)(2,1)S(1)}, u32[]{:S(2)}, u32[]{:S(2)}) collective-permute-start(bf16[2,64,4096]{2,1,0:T(8,128)(2,1)S(1)} %pad_maximum_fusion.6), channel_id=1, source_target_pairs={{0,4},{2,6},{4,0},{6,2},{8,12},{10,14},{12,8},{14,10},{16,20},{18,... | collective-permute-start | bytes 3145736 | tf_op jit(solution)/shard_map/ppermute | solution.py:204
  98.5 26.5 %collective-permute-start.13 = (bf16[64,4096]{1,0:T(8,128)(2,1)S(1)}, bf16[64,4096]{1,0:T(8,128)(2,1)S(1)}, u32[]{:S(2)}, u32[]{:S(2)}) collective-permute-start(bf16[64,4096]{1,0:T(8,128)(2,1)S(1)} %collective-permute-done.5.refs_1_.refs_9_), channel_id=1, source_target_pairs={{0,4},{2,6},{4,0},{6,2},{8,12},{10,14},{12,8},{14,10},{16,20},{18,... | collective-permute-start | bytes 1572872 | tf_op jit(solution)/shard_map/ppermute | solution.py:204
  99.2 32.8 %collective-permute-start.19 = (bf16[64,4096]{1,0:T(8,128)(2,1)S(1)}, bf16[64,4096]{1,0:T(8,128)(2,1)S(1)}, u32[]{:S(2)}, u32[]{:S(2)}) collective-permute-start(bf16[64,4096]{1,0:T(8,128)(2,1)S(1)} %get-tuple-element.68.refs_0_.refs_8_), channel_id=1, source_target_pairs={{0,8},{2,10},{4,12},{6,14},{8,16},{10,18},{12,20},{14,22},{16,24},... | collective-permute-start | bytes 1572872 | tf_op jit(solution)/shard_map/ppermute | solution.py:204
  109.3 52.4 %collective-permute-start.25 = (bf16[64,4096]{1,0:T(8,128)(2,1)S(1)}, bf16[64,4096]{1,0:T(8,128)(2,1)}, u32[]{:S(2)}, u32[]{:S(2)}) collective-permute-start(bf16[64,4096]{1,0:T(8,128)(2,1)S(1)} %get-tuple-element.68.refs_0_.refs_8_), channel_id=1, source_target_pairs={{0,16},{2,18},{4,20},{6,22},{8,24},{10,26},{12,28},{14,30},{16,0},... | collective-permute-start | bytes 1572872 | tf_op jit(solution)/shard_map/ppermute | solution.py:204
  125.1 36.7 %collective-permute-start.26 = (bf16[64,4096]{1,0:T(8,128)(2,1)S(1)}, bf16[64,4096]{1,0:T(8,128)(2,1)}, u32[]{:S(2)}, u32[]{:S(2)}) collective-permute-start(bf16[64,4096]{1,0:T(8,128)(2,1)S(1)} %get-tuple-element.68.refs_0_.refs_8_), channel_id=1, source_target_pairs={{0,24},{2,26},{4,28},{6,30},{8,0},{10,2},{12,4},{14,6},{16,8},{18,... | collective-permute-start | bytes 1572872 | tf_op jit(solution)/shard_map/ppermute | solution.py:204
  164.1 45.6 %collective-permute-start.27 = (bf16[2,64,4096]{2,1,0:T(8,128)(2,1)}, bf16[2,64,4096]{2,1,0:T(8,128)(2,1)}, u32[]{:S(2)}, u32[]{:S(2)}) collective-permute-start(bf16[2,64,4096]{2,1,0:T(8,128)(2,1)} %pad_maximum_fusion.8), channel_id=1, source_target_pairs={{0,4},{2,6},{4,0},{6,2},{8,12},{10,14},{12,8},{14,10},{16,20},{18,... | collective-permute-start | bytes 3145736 | tf_op jit(solution)/shard_map/ppermute | solution.py:204
  168.7 30.3 %collective-permute-start.30 = (bf16[512,256]{1,0:T(8,128)(2,1)}, bf16[512,256]{1,0:T(8,128)(2,1)}, u32[]{:S(2)}, u32[]{:S(2)}) collective-permute-start(bf16[512,256]{1,0:T(8,128)(2,1)} %pad_maximum_fusion.24), channel_id=1, source_target_pairs={{0,24},{2,26},{4,28},{6,30},{8,0},{10,2},{12,4},{14,6},{16,8},{18,... | collective-permute-start | bytes 786440 | tf_op jit(solution)/shard_map/ppermute | solution.py:204
  168.7 33.3 %collective-permute-start.31 = (bf16[512,256]{1,0:T(8,128)(2,1)}, bf16[512,256]{1,0:T(8,128)(2,1)}, u32[]{:S(2)}, u32[]{:S(2)}) collective-permute-start(bf16[512,256]{1,0:T(8,128)(2,1)} %pad_maximum_fusion.25), channel_id=1, source_target_pairs={{0,16},{2,18},{4,20},{6,22},{8,24},{10,26},{12,28},{14,30},{16,0},... | collective-permute-start | bytes 786440 | tf_op jit(solution)/shard_map/ppermute | solution.py:204
  168.7 34.9 %collective-permute-start.32 = (bf16[512,256]{1,0:T(8,128)(2,1)}, bf16[512,256]{1,0:T(8,128)(2,1)}, u32[]{:S(2)}, u32[]{:S(2)}) collective-permute-start(bf16[512,256]{1,0:T(8,128)(2,1)} %pad_maximum_fusion.26), channel_id=1, source_target_pairs={{0,8},{2,10},{4,12},{6,14},{8,16},{10,18},{12,20},{14,22},{16,24},... | collective-permute-start | bytes 786440 | tf_op jit(solution)/shard_map/ppermute | solution.py:204
  179.6 42.8 %collective-permute-start.29 = (bf16[4,256,256]{2,1,0:T(8,128)(2,1)}, bf16[4,256,256]{2,1,0:T(8,128)(2,1)}, u32[]{:S(2)}, u32[]{:S(2)}) collective-permute-start(bf16[4,256,256]{2,1,0:T(8,128)(2,1)} %fusion.19), channel_id=1, source_target_pairs={{0,2},{2,0},{4,6},{6,4},{8,10},{10,8},{12,14},{14,12},{16,18},{18,... | collective-permute-start | bytes 1572872 | tf_op jit(solution)/shard_map/ppermute | solution.py:204
  205.4 34.3 %collective-permute-start.33 = (bf16[512,768]{1,0:T(8,128)(2,1)}, bf16[512,768]{1,0:T(8,128)(2,1)}, u32[]{:S(2)}, u32[]{:S(2)}) collective-permute-start(bf16[512,768]{1,0:T(8,128)(2,1)} %constant_dynamic-update-slice_fusion), channel_id=1, source_target_pairs={{0,1},{1,0},{2,3},{3,2},{4,5},{5,4},{6,7},{7,6},{8,9},{9,8},{10,11... | collective-permute-start | bytes 2359304 | tf_op jit(solution)/shard_map/ppermute | solution.py:208
  208.3 32.8 %collective-permute-start.24 = (bf16[512,512]{1,0:T(8,128)(2,1)}, bf16[512,512]{1,0:T(8,128)(2,1)}, u32[]{:S(2)}, u32[]{:S(2)}) collective-permute-start(bf16[512,512]{1,0:T(8,128)(2,1)} %pad_maximum_fusion.18), channel_id=1, source_target_pairs={{0,4},{2,6},{4,0},{6,2},{8,12},{10,14},{12,8},{14,10},{16,20},{18,... | collective-permute-start | bytes 1572872 | tf_op jit(solution)/shard_map/ppermute | solution.py:204
  245.0 28.0 %collective-permute-start.41 = (bf16[4,256,256]{2,1,0:T(8,128)(2,1)S(1)}, bf16[4,256,256]{2,1,0:T(8,128)(2,1)S(1)}, u32[]{:S(2)}, u32[]{:S(2)}) collective-permute-start(bf16[4,256,256]{2,1,0:T(8,128)(2,1)S(1)} %fusion.18), channel_id=1, source_target_pairs={{0,2},{2,0},{4,6},{6,4},{8,10},{10,8},{12,14},{14,12},{16,18},{18,... | collective-permute-start | bytes 1572872 | tf_op jit(solution)/shard_map/ppermute | solution.py:204
  264.9 28.2 %collective-permute-start.34 = (bf16[512,256]{1,0:T(8,128)(2,1)}, bf16[512,256]{1,0:T(8,128)(2,1)}, u32[]{:S(2)}, u32[]{:S(2)}) collective-permute-start(bf16[512,256]{1,0:T(8,128)(2,1)} %get-tuple-element.129), channel_id=1, source_target_pairs={{0,8},{2,10},{4,12},{6,14},{8,16},{10,18},{12,20},{14,22},{16,24},... | collective-permute-start | bytes 786440 | tf_op jit(solution)/shard_map/ppermute | solution.py:204
  264.9 29.3 %collective-permute-start.36 = (bf16[512,256]{1,0:T(8,128)(2,1)}, bf16[512,256]{1,0:T(8,128)(2,1)}, u32[]{:S(2)}, u32[]{:S(2)}) collective-permute-start(bf16[512,256]{1,0:T(8,128)(2,1)} %get-tuple-element.130), channel_id=1, source_target_pairs={{0,24},{2,26},{4,28},{6,30},{8,0},{10,2},{12,4},{14,6},{16,8},{18,... | collective-permute-start | bytes 786440 | tf_op jit(solution)/shard_map/ppermute | solution.py:204
  268.7 25.4 %collective-permute-start.35 = (bf16[512,256]{1,0:T(8,128)(2,1)}, bf16[512,256]{1,0:T(8,128)(2,1)}, u32[]{:S(2)}, u32[]{:S(2)}) collective-permute-start(bf16[512,256]{1,0:T(8,128)(2,1)} %get-tuple-element.131), channel_id=1, source_target_pairs={{0,16},{2,18},{4,20},{6,22},{8,24},{10,26},{12,28},{14,30},{16,0},... | collective-permute-start | bytes 786440 | tf_op jit(solution)/shard_map/ppermute | solution.py:204
  272.2 28.8 %collective-permute-start.40 = (bf16[512,512]{1,0:T(8,128)(2,1)S(1)}, bf16[512,512]{1,0:T(8,128)(2,1)S(1)}, u32[]{:S(2)}, u32[]{:S(2)}) collective-permute-start(bf16[512,512]{1,0:T(8,128)(2,1)S(1)} %pad_maximum_fusion.20), channel_id=1, source_target_pairs={{0,4},{2,6},{4,0},{6,2},{8,12},{10,14},{12,8},{14,10},{16,20},{18,... | collective-permute-start | bytes 1572872 | tf_op jit(solution)/shard_map/ppermute | solution.py:204
  272.9 28.1 %collective-permute-start.43 = (bf16[4,256,256]{2,1,0:T(8,128)(2,1)S(1)}, bf16[4,256,256]{2,1,0:T(8,128)(2,1)}, u32[]{:S(2)}, u32[]{:S(2)}) collective-permute-start(bf16[4,256,256]{2,1,0:T(8,128)(2,1)S(1)} %fusion.17), channel_id=1, source_target_pairs={{0,2},{2,0},{4,6},{6,4},{8,10},{10,8},{12,14},{14,12},{16,18},{18,... | collective-permute-start | bytes 1572872 | tf_op jit(solution)/shard_map/ppermute | solution.py:204
  349.0 34.3 %collective-permute-start.49 = (bf16[512,256]{1,0:T(8,128)(2,1)S(1)}, bf16[512,256]{1,0:T(8,128)(2,1)S(1)}, u32[]{:S(2)}, u32[]{:S(2)}) collective-permute-start(bf16[512,256]{1,0:T(8,128)(2,1)S(1)} %get-tuple-element.123), channel_id=1, source_target_pairs={{0,8},{2,10},{4,12},{6,14},{8,16},{10,18},{12,20},{14,22},{16,24},... | collective-permute-start | bytes 786440 | tf_op jit(solution)/shard_map/ppermute | solution.py:204
  349.0 36.2 %collective-permute-start.51 = (bf16[512,256]{1,0:T(8,128)(2,1)S(1)}, bf16[512,256]{1,0:T(8,128)(2,1)S(1)}, u32[]{:S(2)}, u32[]{:S(2)}) collective-permute-start(bf16[512,256]{1,0:T(8,128)(2,1)S(1)} %get-tuple-element.124), channel_id=1, source_target_pairs={{0,24},{2,26},{4,28},{6,30},{8,0},{10,2},{12,4},{14,6},{16,8},{18,... | collective-permute-start | bytes 786440 | tf_op jit(solution)/shard_map/ppermute | solution.py:204
  352.8 32.3 %collective-permute-start.50 = (bf16[512,256]{1,0:T(8,128)(2,1)S(1)}, bf16[512,256]{1,0:T(8,128)(2,1)S(1)}, u32[]{:S(2)}, u32[]{:S(2)}) collective-permute-start(bf16[512,256]{1,0:T(8,128)(2,1)S(1)} %get-tuple-element.125), channel_id=1, source_target_pairs={{0,16},{2,18},{4,20},{6,22},{8,24},{10,26},{12,28},{14,30},{16,0},... | collective-permute-start | bytes 786440 | tf_op jit(solution)/shard_map/ppermute | solution.py:204
  354.1 32.1 %collective-permute-start.55 = (bf16[512,256]{1,0:T(8,128)(2,1)S(1)}, bf16[512,256]{1,0:T(8,128)(2,1)S(1)}, u32[]{:S(2)}, u32[]{:S(2)}) collective-permute-start(bf16[512,256]{1,0:T(8,128)(2,1)S(1)} %get-tuple-element.126), channel_id=1, source_target_pairs={{0,24},{2,26},{4,28},{6,30},{8,0},{10,2},{12,4},{14,6},{16,8},{18,... | collective-permute-start | bytes 786440 | tf_op jit(solution)/shard_map/ppermute | solution.py:204
  354.9 39.5 %collective-permute-start.54 = (bf16[512,256]{1,0:T(8,128)(2,1)S(1)}, bf16[512,256]{1,0:T(8,128)(2,1)S(1)}, u32[]{:S(2)}, u32[]{:S(2)}) collective-permute-start(bf16[512,256]{1,0:T(8,128)(2,1)S(1)} %get-tuple-element.127), channel_id=1, source_target_pairs={{0,16},{2,18},{4,20},{6,22},{8,24},{10,26},{12,28},{14,30},{16,0},... | collective-permute-start | bytes 786440 | tf_op jit(solution)/shard_map/ppermute | solution.py:204
  (90 other events, 984.3 us)

commit v4 on v3

--- a/solution.py
+++ b/solution.py
@@ -266,7 +266,7 @@
         ),
         out_shape=[jax.ShapeDtypeStruct((4, total // 2, columns), BF16)] * 2
         + [jax.ShapeDtypeStruct((2, 4, total // 2, columns), BF16)],
-        compiler_params=pltpu.CompilerParams(vmem_limit_bytes=48 * 2**20),
+        compiler_params=pltpu.CompilerParams(vmem_limit_bytes=60 * 2**20),
         cost_estimate=pl.CostEstimate(
             flops=2 * total * features * columns * 12,
             bytes_accessed=16 * features * columns + 4 * total * features,

time: 398 us -> 397 us (level)
  local copies, waits for them, and re-layouts: 26.3 us -> 17.5 us
  Pallas kernels: 148 us -> 152 us
    unnamed x142 -> x132, local copies, waits for them, and re-layouts: 14.7 us -> 6.86 us
  transfers between devices with their start and end apart: 56 -> 56, of which waited for: 17 -> 17; matrix products, arithmetic and copies ran while one was open for 14% -> 13% of each run, Pallas kernels for 33% -> 34%
where the time goes in v4:
time: 397 us; the launch traced here: 395 us
  Pallas kernels  152 us (38%)
  waiting for transfers between devices  102 us (26%)
  starting transfers between devices  79 us (20%)
  other arithmetic  28.1 us (7%)
  local copies, waits for them, and re-layouts  17.5 us (4%)
  matrix products  14.6 us (4%)
    ppermute x48, waiting for transfers between devices, send(): return lax.ppermute(block, 'wide', pairs(move))  101 us
    ppermute x48, starting transfers between devices, send(): return lax.ppermute(block, 'wide', pairs(move))  77 us
    pallas_call x4, Pallas kernels, recall(): pl.pallas_call(functools.partial(recall_kernel, steps), grid=(heads, span...  60.8 us
    pallas_call x4, Pallas kernels, project(): pl.pallas_call(project_kernel, grid_spec=pltpu.PrefetchScalarGridSpec(num...  50.4 us
    pallas_call x1, Pallas kernels, renew(): pl.pallas_call(renew_kernel, grid=(heads, span // depth), in_specs=[block...  26.1 us
    pallas_call x4, Pallas kernels, weave(): pl.pallas_call(weave_kernel, grid_spec=pltpu.PrefetchScalarGridSpec(num_s...  15 us
  transfers between devices with their start and end apart: 56, of which 17 were waited for; matrix products, arithmetic and copies ran while one was open for 13% of the time, Pallas kernels for 34%

profile of v4, /device:TPU:0, one launch (start us, length us, event | category | flops | bytes accessed | tf_op | source)
XLA Modules:
  0.0 395.3 jit_solution(16955901265939886237)
XLA Ops:
  0.6 5.1 %collective-permute-start.9 = (bf16[64,2048]{1,0:T(8,128)(2,1)}, bf16[64,2048]{1,0:T(8,128)(2,1)}, u32[]{:S(2)}, u32[]{:S(2)}) collective-permute-start(bf16[64,2048]{1,0:T(8,128)(2,1)} %refs_8_.1), channel_id=1, source_target_pairs={{0,24},{2,26},{4,28},{6,30},{8,0},{10,2},{12,4},{14,6},{16,8},{18,... | collective-permute-start | bytes 786440 | tf_op jit(solution)/shard_map/ppermute | solution.py:204
  9.5 3.9 pad_maximum_fusion.refs_19_
  40.2 3.4 collective-permute-done.10
  47.0 3.4 collective-permute-start.11
  50.5 21.3 %collective-permute-done.8.refs_2_.refs_10_ = bf16[64,4096]{1,0:T(8,128)(2,1)S(1)} collective-permute-done((bf16[64,4096]{1,0:T(8,128)(2,1)S(1)}, bf16[64,4096]{1,0:T(8,128)(2,1)S(1)}, u32[]{:S(2)}, u32[]{:S(2)}) %collective-permute-start.8) | collective-permute-done | bytes 524320 | tf_op jit(solution)/shard_map/ppermute | solution.py:204
  72.6 10.8 %collective-permute-start.5 = (bf16[64,4096]{1,0:T(8,128)(2,1)S(1)}, bf16[64,4096]{1,0:T(8,128)(2,1)S(1)}, u32[]{:S(2)}, u32[]{:S(2)}) collective-permute-start(bf16[64,4096]{1,0:T(8,128)(2,1)S(1)} %copy-done.24), channel_id=1, source_target_pairs={{0,8},{2,10},{4,12},{6,14},{8,16},{10,18},{12,20},{14,22},{16,24},... | collective-permute-start | bytes 1572872 | tf_op jit(solution)/shard_map/ppermute | solution.py:204
  83.6 4.9 %collective-permute-done.16 = bf16[4,64,768]{2,1,0:T(8,128)(2,1)S(1)} collective-permute-done((bf16[4,64,768]{2,1,0:T(8,128)(2,1)S(1)}, bf16[4,64,768]{2,1,0:T(8,128)(2,1)S(1)}, u32[]{:S(2)}, u32[]{:S(2)}) %collective-permute-start.16) | collective-permute-done | bytes 393248 | tf_op jit(solution)/shard_map/ppermute | solution.py:204
  91.0 7.0 %collective-permute-done.5.refs_1_.refs_9_ = bf16[64,4096]{1,0:T(8,128)(2,1)S(1)} collective-permute-done((bf16[64,4096]{1,0:T(8,128)(2,1)S(1)}, bf16[64,4096]{1,0:T(8,128)(2,1)S(1)}, u32[]{:S(2)}, u32[]{:S(2)}) %collective-permute-start.5) | collective-permute-done | bytes 524320 | tf_op jit(solution)/shard_map/ppermute | solution.py:204
  100.2 9.1 %collective-permute-done.22 = bf16[256,256]{1,0:T(8,128)(2,1)S(1)} collective-permute-done((bf16[256,256]{1,0:T(8,128)(2,1)S(1)}, bf16[256,256]{1,0:T(8,128)(2,1)S(1)}, u32[]{:S(2)}, u32[]{:S(2)}) %collective-permute-start.22) | collective-permute-done | bytes 131104 | tf_op jit(solution)/shard_map/ppermute | solution.py:204
  111.3 13.1 %collective-permute-done.13.refs_5_.refs_13_ = bf16[64,4096]{1,0:T(8,128)(2,1)S(1)} collective-permute-done((bf16[64,4096]{1,0:T(8,128)(2,1)S(1)}, bf16[64,4096]{1,0:T(8,128)(2,1)S(1)}, u32[]{:S(2)}, u32[]{:S(2)}) %collective-permute-start.13) | collective-permute-done | bytes 524320 | tf_op jit(solution)/shard_map/ppermute | solution.py:204
  124.4 7.0 %collective-permute-start.26 = (bf16[64,4096]{1,0:T(8,128)(2,1)S(1)}, bf16[64,4096]{1,0:T(8,128)(2,1)}, u32[]{:S(2)}, u32[]{:S(2)}) collective-permute-start(bf16[64,4096]{1,0:T(8,128)(2,1)S(1)} %copy-done.23), channel_id=1, source_target_pairs={{0,24},{2,26},{4,28},{6,30},{8,0},{10,2},{12,4},{14,6},{16,8},{18,... | collective-permute-start | bytes 1572872 | tf_op jit(solution)/shard_map/ppermute | solution.py:204
  133.8 12.6 %project.4 = (bf16[4,256,256]{2,1,0:T(8,128)(2,1)}, bf16[4,256,256]{2,1,0:T(8,128)(2,1)}, bf16[2,4,256,256]{3,2,1,0:T(8,128)(2,1)}) custom-call(s32[9]{0:T(128)} %stack.166.order_ref, bf16[64,4096]{1,0:T(8,128)(2,1)} %get-tuple-element.55.refs_0_.refs_8_, bf16[64,4096]{1,0:T(8,128)(2,1)} %copy-done.57, bf16[64,4096]{1,0:T(8,128)(2,1)} %copy-done.30, ...), custom_call_target="tpu_custom_call" | custom-call | flops 6442450944 | bytes 12582912 | tf_op jit(solution)/shard_map/project/pallas_call | solution.py:251
  146.5 12.6 %project.5 = (bf16[4,256,256]{2,1,0:T(8,128)(2,1)}, bf16[4,256,256]{2,1,0:T(8,128)(2,1)}, bf16[2,4,256,256]{3,2,1,0:T(8,128)(2,1)}) custom-call(s32[9]{0:T(128)} %stack.166.order_ref, bf16[64,4096]{1,0:T(8,128)(2,1)} %get-tuple-element.55.refs_0_.refs_8_, bf16[64,4096]{1,0:T(8,128)(2,1)} %copy-done.57, bf16[64,4096]{1,0:T(8,128)(2,1)} %copy-done.30, ...), custom_call_target="tpu_custom_call" | custom-call | flops 6442450944 | bytes 12582912 | tf_op jit(solution)/shard_map/project/pallas_call | solution.py:251
  169.1 7.6 %collective-permute-done.21.mate_ref = bf16[4,256,256]{2,1,0:T(8,128)(2,1)S(1)} collective-permute-done((bf16[4,256,256]{2,1,0:T(8,128)(2,1)S(1)}, bf16[4,256,256]{2,1,0:T(8,128)(2,1)S(1)}, u32[]{:S(2)}, u32[]{:S(2)}) %collective-permute-start.21) | collective-permute-done | bytes 524320 | tf_op jit(solution)/shard_map/ppermute | solution.py:204
  177.6 3.7 weave.4.refs_1_.refs_0_
  181.3 14.8 %recall.4 = bf16[256,512]{1,0:T(8,128)(2,1)} custom-call(f32[4,64,64,512]{3,2,1,0:T(8,128)} %bitcast.198, bf16[4,256,512]{2,1,0:T(8,128)(2,1)} %weave.4.refs_1_.refs_0_, f32[4,256,512]{2,1,0:T(8,128)} %exponential_bitcast_fusion.refs_2_.refs_3_.refs_4_.refs_5_, f32[256,1]{1,0:T(8,128)} %copy.32.refs_3_.refs_5_, ...), custom_call_target="tpu_custom_call" | custom-call | flops 16777216 | bytes 33554432 | tf_op jit(solution)/shard_map/recall/pallas_call | solution.py:368
  197.6 6.0 %collective-permute-done.23 = bf16[256,512]{1,0:T(8,128)(2,1)S(1)} collective-permute-done((bf16[256,512]{1,0:T(8,128)(2,1)}, bf16[256,512]{1,0:T(8,128)(2,1)S(1)}, u32[]{:S(2)}, u32[]{:S(2)}) %collective-permute-start.23) | collective-permute-done | bytes 262176 | tf_op jit(solution)/shard_map/ppermute | solution.py:204
  206.7 12.6 %project.6 = (bf16[4,256,256]{2,1,0:T(8,128)(2,1)}, bf16[4,256,256]{2,1,0:T(8,128)(2,1)}, bf16[2,4,256,256]{3,2,1,0:T(8,128)(2,1)}) custom-call(s32[9]{0:T(128)} %stack.166.order_ref, bf16[64,4096]{1,0:T(8,128)(2,1)} %get-tuple-element.68.refs_0_.refs_8_, bf16[64,4096]{1,0:T(8,128)(2,1)} %copy-done.58, ...), custom_call_target="tpu_custom_call" | custom-call | flops 6442450944 | bytes 12582912 | tf_op jit(solution)/shard_map/project/pallas_call | solution.py:251
  219.4 3.8 weave.5.refs_2_.refs_1_
  223.2 12.6 %project.7 = (bf16[4,256,256]{2,1,0:T(8,128)(2,1)}, bf16[4,256,256]{2,1,0:T(8,128)(2,1)}, bf16[2,4,256,256]{3,2,1,0:T(8,128)(2,1)}) custom-call(s32[9]{0:T(128)} %stack.166.order_ref, bf16[64,4096]{1,0:T(8,128)(2,1)} %get-tuple-element.68.refs_0_.refs_8_, bf16[64,4096]{1,0:T(8,128)(2,1)} %copy-done.58, ...), custom_call_target="tpu_custom_call" | custom-call | flops 6442450944 | bytes 12582912 | tf_op jit(solution)/shard_map/project/pallas_call | solution.py:251
  244.2 15.0 %recall.5 = bf16[256,512]{1,0:T(8,128)(2,1)} custom-call(f32[4,64,64,512]{3,2,1,0:T(8,128)} %bitcast.199, bf16[4,256,512]{2,1,0:T(8,128)(2,1)} %weave.4.refs_1_.refs_0_, bf16[4,256,512]{2,1,0:T(8,128)(2,1)} %weave.5.refs_2_.refs_1_, f32[4,256,512]{2,1,0:T(8,128)} %exponential_bitcast_fusion.refs_2_.refs_3_.refs_4_.refs_5_, f32[256,1]{1,0:T(8,128)} %copy.35.refs_4_, ...), custom_call_target="tpu_custom_call" | custom-call | flops 16777216 | bytes 33554432 | tf_op jit(solution)/shard_map/recall/pallas_call | solution.py:368
  262.3 3.8 collective-permute-start.36
  270.3 3.8 weave.6.refs_3_.refs_2_
  274.1 15.4 %recall.6 = bf16[256,512]{1,0:T(8,128)(2,1)} custom-call(f32[4,64,64,512]{3,2,1,0:T(8,128)} %bitcast.200, bf16[4,256,512]{2,1,0:T(8,128)(2,1)} %weave.4.refs_1_.refs_0_, bf16[4,256,512]{2,1,0:T(8,128)(2,1)} %weave.5.refs_2_.refs_1_, bf16[4,256,512]{2,1,0:T(8,128)(2,1)} %weave.6.refs_3_.refs_2_, ...), custom_call_target="tpu_custom_call" | custom-call | flops 16777216 | bytes 33554432 | tf_op jit(solution)/shard_map/recall/pallas_call | solution.py:368
  292.9 3.4 collective-permute-done.42
  299.2 3.7 weave.7.refs_4_.refs_3_
  305.9 15.6 %recall.7 = bf16[256,512]{1,0:T(8,128)(2,1)} custom-call(f32[4,64,64,512]{3,2,1,0:T(8,128)} %bitcast.201, bf16[4,256,512]{2,1,0:T(8,128)(2,1)} %weave.4.refs_1_.refs_0_, bf16[4,256,512]{2,1,0:T(8,128)(2,1)} %weave.5.refs_2_.refs_1_, bf16[4,256,512]{2,1,0:T(8,128)(2,1)} %weave.6.refs_3_.refs_2_, bf16[4,256,512]{2,1,0:T(8,128)(2,1)} %weave.7.refs_4_.refs_3_, ...), custom_call_target="tpu_custom_call" | custom-call | flops 16777216 | bytes 33554432 | tf_op jit(solution)/shard_map/recall/pallas_call | solution.py:368
  322.8 3.8 collective-permute-start.46
  335.0 10.4 %collective-permute-done.45 = bf16[512,256]{1,0:T(8,128)(2,1)S(1)} collective-permute-done((bf16[512,256]{1,0:T(8,128)(2,1)S(1)}, bf16[512,256]{1,0:T(8,128)(2,1)S(1)}, u32[]{:S(2)}, u32[]{:S(2)}) %collective-permute-start.45) | collective-permute-done | bytes 262176 | tf_op jit(solution)/shard_map/ppermute | solution.py:204
  348.2 3.8 collective-permute-start.51
  356.3 26.1 %renew.1 = f32[4,64,64,512]{3,2,1,0:T(8,128)} custom-call(f32[4,64,64,512]{3,2,1,0:T(8,128)} %bitcast.202, bf16[4,256,512]{2,1,0:T(8,128)(2,1)S(1)} %copy-done.3, bf16[4,256,512]{2,1,0:T(8,128)(2,1)S(1)} %copy-done.4, bf16[4,256,512]{2,1,0:T(8,128)(2,1)S(1)} %copy-done.5, bf16[4,256,512]{2,1,0:T(8,128)(2,1)S(1)} %copy-done.6, f32[4,256,512]{2,1,0:T(8,128)S(1)} %copy-done.2), custom_call_target="tpu_custom_call" | custom-call | flops 75497472 | bytes 67108864 | tf_op jit(solution)/shard_map/renew/pallas_call | solution.py:422
  385.3 7.9 %collective-permute-done.54 = bf16[512,256]{1,0:T(8,128)(2,1)S(1)} collective-permute-done((bf16[512,256]{1,0:T(8,128)(2,1)S(1)}, bf16[512,256]{1,0:T(8,128)(2,1)S(1)}, u32[]{:S(2)}, u32[]{:S(2)}) %collective-permute-start.54) | collective-permute-done | bytes 262176 | tf_op jit(solution)/shard_map/ppermute | solution.py:204
  (304 shorter events, 105.4 us)
Async XLA Ops:
  0.6 33.2 %collective-permute-start.9 = (bf16[64,2048]{1,0:T(8,128)(2,1)}, bf16[64,2048]{1,0:T(8,128)(2,1)}, u32[]{:S(2)}, u32[]{:S(2)}) collective-permute-start(bf16[64,2048]{1,0:T(8,128)(2,1)} %refs_8_.1), channel_id=1, source_target_pairs={{0,24},{2,26},{4,28},{6,30},{8,0},{10,2},{12,4},{14,6},{16,8},{18,... | collective-permute-start | bytes 786440 | tf_op jit(solution)/shard_map/ppermute | solution.py:204
  5.7 28.1 %collective-permute-start.6 = (bf16[64,2048]{1,0:T(8,128)(2,1)}, bf16[64,2048]{1,0:T(8,128)(2,1)}, u32[]{:S(2)}, u32[]{:S(2)}) collective-permute-start(bf16[64,2048]{1,0:T(8,128)(2,1)} %refs_8_.1), channel_id=1, source_target_pairs={{0,16},{2,18},{4,20},{6,22},{8,24},{10,26},{12,28},{14,30},{16,0},... | collective-permute-start | bytes 786440 | tf_op jit(solution)/shard_map/ppermute | solution.py:204
  5.8 28.2 %collective-permute-start.3 = (bf16[64,2048]{1,0:T(8,128)(2,1)}, bf16[64,2048]{1,0:T(8,128)(2,1)}, u32[]{:S(2)}, u32[]{:S(2)}) collective-permute-start(bf16[64,2048]{1,0:T(8,128)(2,1)} %refs_8_.1), channel_id=1, source_target_pairs={{0,8},{2,10},{4,12},{6,14},{8,16},{10,18},{12,20},{14,22},{16,24},... | collective-permute-start | bytes 786440 | tf_op jit(solution)/shard_map/ppermute | solution.py:204
  13.4 120.4 %collective-permute-start.17 = (bf16[4,2048,256]{2,1,0:T(8,128)(2,1)}, bf16[4,2048,256]{2,1,0:T(8,128)(2,1)}, u32[]{:S(2)}, u32[]{:S(2)}) collective-permute-start(bf16[4,2048,256]{2,1,0:T(8,128)(2,1)} %pad_maximum_fusion.refs_19_), channel_id=1, source_target_pairs={{0,2},{2,0},{4,6},{6,4},{8,10},{10,8},{12,14},{14,12},{16,18},{18,... | collective-permute-start | bytes 12582920 | tf_op jit(solution)/shard_map/ppermute | solution.py:204
  32.2 65.8 %collective-permute-start.12 = (bf16[2,64,4096]{2,1,0:T(8,128)(2,1)S(1)}, bf16[2,64,4096]{2,1,0:T(8,128)(2,1)}, u32[]{:S(2)}, u32[]{:S(2)}) collective-permute-start(bf16[2,64,4096]{2,1,0:T(8,128)(2,1)S(1)} %pad_maximum_fusion.5), channel_id=1, source_target_pairs={{0,4},{2,6},{4,0},{6,2},{8,12},{10,14},{12,8},{14,10},{16,20},{18,... | collective-permute-start | bytes 3145736 | tf_op jit(solution)/shard_map/ppermute | solution.py:204
  43.6 55.1 %collective-permute-start.15 = (bf16[4,64,2048]{2,1,0:T(8,128)(2,1)S(1)}, bf16[4,64,2048]{2,1,0:T(8,128)(2,1)S(1)}, u32[]{:S(2)}, u32[]{:S(2)}) collective-permute-start(bf16[4,64,2048]{2,1,0:T(8,128)(2,1)S(1)} %fusion.14), channel_id=1, source_target_pairs={{0,4},{2,6},{4,0},{6,2},{8,12},{10,14},{12,8},{14,10},{16,20},{18,... | collective-permute-start | bytes 3145736 | tf_op jit(solution)/shard_map/ppermute | solution.py:204
  44.8 27.0 %collective-permute-start.8 = (bf16[64,4096]{1,0:T(8,128)(2,1)S(1)}, bf16[64,4096]{1,0:T(8,128)(2,1)S(1)}, u32[]{:S(2)}, u32[]{:S(2)}) collective-permute-start(bf16[64,4096]{1,0:T(8,128)(2,1)S(1)} %copy-done.24), channel_id=1, source_target_pairs={{0,16},{2,18},{4,20},{6,22},{8,24},{10,26},{12,28},{14,30},{16,0},... | collective-permute-start | bytes 1572872 | tf_op jit(solution)/shard_map/ppermute | solution.py:204
  47.0 25.7 %collective-permute-start.11 = (bf16[64,4096]{1,0:T(8,128)(2,1)S(1)}, bf16[64,4096]{1,0:T(8,128)(2,1)S(1)}, u32[]{:S(2)}, u32[]{:S(2)}) collective-permute-start(bf16[64,4096]{1,0:T(8,128)(2,1)S(1)} %copy-done.24), channel_id=1, source_target_pairs={{0,24},{2,26},{4,28},{6,30},{8,0},{10,2},{12,4},{14,6},{16,8},{18,... | collective-permute-start | bytes 1572872 | tf_op jit(solution)/shard_map/ppermute | solution.py:204
  72.6 25.4 %collective-permute-start.5 = (bf16[64,4096]{1,0:T(8,128)(2,1)S(1)}, bf16[64,4096]{1,0:T(8,128)(2,1)S(1)}, u32[]{:S(2)}, u32[]{:S(2)}) collective-permute-start(bf16[64,4096]{1,0:T(8,128)(2,1)S(1)} %copy-done.24), channel_id=1, source_target_pairs={{0,8},{2,10},{4,12},{6,14},{8,16},{10,18},{12,20},{14,22},{16,24},... | collective-permute-start | bytes 1572872 | tf_op jit(solution)/shard_map/ppermute | solution.py:204
  88.5 44.3 %collective-permute-start.14 = (bf16[2,64,4096]{2,1,0:T(8,128)(2,1)S(1)}, bf16[2,64,4096]{2,1,0:T(8,128)(2,1)S(1)}, u32[]{:S(2)}, u32[]{:S(2)}) collective-permute-start(bf16[2,64,4096]{2,1,0:T(8,128)(2,1)S(1)} %pad_maximum_fusion.6), channel_id=1, source_target_pairs={{0,4},{2,6},{4,0},{6,2},{8,12},{10,14},{12,8},{14,10},{16,20},{18,... | collective-permute-start | bytes 3145736 | tf_op jit(solution)/shard_map/ppermute | solution.py:204
  98.0 26.4 %collective-permute-start.13 = (bf16[64,4096]{1,0:T(8,128)(2,1)S(1)}, bf16[64,4096]{1,0:T(8,128)(2,1)S(1)}, u32[]{:S(2)}, u32[]{:S(2)}) collective-permute-start(bf16[64,4096]{1,0:T(8,128)(2,1)S(1)} %collective-permute-done.5.refs_1_.refs_9_), channel_id=1, source_target_pairs={{0,4},{2,6},{4,0},{6,2},{8,12},{10,14},{12,8},{14,10},{16,20},{18,... | collective-permute-start | bytes 1572872 | tf_op jit(solution)/shard_map/ppermute | solution.py:204
  98.7 32.7 %collective-permute-start.19 = (bf16[64,4096]{1,0:T(8,128)(2,1)S(1)}, bf16[64,4096]{1,0:T(8,128)(2,1)S(1)}, u32[]{:S(2)}, u32[]{:S(2)}) collective-permute-start(bf16[64,4096]{1,0:T(8,128)(2,1)S(1)} %copy-done.23), channel_id=1, source_target_pairs={{0,8},{2,10},{4,12},{6,14},{8,16},{10,18},{12,20},{14,22},{16,24},... | collective-permute-start | bytes 1572872 | tf_op jit(solution)/shard_map/ppermute | solution.py:204
  109.3 50.6 %collective-permute-start.25 = (bf16[64,4096]{1,0:T(8,128)(2,1)S(1)}, bf16[64,4096]{1,0:T(8,128)(2,1)}, u32[]{:S(2)}, u32[]{:S(2)}) collective-permute-start(bf16[64,4096]{1,0:T(8,128)(2,1)S(1)} %copy-done.23), channel_id=1, source_target_pairs={{0,16},{2,18},{4,20},{6,22},{8,24},{10,26},{12,28},{14,30},{16,0},... | collective-permute-start | bytes 1572872 | tf_op jit(solution)/shard_map/ppermute | solution.py:204
  124.4 35.5 %collective-permute-start.26 = (bf16[64,4096]{1,0:T(8,128)(2,1)S(1)}, bf16[64,4096]{1,0:T(8,128)(2,1)}, u32[]{:S(2)}, u32[]{:S(2)}) collective-permute-start(bf16[64,4096]{1,0:T(8,128)(2,1)S(1)} %copy-done.23), channel_id=1, source_target_pairs={{0,24},{2,26},{4,28},{6,30},{8,0},{10,2},{12,4},{14,6},{16,8},{18,... | collective-permute-start | bytes 1572872 | tf_op jit(solution)/shard_map/ppermute | solution.py:204
  162.3 44.4 %collective-permute-start.27 = (bf16[2,64,4096]{2,1,0:T(8,128)(2,1)}, bf16[2,64,4096]{2,1,0:T(8,128)(2,1)}, u32[]{:S(2)}, u32[]{:S(2)}) collective-permute-start(bf16[2,64,4096]{2,1,0:T(8,128)(2,1)} %pad_maximum_fusion.8), channel_id=1, source_target_pairs={{0,4},{2,6},{4,0},{6,2},{8,12},{10,14},{12,8},{14,10},{16,20},{18,... | collective-permute-start | bytes 3145736 | tf_op jit(solution)/shard_map/ppermute | solution.py:204
  165.9 30.3 %collective-permute-start.30 = (bf16[512,256]{1,0:T(8,128)(2,1)S(1)}, bf16[512,256]{1,0:T(8,128)(2,1)S(1)}, u32[]{:S(2)}, u32[]{:S(2)}) collective-permute-start(bf16[512,256]{1,0:T(8,128)(2,1)S(1)} %copy-done.36), channel_id=1, source_target_pairs={{0,24},{2,26},{4,28},{6,30},{8,0},{10,2},{12,4},{14,6},{16,8},{18,... | collective-permute-start | bytes 786440 | tf_op jit(solution)/shard_map/ppermute | solution.py:204
  165.9 31.5 %collective-permute-start.31 = (bf16[512,256]{1,0:T(8,128)(2,1)}, bf16[512,256]{1,0:T(8,128)(2,1)S(1)}, u32[]{:S(2)}, u32[]{:S(2)}) collective-permute-start(bf16[512,256]{1,0:T(8,128)(2,1)} %pad_maximum_fusion.25), channel_id=1, source_target_pairs={{0,16},{2,18},{4,20},{6,22},{8,24},{10,26},{12,28},{14,30},{16,0},... | collective-permute-start | bytes 786440 | tf_op jit(solution)/shard_map/ppermute | solution.py:204
  166.0 31.5 %collective-permute-start.32 = (bf16[512,256]{1,0:T(8,128)(2,1)}, bf16[512,256]{1,0:T(8,128)(2,1)S(1)}, u32[]{:S(2)}, u32[]{:S(2)}) collective-permute-start(bf16[512,256]{1,0:T(8,128)(2,1)} %pad_maximum_fusion.26), channel_id=1, source_target_pairs={{0,8},{2,10},{4,12},{6,14},{8,16},{10,18},{12,20},{14,22},{16,24},... | collective-permute-start | bytes 786440 | tf_op jit(solution)/shard_map/ppermute | solution.py:204
  176.8 42.7 %collective-permute-start.29 = (bf16[4,256,256]{2,1,0:T(8,128)(2,1)}, bf16[4,256,256]{2,1,0:T(8,128)(2,1)}, u32[]{:S(2)}, u32[]{:S(2)}) collective-permute-start(bf16[4,256,256]{2,1,0:T(8,128)(2,1)} %fusion.19), channel_id=1, source_target_pairs={{0,2},{2,0},{4,6},{6,4},{8,10},{10,8},{12,14},{14,12},{16,18},{18,... | collective-permute-start | bytes 1572872 | tf_op jit(solution)/shard_map/ppermute | solution.py:204
  197.5 38.8 %collective-permute-start.33 = (bf16[512,768]{1,0:T(8,128)(2,1)S(1)}, bf16[512,768]{1,0:T(8,128)(2,1)}, u32[]{:S(2)}, u32[]{:S(2)}) collective-permute-start(bf16[512,768]{1,0:T(8,128)(2,1)S(1)} %constant_dynamic-update-slice_fusion), channel_id=1, source_target_pairs={{0,1},{1,0},{2,3},{3,2},{4,5},{5,4},{6,7},{7,6},{8,9},{9,8},{10,11... | collective-permute-start | bytes 2359304 | tf_op jit(solution)/shard_map/ppermute | solution.py:208
  205.4 32.2 %collective-permute-start.24 = (bf16[512,512]{1,0:T(8,128)(2,1)}, bf16[512,512]{1,0:T(8,128)(2,1)}, u32[]{:S(2)}, u32[]{:S(2)}) collective-permute-start(bf16[512,512]{1,0:T(8,128)(2,1)} %pad_maximum_fusion.18), channel_id=1, source_target_pairs={{0,4},{2,6},{4,0},{6,2},{8,12},{10,14},{12,8},{14,10},{16,20},{18,... | collective-permute-start | bytes 1572872 | tf_op jit(solution)/shard_map/ppermute | solution.py:204
  241.3 27.9 %collective-permute-start.41 = (bf16[4,256,256]{2,1,0:T(8,128)(2,1)S(1)}, bf16[4,256,256]{2,1,0:T(8,128)(2,1)S(1)}, u32[]{:S(2)}, u32[]{:S(2)}) collective-permute-start(bf16[4,256,256]{2,1,0:T(8,128)(2,1)S(1)} %fusion.18), channel_id=1, source_target_pairs={{0,2},{2,0},{4,6},{6,4},{8,10},{10,8},{12,14},{14,12},{16,18},{18,... | collective-permute-start | bytes 1572872 | tf_op jit(solution)/shard_map/ppermute | solution.py:204
  262.3 27.2 %collective-permute-start.34 = (bf16[512,256]{1,0:T(8,128)(2,1)S(1)}, bf16[512,256]{1,0:T(8,128)(2,1)}, u32[]{:S(2)}, u32[]{:S(2)}) collective-permute-start(bf16[512,256]{1,0:T(8,128)(2,1)S(1)} %get-tuple-element.129), channel_id=1, source_target_pairs={{0,8},{2,10},{4,12},{6,14},{8,16},{10,18},{12,20},{14,22},{16,24},... | collective-permute-start | bytes 786440 | tf_op jit(solution)/shard_map/ppermute | solution.py:204
  262.3 28.2 %collective-permute-start.36 = (bf16[512,256]{1,0:T(8,128)(2,1)}, bf16[512,256]{1,0:T(8,128)(2,1)}, u32[]{:S(2)}, u32[]{:S(2)}) collective-permute-start(bf16[512,256]{1,0:T(8,128)(2,1)} %get-tuple-element.130), channel_id=1, source_target_pairs={{0,24},{2,26},{4,28},{6,30},{8,0},{10,2},{12,4},{14,6},{16,8},{18,... | collective-permute-start | bytes 786440 | tf_op jit(solution)/shard_map/ppermute | solution.py:204
  266.1 24.4 %collective-permute-start.35 = (bf16[512,256]{1,0:T(8,128)(2,1)S(1)}, bf16[512,256]{1,0:T(8,128)(2,1)}, u32[]{:S(2)}, u32[]{:S(2)}) collective-permute-start(bf16[512,256]{1,0:T(8,128)(2,1)S(1)} %get-tuple-element.131), channel_id=1, source_target_pairs={{0,16},{2,18},{4,20},{6,22},{8,24},{10,26},{12,28},{14,30},{16,0},... | collective-permute-start | bytes 786440 | tf_op jit(solution)/shard_map/ppermute | solution.py:204
  268.5 28.7 %collective-permute-start.40 = (bf16[512,512]{1,0:T(8,128)(2,1)S(1)}, bf16[512,512]{1,0:T(8,128)(2,1)}, u32[]{:S(2)}, u32[]{:S(2)}) collective-permute-start(bf16[512,512]{1,0:T(8,128)(2,1)S(1)} %pad_maximum_fusion.20), channel_id=1, source_target_pairs={{0,4},{2,6},{4,0},{6,2},{8,12},{10,14},{12,8},{14,10},{16,20},{18,... | collective-permute-start | bytes 1572872 | tf_op jit(solution)/shard_map/ppermute | solution.py:204
  269.2 29.1 %collective-permute-start.43 = (bf16[4,256,256]{2,1,0:T(8,128)(2,1)}, bf16[4,256,256]{2,1,0:T(8,128)(2,1)S(1)}, u32[]{:S(2)}, u32[]{:S(2)}) collective-permute-start(bf16[4,256,256]{2,1,0:T(8,128)(2,1)} %fusion.17), channel_id=1, source_target_pairs={{0,2},{2,0},{4,6},{6,4},{8,10},{10,8},{12,14},{14,12},{16,18},{18,... | collective-permute-start | bytes 1572872 | tf_op jit(solution)/shard_map/ppermute | solution.py:204
  348.1 34.3 %collective-permute-start.49 = (bf16[512,256]{1,0:T(8,128)(2,1)S(1)}, bf16[512,256]{1,0:T(8,128)(2,1)S(1)}, u32[]{:S(2)}, u32[]{:S(2)}) collective-permute-start(bf16[512,256]{1,0:T(8,128)(2,1)S(1)} %get-tuple-element.123), channel_id=1, source_target_pairs={{0,8},{2,10},{4,12},{6,14},{8,16},{10,18},{12,20},{14,22},{16,24},... | collective-permute-start | bytes 786440 | tf_op jit(solution)/shard_map/ppermute | solution.py:204
  348.2 36.1 %collective-permute-start.51 = (bf16[512,256]{1,0:T(8,128)(2,1)S(1)}, bf16[512,256]{1,0:T(8,128)(2,1)S(1)}, u32[]{:S(2)}, u32[]{:S(2)}) collective-permute-start(bf16[512,256]{1,0:T(8,128)(2,1)S(1)} %get-tuple-element.124), channel_id=1, source_target_pairs={{0,24},{2,26},{4,28},{6,30},{8,0},{10,2},{12,4},{14,6},{16,8},{18,... | collective-permute-start | bytes 786440 | tf_op jit(solution)/shard_map/ppermute | solution.py:204
  352.0 32.3 %collective-permute-start.50 = (bf16[512,256]{1,0:T(8,128)(2,1)S(1)}, bf16[512,256]{1,0:T(8,128)(2,1)S(1)}, u32[]{:S(2)}, u32[]{:S(2)}) collective-permute-start(bf16[512,256]{1,0:T(8,128)(2,1)S(1)} %get-tuple-element.125), channel_id=1, source_target_pairs={{0,16},{2,18},{4,20},{6,22},{8,24},{10,26},{12,28},{14,30},{16,0},... | collective-permute-start | bytes 786440 | tf_op jit(solution)/shard_map/ppermute | solution.py:204
  353.2 32.1 %collective-permute-start.55 = (bf16[512,256]{1,0:T(8,128)(2,1)S(1)}, bf16[512,256]{1,0:T(8,128)(2,1)S(1)}, u32[]{:S(2)}, u32[]{:S(2)}) collective-permute-start(bf16[512,256]{1,0:T(8,128)(2,1)S(1)} %get-tuple-element.126), channel_id=1, source_target_pairs={{0,24},{2,26},{4,28},{6,30},{8,0},{10,2},{12,4},{14,6},{16,8},{18,... | collective-permute-start | bytes 786440 | tf_op jit(solution)/shard_map/ppermute | solution.py:204
  353.9 39.3 %collective-permute-start.54 = (bf16[512,256]{1,0:T(8,128)(2,1)S(1)}, bf16[512,256]{1,0:T(8,128)(2,1)S(1)}, u32[]{:S(2)}, u32[]{:S(2)}) collective-permute-start(bf16[512,256]{1,0:T(8,128)(2,1)S(1)} %get-tuple-element.127), channel_id=1, source_target_pairs={{0,16},{2,18},{4,20},{6,22},{8,24},{10,26},{12,28},{14,30},{16,0},... | collective-permute-start | bytes 786440 | tf_op jit(solution)/shard_map/ppermute | solution.py:204
  (85 other events, 850.9 us)
